TPU v7x, 128 devices: a whole 4x4x4 slice. The times are simulated.
128 devices in a mesh: ex: 16 (over y, x), lay: 8 (over z, core).
Axes of the slice: x: 4, y: 4, z: 4, core: 2. Of those that a mesh axis runs over, the one named last changes fastest.
Arguments:
- grads: bfloat16 [8, 16384, 4096], P('lay', 'ex'), may hold values from -0.119628906 to 0.119628906
- prec_in: bfloat16 [8, 64, 64], P('lay'), as said below
- prec_out: bfloat16 [8, 64, 64], P('lay'), as said below
- requests: int32 [16, 16], replicated, may hold values from 0 to 7
- pairs: int32 [1024, 2], P('ex'), may hold values from 0 to 127, as said below
Outputs:
- gram: float32 [1024, 128, 128], P(('ex', 'lay'))
Inputs may be any that keep to these rules, and one draw needn't show every extreme that they name: Each device's listed first blocks are its own: pairs[p, 0] lies in 8 * (p // 64) to 8 * (p // 64 + 1) - 1. pairs[p, 1] is a device number of ex. The 64 pairs of one device are distinct and name every device number at least once. `prec_in`: each matrix has a diagonal between 1.5 and 6 and exceeds the sum of magnitudes of the rest of its row. `prec_out`: each matrix has a diagonal between 1.5 and 6 and exceeds the sum of magnitudes of the rest of its row.
All inputs are finite; a program needn't handle non-finite values.
Results may differ from a plain program's by a relative error of at most 0.0026.
Values may be sent and summed in bfloat16 or wider, within the bound.
No kernel may reach another device: no remote copies, remote signals or barrier semaphores. Data moves between devices by JAX's collectives and lax.ppermute only.
A program may use at most 128 MiB of HBM per device.

v0:
```python
import jax
import jax.numpy as jnp
from jax import lax
from jax.sharding import PartitionSpec as P

BLOCK = 128


def precondition(grads, prec_in, prec_out):
    layer_count, example_rows, width = grads.shape
    rank = prec_in.shape[-1]
    turned = jnp.swapaxes(grads, 1, 2).reshape(layer_count, rank, rank, example_rows)
    inner = jnp.einsum(
        "loie,lij->loje", turned, prec_in, preferred_element_type=jnp.float32
    ).astype(jnp.bfloat16)
    outer = jnp.einsum("lpo,loje->lpje", prec_out, inner, preferred_element_type=jnp.float32)
    return outer.astype(jnp.bfloat16).reshape(layer_count, width, example_rows)


def pick_tiles(products, first, source):
    return products[first, :, source, :]


def on_device(grads, prec_in, prec_out, requests, pairs):
    layer_count, example_rows, width = grads.shape
    blocks = grads.reshape(layer_count, example_rows // BLOCK, BLOCK, width)
    block_count = blocks.shape[1]
    member = lax.axis_index("ex")
    wanted = lax.dynamic_index_in_dim(requests, member, axis=1, keepdims=False)
    outgoing = jnp.take(blocks, wanted, axis=1)
    incoming = lax.all_to_all(outgoing, "ex", split_axis=1, concat_axis=1, tiled=True)
    holders = incoming.shape[1]
    left = precondition(grads, prec_in, prec_out)
    right = incoming.reshape(layer_count, holders * BLOCK, width)
    products = jnp.einsum("lqx,lmq->xm", left, right, preferred_element_type=jnp.float32)
    products = products.reshape(block_count, BLOCK, holders, BLOCK)
    first = pairs[:, 0] - member * block_count
    source = pairs[:, 1]
    pair_count = pairs.shape[0]
    share = pair_count // lax.axis_size("lay")
    terms = pick_tiles(products, first, source)
    total = lax.psum(terms, "lay")
    return lax.dynamic_slice_in_dim(total, lax.axis_index("lay") * share, share, 0)


def solution(mesh):
    placed = (P("lay", "ex", None), P("lay", None, None), P("lay", None, None), P(), P("ex", None))
    return jax.shard_map(
        on_device,
        mesh=mesh,
        in_specs=placed,
        out_specs=P(("ex", "lay"), None, None),
        check_vma=False,
    )
```

profile of v0, /device:TPU:0, one launch (start us, length us, event | category | flops | bytes accessed | tf_op | source)
XLA Modules:
  0.0 400.7 jit_solution(12002217262961592764)
XLA Ops:
  6.5 0.0 copy-start
  6.5 0.9 fusion.8
  7.4 0.9 and_reduce_fusion
  8.3 10.6 %gather_fusion = bf16[16,128,4096]{2,1,0:T(8,128)(2,1)} fusion(bf16[8,128,4096]{2,1,0:T(8,128)(2,1)} %bitcast.39, s32[1024]{0:T(1024)S(1)} %pad_clamp_fusion), kind=kCustom, calls=%fused_computation | custom fusion | bytes 33554496 | tf_op jit(solution)/shard_map/jit(_take)/gather | solution.py:30
  19.0 14.2 %bitcast_select_fusion = bf16[1,16,128,4096]{3,2,0,1:T(8,128)(2,1)} fusion(bf16[16,128,4096]{2,1,0:T(8,128)(2,1)} %gather_fusion, pred[16]{0:T(512)(128)(4,1)S(1)} %and_reduce_fusion), kind=kLoop, calls=%fused_computation.4 | loop fusion | flops 8388608 | bytes 33554448 | tf_op jit(solution)/shard_map/jit(_take)/select_n | solution.py:30
  33.1 7.1 %all-to-all-start = ((bf16[1,16,128,4096]{3,2,0,1:T(8,128)(2,1)}), bf16[1,16,128,4096]{3,2,0,1:T(8,128)(2,1)}, u32[]{:S(2)}, u32[]{:S(2)}) async-start(bf16[1,16,128,4096]{3,2,0,1:T(8,128)(2,1)} %bitcast_select_fusion), calls=%async_computation | async-start | bytes 33554432 | tf_op jit(solution)/shard_map/all_to_all | solution.py:31
  40.2 0.0 all-reduce.2.cloned.1.call-start
  40.2 12.0 %copy.14 = bf16[1,1024,4096]{1,2,0:T(8,128)(2,1)} copy(bf16[1,1024,4096]{2,1,0:T(8,128)(2,1)} %param.5) | data formatting | bytes 16777216 | tf_op args[0]
  52.2 0.0 copy-done
  52.2 0.0 copy-start.2
  52.2 5.8 %convert_bitcast_fusion.1 = bf16[64,64,1024]{2,1,0:T(8,128)(2,1)S(1)} fusion(bf16[64,64,1024]{2,1,0:T(8,128)(2,1)} %bitcast.40, bf16[1,64,64]{2,1,0:T(8,128)(2,1)S(1)} %copy-done), kind=kOutput, calls=%fused_computation.8 | convolution fusion | flops 541065216 | bytes 16785408 | tf_op jit(solution)/shard_map/loie,lij->loje/dot_general | solution.py:13
  58.0 0.0 copy-done.2
  58.0 12.9 %convert_bitcast_fusion = bf16[64,64,1024]{2,0,1:T(8,128)(2,1)} fusion(bf16[64,64,1024]{2,1,0:T(8,128)(2,1)S(1)} %convert_bitcast_fusion.1, bf16[1,64,64]{2,1,0:T(8,128)(2,1)S(1)} %copy-done.2), kind=kOutput, calls=%fused_computation.7 | convolution fusion | flops 541065216 | bytes 16785408 | tf_op jit(solution)/shard_map/lpo,loje->lpje/dot_general | solution.py:16
  70.9 11.3 %copy.17 = bf16[64,64,1024]{2,1,0:T(8,128)(2,1)} copy(bf16[64,64,1024]{2,0,1:T(8,128)(2,1)} %convert_bitcast_fusion) | data formatting | bytes 16777216 | tf_op jit(solution)/shard_map/convert_element_type | solution.py:17
  82.2 0.0 copy-start.3
  82.2 11.2 %copy.22 = bf16[1024,4096]{1,0:T(8,128)(2,1)} copy(bf16[1024,4096]{0,1:T(8,128)(2,1)} %bitcast.41) | data formatting | bytes 16777216 | tf_op jit(solution)/shard_map/lqx,lmq->xm/dot_general | solution.py:35
  93.4 0.0 copy-done.3
  93.4 196.5 %all-to-all-done = bf16[1,16,128,4096]{3,2,0,1:T(8,128)(2,1)} async-done(((bf16[1,16,128,4096]{3,2,0,1:T(8,128)(2,1)}), bf16[1,16,128,4096]{3,2,0,1:T(8,128)(2,1)}, u32[]{:S(2)}, u32[]{:S(2)}) %all-to-all-start) | async-done | bytes 16777248 | tf_op jit(solution)/shard_map/all_to_all | solution.py:31
  289.9 0.0 copy-start.1
  289.9 24.1 %fusion = f32[8,128,16,128]{3,1,2,0:T(8,128)} fusion(bf16[8,128,4096,1]{2,1,3,0:T(8,128)(2,1)} %bitcast.42, bf16[1,16,128,4096]{3,2,0,1:T(8,128)(2,1)} %all-to-all-done), kind=kOutput, calls=%fused_computation.2 | convolution fusion | flops 17179869184 | bytes 33554432 | tf_op jit(solution)/shard_map/lqx,lmq->xm/dot_general | solution.py:35
  314.0 6.1 %gather_fusion.1 = f32[64,128,128]{2,1,0:T(8,128)} fusion(f32[8,128,16,128]{3,1,2,0:T(8,128)} %fusion, s32[64]{0:T(128)S(1)} %fusion.14), kind=kCustom, calls=%fused_computation.1 | custom fusion | bytes 8389120 | tf_op jit(solution)/shard_map/gather | solution.py:21
  320.2 0.0 all-reduce.2.cloned.1.call-update
  320.2 71.8 %all-reduce.2.cloned.1.call-done = f32[64,128,128]{2,1,0:T(8,128)} async-done(((f32[64,128,128]{2,1,0:T(8,128)}), f32[64,128,128]{2,1,0:T(8,128)}) %all-reduce.2.cloned.1.call-update) | async-done | bytes 4194320 | tf_op jit(solution)/shard_map/psum | solution.py:42
  392.0 1.9 constant_dynamic-slice_fusion
  393.9 0.0 copy-done.1
  (2 shorter events, 0.0 us)
Async XLA Ops:
  6.5 45.7 %copy-start = (bf16[1,64,64]{2,1,0:T(8,128)(2,1)S(1)}, bf16[1,64,64]{2,1,0:T(8,128)(2,1)}, u32[]{:S(2)}) copy-start(bf16[1,64,64]{2,1,0:T(8,128)(2,1)} %param.6) | copy-start | bytes 24580
  33.1 256.8 %all-to-all-start = ((bf16[1,16,128,4096]{3,2,0,1:T(8,128)(2,1)}), bf16[1,16,128,4096]{3,2,0,1:T(8,128)(2,1)}, u32[]{:S(2)}, u32[]{:S(2)}) async-start(bf16[1,16,128,4096]{3,2,0,1:T(8,128)(2,1)} %bitcast_select_fusion), calls=%async_computation | async-start | bytes 33554432 | tf_op jit(solution)/shard_map/all_to_all | solution.py:31
  40.2 351.8 %all-reduce.2.cloned.1.call-start = ((), (), s32[]{:S(2)}) async-start(), calls=%async_computation.1 | async-start | bytes 8388608 | tf_op jit(solution)/shard_map/psum | solution.py:42
  52.2 5.8 %copy-start.2 = (bf16[1,64,64]{2,1,0:T(8,128)(2,1)S(1)}, bf16[1,64,64]{2,1,0:T(8,128)(2,1)}, u32[]{:S(2)}) copy-start(bf16[1,64,64]{2,1,0:T(8,128)(2,1)} %param.7) | copy-start | bytes 24580
  82.2 11.2 %copy-start.3 = (s32[64,2]{0,1:T(2,128)S(1)}, s32[64,2]{0,1:T(2,128)}, u32[]{:S(2)}) copy-start(s32[64,2]{0,1:T(2,128)} %param.9) | copy-start | bytes 1540
  289.9 103.9 %copy-start.1 = (bf16[1,64,64]{2,1,0:T(8,128)(2,1)S(1)}, bf16[1,64,64]{2,1,0:T(8,128)(2,1)}, u32[]{:S(2)}) copy-start(bf16[1,64,64]{2,1,0:T(8,128)(2,1)} %param.6) | copy-start | bytes 24580
Sparse Core Ops, SparseCore 0:
  320.3 71.6 all-reduce.1
where the time goes:
time: 402 us; the launch traced here: 401 us
  waiting for transfers between devices  268 us (67%)
  local copies, waits for them, and re-layouts  53.1 us (13%)
  matrix products  42.8 us (11%)
  other arithmetic  15.9 us (4%)
  between operations  13.4 us (3%)
  starting transfers between devices  7.13 us (2%)
    all_to_all x1, waiting for transfers between devices, on_device(): lax.all_to_all(outgoing, 'ex', split_axis=1, concat_axis=1, tiled=True)  197 us
    psum x1, waiting for transfers between devices, on_device(): total = lax.psum(terms, 'lay')  71.8 us
    dot_general x1, matrix products, on_device(): jnp.einsum('lqx,lmq->xm', left, right, preferred_element_type=jnp.float32)  24.1 us
    select_n x2, other arithmetic, on_device(): outgoing = jnp.take(blocks, wanted, axis=1)  15 us
    dot_general x1, matrix products, precondition(): jnp.einsum('lpo,loje->lpje', prec_out, inner, preferred_element_type=jnp....  12.9 us
    unnamed x9, local copies, waits for them, and re-layouts  12 us
    convert_element_type x1, local copies, waits for them, and re-layouts, precondition(): return outer.astype(jnp.bfloat16).reshape(layer_count, width, example_rows)  11.3 us
    dot_general x1, local copies, waits for them, and re-layouts, on_device(): jnp.einsum('lqx,lmq->xm', left, right, preferred_element_type=jnp.float32)  11.2 us
  transfers between devices with their start and end apart: 2, of which 2 were waited for; matrix products, arithmetic and copies ran while one was open for 13% of the time, Pallas kernels for 0%

commit v1 on v0

v1 whole, which is shorter than its diff:
```python
import functools

import jax
import jax.numpy as jnp
from jax import lax
from jax.experimental import pallas as pl
from jax.experimental.pallas import tpu as pltpu
from jax.sharding import PartitionSpec as P

BLOCK = 128
SIDE = 4
PARTS = ((0, 48), (96, 16))
VMEM = 60 * 2**20
bf16, f32 = jnp.bfloat16, jnp.float32


def params(limit=VMEM):
    return pltpu.CompilerParams(vmem_limit_bytes=limit)


def bundle_kernel(index_ref, block_ref, out_ref):
    out_ref[...] = block_ref[...]


def bundle(blocks, index, row, rows):
    count, width = index.shape[0], blocks.shape[-1]
    return pl.pallas_call(
        bundle_kernel,
        out_shape=jax.ShapeDtypeStruct((count, rows, width), blocks.dtype),
        grid_spec=pltpu.PrefetchScalarGridSpec(
            num_scalar_prefetch=1,
            grid=(count,),
            in_specs=[pl.BlockSpec((1, rows, width), lambda k, index: (index[k], row // rows, 0))],
            out_specs=pl.BlockSpec((1, rows, width), lambda k, index: (k, 0, 0)),
        ),
        compiler_params=params(8 * 2**20),
        cost_estimate=pl.CostEstimate(flops=0, bytes_accessed=4 * count * rows * width, transcendentals=0),
    )(index, blocks)


def left_kernel(rank, lanes, grads_ref, inner_w_ref, outer_w_ref, out_ref, inner_ref):
    group = inner_w_ref.shape[0]
    splits = rank // lanes
    per = group // splits
    width = grads_ref.shape[1]
    for g in range(width // group):
        part = grads_ref[:, g * group : (g + 1) * group]
        inner = lax.dot_general(
            inner_w_ref[...], part, (((1,), (1,)), ((), ())), preferred_element_type=f32
        ).astype(bf16)
        for s in range(splits):
            inner_ref[s, g * per : (g + 1) * per, :] = inner[s * per : (s + 1) * per]
    step = 256
    for s in range(splits):
        for at in range(0, rank * lanes, step):
            outer = jnp.dot(
                outer_w_ref[at : at + step, :], inner_ref[s], preferred_element_type=f32
            ).astype(bf16)
            for k in range(step // lanes):
                first = (at // lanes + k) * rank + s * lanes
                out_ref[first : first + lanes, :] = outer[k * lanes : (k + 1) * lanes]


def left_transposed(grads, prec_in, prec_out):
    examples, width = grads.shape
    rank = prec_in.shape[-1]
    lanes, outs, tile = 16, 4, 256
    splits = rank // lanes
    inner_w = jnp.einsum(
        "isj,oq->sojqi", prec_in.reshape(rank, splits, lanes), jnp.eye(outs, dtype=bf16)
    ).reshape(rank * outs, rank * outs)
    outer_w = jnp.einsum("po,jk->pjok", prec_out, jnp.eye(lanes, dtype=bf16)).reshape(
        rank * lanes, rank * lanes
    )
    return pl.pallas_call(
        functools.partial(left_kernel, rank, lanes),
        out_shape=jax.ShapeDtypeStruct((width, examples), bf16),
        grid=(examples // tile,),
        in_specs=[
            pl.BlockSpec((tile, width), lambda i: (i, 0)),
            pl.BlockSpec(inner_w.shape, lambda i: (0, 0)),
            pl.BlockSpec(outer_w.shape, lambda i: (0, 0)),
        ],
        out_specs=pl.BlockSpec((width, tile), lambda i: (0, i)),
        scratch_shapes=[pltpu.VMEM((splits, rank * lanes, tile), bf16)],
        compiler_params=params(),
        cost_estimate=pl.CostEstimate(
            flops=2 * examples * width * (rank * outs + rank * lanes),
            bytes_accessed=4 * examples * width,
            transcendentals=0,
        ),
    )(grads, inner_w, outer_w)


def tiles_kernel(count, block_ref, row_a_ref, row_b_ref, left_ref, *refs):
    rights, (keep_ref, give_ref, product_ref) = refs[:count], refs[count:]
    step = pl.program_id(0)
    per = left_ref.shape[1] // BLOCK
    at = 0
    for right_ref in rights:
        rows = right_ref.shape[0]
        product = jnp.dot(right_ref[...], left_ref[...], preferred_element_type=f32)
        for b in range(per):
            product_ref[step * per + b, at : at + rows, :] = product[:, b * BLOCK : (b + 1) * BLOCK]
        at += rows

    @pl.when(step == pl.num_programs(0) - 1)
    def _():
        half = keep_ref.shape[1] // 2
        for out_ref, base in ((keep_ref, 0), (give_ref, keep_ref.shape[0])):
            for q in range(out_ref.shape[0]):
                block = block_ref[base + q]
                row_a = pl.multiple_of(row_a_ref[base + q], 16)
                row_b = pl.multiple_of(row_b_ref[base + q], 16)
                out_ref[q, :half, :] = product_ref[block, pl.ds(row_a, half), :]
                out_ref[q, half:, :] = product_ref[block, pl.ds(row_b, half), :]


def tiles(left, rights, rows, block, row_a, row_b):
    width, examples = left.shape
    total = sum(r.shape[0] for r in rights)
    pairs = block.shape[0]
    step = 256
    out = jax.ShapeDtypeStruct((pairs // 2, 2 * rows, BLOCK), f32)
    out_spec = pl.BlockSpec(out.shape, lambda i, *_: (0, 0, 0))
    return pl.pallas_call(
        functools.partial(tiles_kernel, len(rights)),
        out_shape=(out, out),
        grid_spec=pltpu.PrefetchScalarGridSpec(
            num_scalar_prefetch=3,
            grid=(examples // step,),
            in_specs=[pl.BlockSpec((width, step), lambda i, *_: (0, i))]
            + [pl.BlockSpec(r.shape, lambda i, *_: (0, 0), pipeline_mode=pl.Buffered(1)) for r in rights],
            out_specs=(out_spec, out_spec),
            scratch_shapes=[pltpu.VMEM((examples // BLOCK, total, BLOCK), f32)],
        ),
        compiler_params=params(),
        cost_estimate=pl.CostEstimate(
            flops=2 * total * width * examples,
            bytes_accessed=2 * width * (examples + total),
            transcendentals=0,
        ),
    )(block, row_a, row_b, left, *rights)


def merge_kernel(keep_ref, got_ref, own_ref, *send_refs):
    per = own_ref.shape[0]
    own_ref[...] = keep_ref[:per] + got_ref[:per]
    for k, ref in enumerate(send_refs, 1):
        ref[...] = (keep_ref[k * per : (k + 1) * per] + got_ref[k * per : (k + 1) * per]).astype(bf16)


def merge(keep, got):
    shape = (keep.shape[0] // SIDE, *keep.shape[1:])
    return pl.pallas_call(
        merge_kernel,
        out_shape=(jax.ShapeDtypeStruct(shape, f32),)
        + (jax.ShapeDtypeStruct(shape, bf16),) * (SIDE - 1),
        compiler_params=params(32 * 2**20),
    )(keep, got)


def finish_kernel(*refs):
    ins, out_ref = refs[:-1], refs[-1]
    for k in range(out_ref.shape[0]):
        columns = []
        for at in range(0, len(ins), SIDE):
            total = ins[at][k]
            for ref in ins[at + 1 : at + SIDE]:
                total = total + ref[k].astype(f32)
            columns.append(total)
        out_ref[k] = jnp.concatenate(columns, axis=0).T


def finish(parts):
    ins = [x for part in parts for x in part]
    return pl.pallas_call(
        finish_kernel,
        out_shape=jax.ShapeDtypeStruct((ins[0].shape[0], BLOCK, BLOCK), f32),
        compiler_params=params(16 * 2**20),
    )(*ins)


def shift(array, dy, dx):
    pairs = [
        (y * SIDE + x, (y + dy) % SIDE * SIDE + (x + dx) % SIDE)
        for y in range(SIDE)
        for x in range(SIDE)
    ]
    return lax.ppermute(array, "ex", pairs)


def swap_cores(array):
    return lax.ppermute(array, "lay", [(i, i ^ 1) for i in range(2 * SIDE)])


def shift_z(array, dz):
    pairs = [(z * 2 + c, (z + dz) % SIDE * 2 + c) for z in range(SIDE) for c in range(2)]
    return lax.ppermute(array, "lay", pairs)


class Rounds:
    def __init__(self, window):
        self.done, self.window = [], window

    def __call__(self, *sends):
        ins = [s[0] for s in sends]
        if len(self.done) >= self.window:
            gate = self.done[-self.window]
            ins = lax.optimization_barrier((*ins, *gate))[: len(ins)]
        out = [shift(v, dy, dx) for v, (_, dy, dx) in zip(ins, sends)]
        self.done.append(out)
        return out


def turn(pieces):
    return [jnp.concatenate([p[k : k + 1] for p in pieces]) for k in range(SIDE)]


def on_device(grads, prec_in, prec_out, requests, pairs):
    grads, prec_in, prec_out = grads[0], prec_in[0], prec_out[0]
    examples, width = grads.shape
    block_count = examples // BLOCK
    blocks = grads.reshape(block_count, BLOCK, width)
    member, layer = lax.axis_index("ex"), lax.axis_index("lay")
    my_y, my_x = member // SIDE, member % SIDE
    my_z, my_core = layer // 2, layer % 2

    wanted = lax.dynamic_index_in_dim(requests, member, axis=1, keepdims=False).reshape(SIDE, SIDE)
    wanted = jnp.concatenate([wanted, wanted], 0)
    wanted = jnp.concatenate([wanted, wanted], 1)
    wanted = lax.dynamic_slice(wanted, (my_y, my_x), (SIDE, SIDE))

    rounds = Rounds(2)
    out_a, out_b, in_a, in_b = [], [], [], []
    for row, rows in PARTS:
        a = [bundle(blocks, wanted[d], row, rows) for d in range(SIDE)]
        b = [bundle(blocks, wanted[:, d], row + rows, rows) for d in range(SIDE)]
        a1, a3, b2 = rounds((a[1], 1, 0), (a[3], 3, 0), (b[2], 0, 2))
        b1, b3, a2 = rounds((b[1], 0, 1), (b[3], 0, 3), (a[2], 2, 0))
        out_a.append(turn([a[0], a1, a2, a3]))
        out_b.append(turn([b[0], b1, b2, b3]))
    for a, b in zip(out_a, out_b):
        a1, a3, b2 = rounds((a[1], 0, 1), (a[3], 0, 3), (b[2], 2, 0))
        b1, b3, a2 = rounds((b[1], 1, 0), (b[3], 3, 0), (a[2], 0, 2))
        in_a.append([a[0], a1, a2, a3])
        in_b.append([b[0], b1, b2, b3])

    left = left_transposed(grads, prec_in, prec_out)

    first = pairs[:, 0] - member * block_count
    dy = (my_y - pairs[:, 1] // SIDE) % SIDE
    dx = (my_x - pairs[:, 1] % SIDE) % SIDE
    listed = jnp.stack([first, dx * SIDE + dy, dy * SIDE + dx])
    listed = listed.reshape(3, SIDE, 2, -1)
    listed = jnp.concatenate([listed, listed], 1)
    listed = lax.dynamic_slice_in_dim(listed, my_z, SIDE, 1)
    listed = jnp.where(my_core == 0, listed, listed[:, :, ::-1])
    listed = listed.transpose(0, 2, 1, 3).reshape(3, -1)

    sums = []
    for (_, rows), a, b in zip(PARTS, in_a, in_b):
        rights = [r.reshape(SIDE * rows, width) for r in a + b]
        keep, give = tiles(
            left, rights, rows, listed[0], listed[1] * rows, (listed[2] + SIDE * SIDE) * rows
        )
        own, *sends = merge(keep, swap_cores(give))
        sums.append([own] + [shift_z(s, k) for k, s in enumerate(sends, 1)])
    return finish(sums)


def solution(mesh):
    placed = (P("lay", "ex", None), P("lay", None, None), P("lay", None, None), P(), P("ex", None))
    return jax.shard_map(
        on_device,
        mesh=mesh,
        in_specs=placed,
        out_specs=P(("ex", "lay"), None, None),
        check_vma=False,
    )
```

time: 402 us -> 326 us (0.81)
  waiting for transfers between devices: 268 us -> 119 us
  Pallas kernels: 0 us -> 74.2 us
  matrix products: 42.8 us -> 0 us
  starting transfers between devices: 7.13 us -> 45.1 us
  local copies, waits for them, and re-layouts: 53.1 us -> 71 us
  between operations: 13.4 us -> 0.68 us
    all_to_all x1 -> x0, waiting for transfers between devices: 197 us -> none  [on_device(): lax.all_to_all(outgoing, 'ex', split_axis=1, concat_axis=1, tiled=True)]
    ppermute x0 -> x32, waiting for transfers between devices: none -> 119 us  [the longest x24 108 us: shift(): return lax.ppermute(array, 'ex', pairs)]
    pallas_call x0 -> x22, Pallas kernels: none -> 74.2 us  [the longest x2 38.5 us: tiles(): pl.pallas_call(functools.partial(tiles_kernel, len(rights)), out_shape=(o...]
    psum x1 -> x0, waiting for transfers between devices: 71.8 us -> none  [on_device(): total = lax.psum(terms, 'lay')]
    ppermute x0 -> x32, starting transfers between devices: none -> 45.1 us  [the longest x24 35.2 us: shift(): return lax.ppermute(array, 'ex', pairs)]
    dot_general x3 -> x0, matrix products: 42.8 us -> none  [the longest x1 24.1 us: on_device(): jnp.einsum('lqx,lmq->xm', left, right, preferred_element_type=jnp.float32)]
    reshape x0 -> x3, local copies, waits for them, and re-layouts: none -> 30.7 us  [the longest x1 29.8 us: left_transposed(): jnp.einsum('po,jk->pjok', prec_out, jnp.eye(lanes, dtype=bf16))]
    slice x0 -> x17, local copies, waits for them, and re-layouts: none -> 17.6 us  [the longest x16 17.4 us: turn(): return [jnp.concatenate([p[k:k + 1] for p in pieces]) for k in range(SIDE)]]
  transfers between devices with their start and end apart: 2 -> 32, of which waited for: 2 -> 11; matrix products, arithmetic and copies ran while one was open for 13% -> 21% of each run, Pallas kernels for 0% -> 22%
where the time goes in v1:
time: 326 us
  waiting for transfers between devices  119 us (37%)
  Pallas kernels  74.2 us (23%)
  local copies, waits for them, and re-layouts  71 us (22%)
  starting transfers between devices  45.1 us (14%)
  other arithmetic  16.2 us (5%)
    ppermute x24, waiting for transfers between devices, shift(): return lax.ppermute(array, 'ex', pairs)  108 us
    pallas_call x2, Pallas kernels, tiles(): pl.pallas_call(functools.partial(tiles_kernel, len(rights)), out_shape=(o...  38.5 us
    ppermute x24, starting transfers between devices, shift(): return lax.ppermute(array, 'ex', pairs)  35.2 us
    reshape x1, local copies, waits for them, and re-layouts, left_transposed(): jnp.einsum('po,jk->pjok', prec_out, jnp.eye(lanes, dtype=bf16))  29.8 us
    unnamed x105, local copies, waits for them, and re-layouts  19 us
    pallas_call x16, Pallas kernels, bundle(): pl.pallas_call(bundle_kernel, out_shape=jax.ShapeDtypeStruct((count, rows...  18.8 us
    slice x16, local copies, waits for them, and re-layouts, turn(): return [jnp.concatenate([p[k:k + 1] for p in pieces]) for k in range(SIDE)]  17.4 us
    pallas_call x1, Pallas kernels, left_transposed(): pl.pallas_call(functools.partial(left_kernel, rank, lanes), out_shape=jax...  15.6 us
  transfers between devices with their start and end apart: 32, of which 11 were waited for; matrix products, arithmetic and copies ran while one was open for 21% of the time, Pallas kernels for 22%

profile of v1, /device:TPU:0, one launch (start us, length us, event | category | flops | bytes accessed | tf_op | source)
XLA Modules:
  0.0 325.6 jit_solution(1346896411363029279)
XLA Ops:
  1.1 3.4 %copy-done.2 = bf16[1,1024,4096]{2,1,0:T(8,128)(2,1)S(1)} copy-done((bf16[1,1024,4096]{2,1,0:T(8,128)(2,1)S(1)}, bf16[1,1024,4096]{2,1,0:T(8,128)(2,1)}, u32[]{:S(2)}) %copy-start.2) | copy-done | bytes 8388632
  4.5 2.3 shard_map.59
  6.8 3.1 collective-permute-start.2
  9.9 2.3 shard_map.58
  12.8 2.3 shard_map.57
  15.1 1.0 collective-permute-start
  16.3 2.3 shard_map.63
  18.7 2.8 collective-permute-start.5
  21.4 2.3 shard_map.62
  23.7 0.8 collective-permute-start.4
  24.5 3.4 %copy-done.3 = bf16[1,1024,4096]{2,1,0:T(8,128)(2,1)S(1)} copy-done((bf16[1,1024,4096]{2,1,0:T(8,128)(2,1)S(1)}, bf16[1,1024,4096]{2,1,0:T(8,128)(2,1)}, u32[]{:S(2)}) %copy-start.3) | copy-done | bytes 8388632
  33.0 1.2 copy-done.7
  34.8 0.8 copy-done.14
  45.4 0.9 reshape.289.inner_w_ref
  46.3 6.0 %multiply_bitcast_fusion = bf16[64,16,64,16]{3,2,1,0:T(8,128)(2,1)} fusion(bf16[64,64]{1,0:T(8,128)(2,1)S(1)} %bitcast.60, bf16[16,16]{1,0:T(8,128)(2,1)S(1)} %fusion.6), kind=kLoop, calls=%fused_computation | loop fusion | flops 1048576 | bytes 2105856 | tf_op jit(solution)/shard_map/po,jk->pjok/transpose | solution.py:72
  52.3 29.8 %reshape.290.outer_w_ref = bf16[1024,1024]{1,0:T(8,128)(2,1)} reshape(bf16[64,16,64,16]{3,2,1,0:T(8,128)(2,1)} %multiply_bitcast_fusion) | data formatting | bytes 4194304 | tf_op jit(solution)/shard_map/reshape | solution.py:72
  82.1 1.2 fusion.19
  84.6 1.9 fusion.27
  86.5 1.1 fusion.15
  88.4 0.9 collective-permute-start.3
  89.3 0.8 fusion.23
  90.1 15.6 %shard_map.55.left_ref = bf16[4096,1024]{1,0:T(8,128)(2,1)} custom-call(bf16[1024,4096]{1,0:T(8,128)(2,1)} %bitcast.36, bf16[256,256]{1,0:T(8,128)(2,1)} %reshape.289.inner_w_ref, bf16[1024,1024]{1,0:T(8,128)(2,1)} %reshape.290.outer_w_ref), custom_call_target="tpu_custom_call" | custom-call | flops 10737418240 | bytes 16777216 | tf_op jit(solution)/shard_map/pallas_call | solution.py:75
  105.7 2.0 collective-permute-start.6
  107.7 1.3 collective-permute-start.7
  109.0 2.0 collective-permute-start.8
  111.0 23.5 %collective-permute-done.3 = bf16[4,48,4096]{2,1,0:T(8,128)(2,1)} collective-permute-done((bf16[4,48,4096]{2,1,0:T(8,128)(2,1)S(1)}, bf16[4,48,4096]{2,1,0:T(8,128)(2,1)}, u32[]{:S(2)}, u32[]{:S(2)}) %collective-permute-start.3) | collective-permute-done | bytes 1572896 | tf_op jit(solution)/shard_map/ppermute | solution.py:190
  134.5 3.2 collective-permute-start.11
  137.7 1.5 fusion.22
  139.2 1.5 fusion.21
  140.7 1.5 fusion.20
  142.2 1.4 pad_maximum_fusion
  143.7 1.5 fusion.18
  145.1 1.5 fusion.17
  146.6 1.5 fusion.16
  150.1 1.4 pad_maximum_fusion.7
  152.5 2.2 collective-permute-start.12
  155.2 13.7 %collective-permute-done.12 = bf16[4,16,4096]{2,1,0:T(8,128)(2,1)S(1)} collective-permute-done((bf16[4,16,4096]{2,1,0:T(8,128)(2,1)S(1)}, bf16[4,16,4096]{2,1,0:T(8,128)(2,1)S(1)}, u32[]{:S(2)}, u32[]{:S(2)}) %collective-permute-start.12) | collective-permute-done | bytes 524320 | tf_op jit(solution)/shard_map/ppermute | solution.py:190
  168.9 1.4 collective-permute-start.13
  170.9 1.9 collective-permute-start.15
  172.8 1.8 collective-permute-start.16
  178.1 36.1 %collective-permute-done.9 = bf16[4,48,4096]{2,1,0:T(8,128)(2,1)S(1)} collective-permute-done((bf16[4,48,4096]{2,1,0:T(8,128)(2,1)S(1)}, bf16[4,48,4096]{2,1,0:T(8,128)(2,1)S(1)}, u32[]{:S(2)}, u32[]{:S(2)}) %collective-permute-start.9) | collective-permute-done | bytes 1572896 | tf_op jit(solution)/shard_map/ppermute | solution.py:190
  214.2 2.3 collective-permute-start.17
  216.7 0.9 pad_maximum_fusion.9
  217.6 0.9 pad_maximum_fusion.12
  218.5 9.2 %collective-permute-done.16 = bf16[4,48,4096]{2,1,0:T(8,128)(2,1)S(1)} collective-permute-done((bf16[4,48,4096]{2,1,0:T(8,128)(2,1)S(1)}, bf16[4,48,4096]{2,1,0:T(8,128)(2,1)S(1)}, u32[]{:S(2)}, u32[]{:S(2)}) %collective-permute-start.16) | collective-permute-done | bytes 1572896 | tf_op jit(solution)/shard_map/ppermute | solution.py:190
  228.4 6.2 %collective-permute-done.17 = bf16[4,48,4096]{2,1,0:T(8,128)(2,1)S(1)} collective-permute-done((bf16[4,48,4096]{2,1,0:T(8,128)(2,1)S(1)}, bf16[4,48,4096]{2,1,0:T(8,128)(2,1)S(1)}, u32[]{:S(2)}, u32[]{:S(2)}) %collective-permute-start.17) | collective-permute-done | bytes 1572896 | tf_op jit(solution)/shard_map/ppermute | solution.py:190
  234.6 1.5 collective-permute-start.23
  236.2 21.7 %shard_map.70 = (f32[32,96,128]{2,1,0:T(8,128)}, f32[32,96,128]{2,1,0:T(8,128)}) custom-call(s32[64]{0:T(128)} %squeeze.27.block_ref, s32[64]{0:T(128)} %mul.49.row_a_ref, s32[64]{0:T(128)} %mul.51.row_b_ref, bf16[4096,1024]{1,0:T(8,128)(2,1)} %shard_map.55.left_ref, bf16[192,4096]{1,0:T(8,128)(2,1)} %bitcast.55, bf16[192,4096]{1,0:T(8,128)(2,1)} %bitcast.61, ...), custom_call_target="tpu_custom_call" | custom-call | flops 12884901888 | bytes 20971520 | tf_op jit(solution)/shard_map/pallas_call | solution.py:126
  258.1 1.9 collective-permute-start.25
  260.0 3.0 collective-permute-start.26
  263.1 1.8 pad_maximum_fusion.8
  265.0 1.9 pad_maximum_fusion.15
  266.9 5.3 %collective-permute-done.24 = bf16[4,16,4096]{2,1,0:T(8,128)(2,1)S(1)} collective-permute-done((bf16[4,16,4096]{2,1,0:T(8,128)(2,1)S(1)}, bf16[4,16,4096]{2,1,0:T(8,128)(2,1)S(1)}, u32[]{:S(2)}, u32[]{:S(2)}) %collective-permute-start.24) | collective-permute-done | bytes 524320 | tf_op jit(solution)/shard_map/ppermute | solution.py:190
  272.3 1.9 collective-permute-done.25
  274.2 12.4 %collective-permute-done.26 = bf16[4,16,4096]{2,1,0:T(8,128)(2,1)S(1)} collective-permute-done((bf16[4,16,4096]{2,1,0:T(8,128)(2,1)S(1)}, bf16[4,16,4096]{2,1,0:T(8,128)(2,1)S(1)}, u32[]{:S(2)}, u32[]{:S(2)}) %collective-permute-start.26) | collective-permute-done | bytes 524320 | tf_op jit(solution)/shard_map/ppermute | solution.py:190
  287.6 16.8 %shard_map.74 = (f32[32,32,128]{2,1,0:T(8,128)}, f32[32,32,128]{2,1,0:T(8,128)}) custom-call(s32[64]{0:T(128)} %squeeze.27.block_ref, s32[64]{0:T(128)} %mul.53.row_a_ref, s32[64]{0:T(128)} %mul.55.row_b_ref, bf16[4096,1024]{1,0:T(8,128)(2,1)} %shard_map.55.left_ref, bf16[64,4096]{1,0:T(8,128)(2,1)} %bitcast.57, bf16[64,4096]{1,0:T(8,128)(2,1)} %bitcast.20.refs_1_, ...), custom_call_target="tpu_custom_call" | custom-call | flops 4294967296 | bytes 12582912 | tf_op jit(solution)/shard_map/pallas_call | solution.py:126
  304.6 2.0 collective-permute-start.19
  306.6 3.6 %collective-permute-start.20 = (bf16[8,96,128]{2,1,0:T(8,128)(2,1)S(1)}, bf16[8,96,128]{2,1,0:T(8,128)(2,1)S(1)}, u32[]{:S(2)}, u32[]{:S(2)}) collective-permute-start(bf16[8,96,128]{2,1,0:T(8,128)(2,1)S(1)} %get-tuple-element.51), channel_id=1, source_target_pairs={{0,4},{1,5},{2,6},{3,7},{4,0},{5,1},{6,2},{7,3},{8,12},{9,13},{10,... | collective-permute-start | bytes 589832 | tf_op jit(solution)/shard_map/ppermute | solution.py:199
  310.1 1.0 collective-permute-start.21
  311.2 1.1 collective-permute-start.29
  312.8 7.6 %collective-permute-done.29.refs_5_ = bf16[8,32,128]{2,1,0:T(8,128)(2,1)S(1)} collective-permute-done((bf16[8,32,128]{2,1,0:T(8,128)(2,1)S(1)}, bf16[8,32,128]{2,1,0:T(8,128)(2,1)S(1)}, u32[]{:S(2)}, u32[]{:S(2)}) %collective-permute-start.29) | collective-permute-done | bytes 65568 | tf_op jit(solution)/shard_map/ppermute | solution.py:199
  320.3 1.7 collective-permute-start.31
  322.5 2.2 collective-permute-done.31.refs_7_
  324.6 1.0 shard_map.76
  (182 shorter events, 30.3 us)
Async XLA Ops:
  1.1 3.4 %copy-start.2 = (bf16[1,1024,4096]{2,1,0:T(8,128)(2,1)S(1)}, bf16[1,1024,4096]{2,1,0:T(8,128)(2,1)}, u32[]{:S(2)}) copy-start(bf16[1,1024,4096]{2,1,0:T(8,128)(2,1)} %param.5) | copy-start | bytes 25165828
  6.8 80.8 %collective-permute-start.2 = (bf16[4,48,4096]{2,1,0:T(8,128)(2,1)}, bf16[4,48,4096]{2,1,0:T(8,128)(2,1)}, u32[]{:S(2)}, u32[]{:S(2)}) collective-permute-start(bf16[4,48,4096]{2,1,0:T(8,128)(2,1)} %shard_map.59), channel_id=1, source_target_pairs={{0,96},{8,104},{16,112},{24,120},{32,0},{40,8},{48,16},{56,24},{64... | collective-permute-start | bytes 4718600 | tf_op jit(solution)/shard_map/ppermute | solution.py:190
  9.9 6.4 %slice-start = ((s8[8388608]{0:T(1024)(128)(4,1)}), s8[4194304]{0:T(1024)(128)(4,1)S(1)}, s32[]{:S(2)}) async-start(s8[8388608]{0:T(1024)(128)(4,1)} %bitcast.40), calls=%async_computation | async-start | bytes 8388608
  12.2 96.8 %collective-permute-start.1 = (bf16[4,48,4096]{2,1,0:T(8,128)(2,1)}, bf16[4,48,4096]{2,1,0:T(8,128)(2,1)}, u32[]{:S(2)}, u32[]{:S(2)}) collective-permute-start(bf16[4,48,4096]{2,1,0:T(8,128)(2,1)} %shard_map.58), channel_id=1, source_target_pairs={{0,64},{8,72},{16,80},{24,88},{32,96},{40,104},{48,112},{56,120},{... | collective-permute-start | bytes 4718600 | tf_op jit(solution)/shard_map/ppermute | solution.py:190
  12.8 3.5 %slice-start.1 = ((s8[8388608]{0:T(1024)(128)(4,1)}), s8[4194304]{0:T(1024)(128)(4,1)S(1)}, s32[]{:S(2)}) async-start(s8[8388608]{0:T(1024)(128)(4,1)} %bitcast.40), calls=%async_computation.1 | async-start | bytes 8388608
  15.1 90.6 %collective-permute-start = (bf16[4,48,4096]{2,1,0:T(8,128)(2,1)}, bf16[4,48,4096]{2,1,0:T(8,128)(2,1)}, u32[]{:S(2)}, u32[]{:S(2)}) collective-permute-start(bf16[4,48,4096]{2,1,0:T(8,128)(2,1)} %shard_map.57), channel_id=1, source_target_pairs={{0,32},{8,40},{16,48},{24,56},{32,64},{40,72},{48,80},{56,88},{64,... | collective-permute-start | bytes 4718600 | tf_op jit(solution)/shard_map/ppermute | solution.py:190
  18.7 92.3 %collective-permute-start.5 = (bf16[4,48,4096]{2,1,0:T(8,128)(2,1)}, bf16[4,48,4096]{2,1,0:T(8,128)(2,1)}, u32[]{:S(2)}, u32[]{:S(2)}) collective-permute-start(bf16[4,48,4096]{2,1,0:T(8,128)(2,1)} %shard_map.63), channel_id=1, source_target_pairs={{0,24},{8,0},{16,8},{24,16},{32,56},{40,32},{48,40},{56,48},{64,88... | collective-permute-start | bytes 4718600 | tf_op jit(solution)/shard_map/ppermute | solution.py:190
  23.7 82.0 %collective-permute-start.4 = (bf16[4,48,4096]{2,1,0:T(8,128)(2,1)}, bf16[4,48,4096]{2,1,0:T(8,128)(2,1)}, u32[]{:S(2)}, u32[]{:S(2)}) collective-permute-start(bf16[4,48,4096]{2,1,0:T(8,128)(2,1)} %shard_map.62), channel_id=1, source_target_pairs={{0,16},{8,24},{16,0},{24,8},{32,48},{40,56},{48,32},{56,40},{64,80... | collective-permute-start | bytes 4718600 | tf_op jit(solution)/shard_map/ppermute | solution.py:190
  24.5 3.4 %copy-start.3 = (bf16[1,1024,4096]{2,1,0:T(8,128)(2,1)S(1)}, bf16[1,1024,4096]{2,1,0:T(8,128)(2,1)}, u32[]{:S(2)}) copy-start(bf16[1,1024,4096]{2,1,0:T(8,128)(2,1)} %param.5) | copy-start | bytes 25165828
  41.5 3.7 %copy-start.37 = (bf16[1,64,64]{2,1,0:T(8,128)(2,1)S(1)}, bf16[1,64,64]{2,1,0:T(8,128)(2,1)}, u32[]{:S(2)}) copy-start(bf16[1,64,64]{2,1,0:T(8,128)(2,1)} %param.6) | copy-start | bytes 24580
  41.5 4.8 %copy-start.38 = (bf16[1,64,64]{2,1,0:T(8,128)(2,1)S(1)}, bf16[1,64,64]{2,1,0:T(8,128)(2,1)}, u32[]{:S(2)}) copy-start(bf16[1,64,64]{2,1,0:T(8,128)(2,1)} %param.7) | copy-start | bytes 24580
  86.5 1.8 copy-start.8
  86.5 2.7 copy-start.5
  88.4 46.1 %collective-permute-start.3 = (bf16[4,48,4096]{2,1,0:T(8,128)(2,1)S(1)}, bf16[4,48,4096]{2,1,0:T(8,128)(2,1)}, u32[]{:S(2)}, u32[]{:S(2)}) collective-permute-start(bf16[4,48,4096]{2,1,0:T(8,128)(2,1)S(1)} %copy-done.8), channel_id=1, source_target_pairs={{0,8},{8,16},{16,24},{24,0},{32,40},{40,48},{48,56},{56,32},{64,72... | collective-permute-start | bytes 4718600 | tf_op jit(solution)/shard_map/ppermute | solution.py:190
  90.1 17.6 %copy-start.19 = (bf16[4,16,4096]{2,1,0:T(8,128)(2,1)S(1)}, bf16[4,16,4096]{2,1,0:T(8,128)(2,1)}, u32[]{:S(2)}) copy-start(bf16[4,16,4096]{2,1,0:T(8,128)(2,1)} %copy-done.18) | copy-start | bytes 1572868
  90.1 19.0 %copy-start.17 = (bf16[4,16,4096]{2,1,0:T(8,128)(2,1)S(1)}, bf16[4,16,4096]{2,1,0:T(8,128)(2,1)}, u32[]{:S(2)}) copy-start(bf16[4,16,4096]{2,1,0:T(8,128)(2,1)} %copy-done.16) | copy-start | bytes 1572868
  90.1 44.4 %copy-start.15 = (bf16[4,16,4096]{2,1,0:T(8,128)(2,1)S(1)}, bf16[4,16,4096]{2,1,0:T(8,128)(2,1)}, u32[]{:S(2)}) copy-start(bf16[4,16,4096]{2,1,0:T(8,128)(2,1)} %copy-done.14) | copy-start | bytes 1572868
  90.1 44.4 %copy-start.13 = (bf16[4,16,4096]{2,1,0:T(8,128)(2,1)S(1)}, bf16[4,16,4096]{2,1,0:T(8,128)(2,1)}, u32[]{:S(2)}) copy-start(bf16[4,16,4096]{2,1,0:T(8,128)(2,1)} %copy-done.12) | copy-start | bytes 1572868
  105.7 46.2 %collective-permute-start.6 = (bf16[4,16,4096]{2,1,0:T(8,128)(2,1)}, bf16[4,16,4096]{2,1,0:T(8,128)(2,1)S(1)}, u32[]{:S(2)}, u32[]{:S(2)}) collective-permute-start(bf16[4,16,4096]{2,1,0:T(8,128)(2,1)} %copy-done.20), channel_id=1, source_target_pairs={{0,32},{8,40},{16,48},{24,56},{32,64},{40,72},{48,80},{56,88},{64,... | collective-permute-start | bytes 1572872 | tf_op jit(solution)/shard_map/ppermute | solution.py:190
  107.7 47.4 %collective-permute-start.7 = (bf16[4,16,4096]{2,1,0:T(8,128)(2,1)S(1)}, bf16[4,16,4096]{2,1,0:T(8,128)(2,1)S(1)}, u32[]{:S(2)}, u32[]{:S(2)}) collective-permute-start(bf16[4,16,4096]{2,1,0:T(8,128)(2,1)S(1)} %copy-done.19), channel_id=1, source_target_pairs={{0,96},{8,104},{16,112},{24,120},{32,0},{40,8},{48,16},{56,24},{64... | collective-permute-start | bytes 1572872 | tf_op jit(solution)/shard_map/ppermute | solution.py:190
  109.0 46.1 %collective-permute-start.8 = (bf16[4,16,4096]{2,1,0:T(8,128)(2,1)S(1)}, bf16[4,16,4096]{2,1,0:T(8,128)(2,1)S(1)}, u32[]{:S(2)}, u32[]{:S(2)}) collective-permute-start(bf16[4,16,4096]{2,1,0:T(8,128)(2,1)S(1)} %copy-done.17), channel_id=1, source_target_pairs={{0,16},{8,24},{16,0},{24,8},{32,48},{40,56},{48,32},{56,40},{64,80... | collective-permute-start | bytes 1572872 | tf_op jit(solution)/shard_map/ppermute | solution.py:190
  134.5 20.7 %collective-permute-start.10 = (bf16[4,16,4096]{2,1,0:T(8,128)(2,1)S(1)}, bf16[4,16,4096]{2,1,0:T(8,128)(2,1)S(1)}, u32[]{:S(2)}, u32[]{:S(2)}) collective-permute-start(bf16[4,16,4096]{2,1,0:T(8,128)(2,1)S(1)} %copy-done.15), channel_id=1, source_target_pairs={{0,8},{8,16},{16,24},{24,0},{32,40},{40,48},{48,56},{56,32},{64,72... | collective-permute-start | bytes 1572872 | tf_op jit(solution)/shard_map/ppermute | solution.py:190
  134.5 20.7 %collective-permute-start.11 = (bf16[4,16,4096]{2,1,0:T(8,128)(2,1)S(1)}, bf16[4,16,4096]{2,1,0:T(8,128)(2,1)S(1)}, u32[]{:S(2)}, u32[]{:S(2)}) collective-permute-start(bf16[4,16,4096]{2,1,0:T(8,128)(2,1)S(1)} %copy-done.13), channel_id=1, source_target_pairs={{0,24},{8,0},{16,8},{24,16},{32,56},{40,32},{48,40},{56,48},{64,88... | collective-permute-start | bytes 1572872 | tf_op jit(solution)/shard_map/ppermute | solution.py:190
  140.7 1.5 copy-start.28
  146.6 1.5 copy-start.27
  151.5 3.2 copy-start.22
  152.5 16.4 %collective-permute-start.12 = (bf16[4,16,4096]{2,1,0:T(8,128)(2,1)S(1)}, bf16[4,16,4096]{2,1,0:T(8,128)(2,1)S(1)}, u32[]{:S(2)}, u32[]{:S(2)}) collective-permute-start(bf16[4,16,4096]{2,1,0:T(8,128)(2,1)S(1)} %copy-done.11), channel_id=1, source_target_pairs={{0,64},{8,72},{16,80},{24,88},{32,96},{40,104},{48,112},{56,120},{... | collective-permute-start | bytes 1572872 | tf_op jit(solution)/shard_map/ppermute | solution.py:190
  155.1 59.1 %collective-permute-start.9 = (bf16[4,48,4096]{2,1,0:T(8,128)(2,1)S(1)}, bf16[4,48,4096]{2,1,0:T(8,128)(2,1)S(1)}, u32[]{:S(2)}, u32[]{:S(2)}) collective-permute-start(bf16[4,48,4096]{2,1,0:T(8,128)(2,1)S(1)} %get-tuple-element.38), channel_id=1, source_target_pairs={{0,8},{8,16},{16,24},{24,0},{32,40},{40,48},{48,56},{56,32},{64,72... | collective-permute-start | bytes 4718600 | tf_op jit(solution)/shard_map/ppermute | solution.py:190
  168.9 59.5 %collective-permute-start.13 = (bf16[4,48,4096]{2,1,0:T(8,128)(2,1)S(1)}, bf16[4,48,4096]{2,1,0:T(8,128)(2,1)S(1)}, u32[]{:S(2)}, u32[]{:S(2)}) collective-permute-start(bf16[4,48,4096]{2,1,0:T(8,128)(2,1)S(1)} %pad_maximum_fusion.6), channel_id=1, source_target_pairs={{0,16},{8,24},{16,0},{24,8},{32,48},{40,56},{48,32},{56,40},{64,80... | collective-permute-start | bytes 4718600 | tf_op jit(solution)/shard_map/ppermute | solution.py:190
  170.3 48.2 %collective-permute-start.14 = (bf16[4,48,4096]{2,1,0:T(8,128)(2,1)S(1)}, bf16[4,48,4096]{2,1,0:T(8,128)(2,1)S(1)}, u32[]{:S(2)}, u32[]{:S(2)}) collective-permute-start(bf16[4,48,4096]{2,1,0:T(8,128)(2,1)S(1)} %get-tuple-element.43), channel_id=1, source_target_pairs={{0,24},{8,0},{16,8},{24,16},{32,56},{40,32},{48,40},{56,48},{64,88... | collective-permute-start | bytes 4718600 | tf_op jit(solution)/shard_map/ppermute | solution.py:190
  170.9 57.5 %collective-permute-start.15 = (bf16[4,48,4096]{2,1,0:T(8,128)(2,1)S(1)}, bf16[4,48,4096]{2,1,0:T(8,128)(2,1)S(1)}, u32[]{:S(2)}, u32[]{:S(2)}) collective-permute-start(bf16[4,48,4096]{2,1,0:T(8,128)(2,1)S(1)} %get-tuple-element.44), channel_id=1, source_target_pairs={{0,32},{8,40},{16,48},{24,56},{32,64},{40,72},{48,80},{56,88},{64,... | collective-permute-start | bytes 4718600 | tf_op jit(solution)/shard_map/ppermute | solution.py:190
  172.8 54.9 %collective-permute-start.16 = (bf16[4,48,4096]{2,1,0:T(8,128)(2,1)S(1)}, bf16[4,48,4096]{2,1,0:T(8,128)(2,1)S(1)}, u32[]{:S(2)}, u32[]{:S(2)}) collective-permute-start(bf16[4,48,4096]{2,1,0:T(8,128)(2,1)S(1)} %pad_maximum_fusion.3), channel_id=1, source_target_pairs={{0,64},{8,72},{16,80},{24,88},{32,96},{40,104},{48,112},{56,120},{... | collective-permute-start | bytes 4718600 | tf_op jit(solution)/shard_map/ppermute | solution.py:190
  176.0 40.4 %copy-start.36 = (bf16[1,16,4096]{2,1,0:T(8,128)(2,1)S(1)}, bf16[1,16,4096]{2,1,0:T(8,128)(2,1)}, u32[]{:S(2)}) copy-start(bf16[1,16,4096]{2,1,0:T(8,128)(2,1)} %get-tuple-element.109) | copy-start | bytes 393220
  176.7 39.8 %copy-start.35 = (bf16[1,16,4096]{2,1,0:T(8,128)(2,1)S(1)}, bf16[1,16,4096]{2,1,0:T(8,128)(2,1)}, u32[]{:S(2)}) copy-start(bf16[1,16,4096]{2,1,0:T(8,128)(2,1)} %get-tuple-element.122) | copy-start | bytes 393220
  177.4 39.2 %copy-start.29 = (bf16[1,16,4096]{2,1,0:T(8,128)(2,1)S(1)}, bf16[1,16,4096]{2,1,0:T(8,128)(2,1)}, u32[]{:S(2)}) copy-start(bf16[1,16,4096]{2,1,0:T(8,128)(2,1)} %get-tuple-element.123) | copy-start | bytes 393220
  177.4 39.3 %copy-start.30 = (bf16[1,16,4096]{2,1,0:T(8,128)(2,1)S(1)}, bf16[1,16,4096]{2,1,0:T(8,128)(2,1)}, u32[]{:S(2)}) copy-start(bf16[1,16,4096]{2,1,0:T(8,128)(2,1)} %get-tuple-element.124) | copy-start | bytes 393220
  214.2 3.4 %copy-start.40 = (bf16[4,48,4096]{2,1,0:T(8,128)(2,1)}, bf16[4,48,4096]{2,1,0:T(8,128)(2,1)S(1)}, u32[]{:S(2)}) copy-start(bf16[4,48,4096]{2,1,0:T(8,128)(2,1)S(1)} %collective-permute-done.9) | copy-start | bytes 4718596
  214.2 20.4 %collective-permute-start.17 = (bf16[4,48,4096]{2,1,0:T(8,128)(2,1)S(1)}, bf16[4,48,4096]{2,1,0:T(8,128)(2,1)S(1)}, u32[]{:S(2)}, u32[]{:S(2)}) collective-permute-start(bf16[4,48,4096]{2,1,0:T(8,128)(2,1)S(1)} %get-tuple-element.46), channel_id=1, source_target_pairs={{0,96},{8,104},{16,112},{24,120},{32,0},{40,8},{48,16},{56,24},{64... | collective-permute-start | bytes 4718600 | tf_op jit(solution)/shard_map/ppermute | solution.py:190
  218.5 17.6 %copy-start.42 = (bf16[4,48,4096]{2,1,0:T(8,128)(2,1)}, bf16[4,48,4096]{2,1,0:T(8,128)(2,1)S(1)}, u32[]{:S(2)}) copy-start(bf16[4,48,4096]{2,1,0:T(8,128)(2,1)S(1)} %collective-permute-done.14) | copy-start | bytes 4718596
  227.7 8.4 %copy-start.44 = (bf16[4,48,4096]{2,1,0:T(8,128)(2,1)}, bf16[4,48,4096]{2,1,0:T(8,128)(2,1)S(1)}, u32[]{:S(2)}) copy-start(bf16[4,48,4096]{2,1,0:T(8,128)(2,1)S(1)} %collective-permute-done.16) | copy-start | bytes 4718596
  227.7 32.3 %collective-permute-start.22 = (bf16[4,16,4096]{2,1,0:T(8,128)(2,1)}, bf16[4,16,4096]{2,1,0:T(8,128)(2,1)}, u32[]{:S(2)}, u32[]{:S(2)}) collective-permute-start(bf16[4,16,4096]{2,1,0:T(8,128)(2,1)} %get-tuple-element.53), channel_id=1, source_target_pairs={{0,8},{8,16},{16,24},{24,0},{32,40},{40,48},{48,56},{56,32},{64,72... | collective-permute-start | bytes 1572872 | tf_op jit(solution)/shard_map/ppermute | solution.py:190
  228.4 7.8 %copy-start.41 = (bf16[4,48,4096]{2,1,0:T(8,128)(2,1)}, bf16[4,48,4096]{2,1,0:T(8,128)(2,1)S(1)}, u32[]{:S(2)}) copy-start(bf16[4,48,4096]{2,1,0:T(8,128)(2,1)S(1)} %collective-permute-done.13) | copy-start | bytes 4718596
  228.4 7.8 %copy-start.43 = (bf16[4,48,4096]{2,1,0:T(8,128)(2,1)}, bf16[4,48,4096]{2,1,0:T(8,128)(2,1)S(1)}, u32[]{:S(2)}) copy-start(bf16[4,48,4096]{2,1,0:T(8,128)(2,1)S(1)} %collective-permute-done.15) | copy-start | bytes 4718596
  234.6 1.5 copy-start.45
  234.6 28.4 %collective-permute-start.23 = (bf16[4,16,4096]{2,1,0:T(8,128)(2,1)S(1)}, bf16[4,16,4096]{2,1,0:T(8,128)(2,1)}, u32[]{:S(2)}, u32[]{:S(2)}) collective-permute-start(bf16[4,16,4096]{2,1,0:T(8,128)(2,1)S(1)} %pad_maximum_fusion.14), channel_id=1, source_target_pairs={{0,16},{8,24},{16,0},{24,8},{32,48},{40,56},{48,32},{56,40},{64,80... | collective-permute-start | bytes 1572872 | tf_op jit(solution)/shard_map/ppermute | solution.py:190
  236.2 27.0 %copy-start.33 = (bf16[1,16,4096]{2,1,0:T(8,128)(2,1)S(1)}, bf16[1,16,4096]{2,1,0:T(8,128)(2,1)}, u32[]{:S(2)}) copy-start(bf16[1,16,4096]{2,1,0:T(8,128)(2,1)} %get-tuple-element.125) | copy-start | bytes 393220
  236.2 28.8 %copy-start.34 = (bf16[1,16,4096]{2,1,0:T(8,128)(2,1)S(1)}, bf16[1,16,4096]{2,1,0:T(8,128)(2,1)}, u32[]{:S(2)}) copy-start(bf16[1,16,4096]{2,1,0:T(8,128)(2,1)} %get-tuple-element.106) | copy-start | bytes 393220
  257.9 46.5 %collective-permute-start.18 = (f32[32,96,128]{2,1,0:T(8,128)}, f32[32,96,128]{2,1,0:T(8,128)S(1)}, u32[]{:S(2)}, u32[]{:S(2)}) collective-permute-start(f32[32,96,128]{2,1,0:T(8,128)} %get-tuple-element.48), channel_id=1, source_target_pairs={{0,1},{1,0},{2,3},{3,2},{4,5},{5,4},{6,7},{7,6},{8,9},{9,8},{10,11... | collective-permute-start | bytes 4718600 | tf_op jit(solution)/shard_map/ppermute | solution.py:194
  257.9 14.3 %collective-permute-start.24 = (bf16[4,16,4096]{2,1,0:T(8,128)(2,1)S(1)}, bf16[4,16,4096]{2,1,0:T(8,128)(2,1)S(1)}, u32[]{:S(2)}, u32[]{:S(2)}) collective-permute-start(bf16[4,16,4096]{2,1,0:T(8,128)(2,1)S(1)} %get-tuple-element.55), channel_id=1, source_target_pairs={{0,24},{8,0},{16,8},{24,16},{32,56},{40,32},{48,40},{56,48},{64,88... | collective-permute-start | bytes 1572872 | tf_op jit(solution)/shard_map/ppermute | solution.py:190
  258.1 16.1 %collective-permute-start.25 = (bf16[4,16,4096]{2,1,0:T(8,128)(2,1)}, bf16[4,16,4096]{2,1,0:T(8,128)(2,1)S(1)}, u32[]{:S(2)}, u32[]{:S(2)}) collective-permute-start(bf16[4,16,4096]{2,1,0:T(8,128)(2,1)} %get-tuple-element.56), channel_id=1, source_target_pairs={{0,32},{8,40},{16,48},{24,56},{32,64},{40,72},{48,80},{56,88},{64,... | collective-permute-start | bytes 1572872 | tf_op jit(solution)/shard_map/ppermute | solution.py:190
  260.0 26.6 %collective-permute-start.26 = (bf16[4,16,4096]{2,1,0:T(8,128)(2,1)S(1)}, bf16[4,16,4096]{2,1,0:T(8,128)(2,1)S(1)}, u32[]{:S(2)}, u32[]{:S(2)}) collective-permute-start(bf16[4,16,4096]{2,1,0:T(8,128)(2,1)S(1)} %pad_maximum_fusion.11), channel_id=1, source_target_pairs={{0,64},{8,72},{16,80},{24,88},{32,96},{40,104},{48,112},{56,120},{... | collective-permute-start | bytes 1572872 | tf_op jit(solution)/shard_map/ppermute | solution.py:190
  263.0 23.6 %collective-permute-start.27 = (bf16[4,16,4096]{2,1,0:T(8,128)(2,1)S(1)}, bf16[4,16,4096]{2,1,0:T(8,128)(2,1)S(1)}, u32[]{:S(2)}, u32[]{:S(2)}) collective-permute-start(bf16[4,16,4096]{2,1,0:T(8,128)(2,1)S(1)} %get-tuple-element.58), channel_id=1, source_target_pairs={{0,96},{8,104},{16,112},{24,120},{32,0},{40,8},{48,16},{56,24},{64... | collective-permute-start | bytes 1572872 | tf_op jit(solution)/shard_map/ppermute | solution.py:190
  272.2 14.3 %copy-start.46 = (bf16[4,16,4096]{2,1,0:T(8,128)(2,1)}, bf16[4,16,4096]{2,1,0:T(8,128)(2,1)S(1)}, u32[]{:S(2)}) copy-start(bf16[4,16,4096]{2,1,0:T(8,128)(2,1)S(1)} %collective-permute-done.24) | copy-start | bytes 1572868
  274.2 12.4 %copy-start.47 = (bf16[4,16,4096]{2,1,0:T(8,128)(2,1)}, bf16[4,16,4096]{2,1,0:T(8,128)(2,1)S(1)}, u32[]{:S(2)}) copy-start(bf16[4,16,4096]{2,1,0:T(8,128)(2,1)S(1)} %collective-permute-done.25) | copy-start | bytes 1572868
  287.6 16.8 %copy-start.9 = (f32[32,96,128]{2,1,0:T(8,128)S(1)}, f32[32,96,128]{2,1,0:T(8,128)}, u32[]{:S(2)}) copy-start(f32[32,96,128]{2,1,0:T(8,128)} %get-tuple-element.47.keep_ref) | copy-start | bytes 4718596
  304.4 6.8 %collective-permute-start.28 = (f32[32,32,128]{2,1,0:T(8,128)}, f32[32,32,128]{2,1,0:T(8,128)S(1)}, u32[]{:S(2)}, u32[]{:S(2)}) collective-permute-start(f32[32,32,128]{2,1,0:T(8,128)} %get-tuple-element.60), channel_id=1, source_target_pairs={{0,1},{1,0},{2,3},{3,2},{4,5},{5,4},{6,7},{7,6},{8,9},{9,8},{10,11... | collective-permute-start | bytes 1572872 | tf_op jit(solution)/shard_map/ppermute | solution.py:194
  304.4 6.8 %copy-start.21 = (f32[32,32,128]{2,1,0:T(8,128)S(1)}, f32[32,32,128]{2,1,0:T(8,128)}, u32[]{:S(2)}) copy-start(f32[32,32,128]{2,1,0:T(8,128)} %get-tuple-element.59.keep_ref) | copy-start | bytes 1572868
  304.4 21.2 %copy-start.1 = (s32[16,16]{1,0:T(8,128)S(1)}, s32[16,16]{1,0:T(8,128)}, u32[]{:S(2)}) copy-start(s32[16,16]{1,0:T(8,128)} %param.8) | copy-start | bytes 3076
  304.6 20.1 %collective-permute-start.19 = (bf16[8,96,128]{2,1,0:T(8,128)(2,1)S(1)}, bf16[8,96,128]{2,1,0:T(8,128)(2,1)S(1)}, u32[]{:S(2)}, u32[]{:S(2)}) collective-permute-start(bf16[8,96,128]{2,1,0:T(8,128)(2,1)S(1)} %get-tuple-element.50), channel_id=1, source_target_pairs={{0,2},{1,3},{2,4},{3,5},{4,6},{5,7},{6,0},{7,1},{8,10},{9,11},{10,... | collective-permute-start | bytes 589832 | tf_op jit(solution)/shard_map/ppermute | solution.py:199
  306.6 18.1 %collective-permute-start.20 = (bf16[8,96,128]{2,1,0:T(8,128)(2,1)S(1)}, bf16[8,96,128]{2,1,0:T(8,128)(2,1)S(1)}, u32[]{:S(2)}, u32[]{:S(2)}) collective-permute-start(bf16[8,96,128]{2,1,0:T(8,128)(2,1)S(1)} %get-tuple-element.51), channel_id=1, source_target_pairs={{0,4},{1,5},{2,6},{3,7},{4,0},{5,1},{6,2},{7,3},{8,12},{9,13},{10,... | collective-permute-start | bytes 589832 | tf_op jit(solution)/shard_map/ppermute | solution.py:199
  310.1 14.5 %collective-permute-start.21 = (bf16[8,96,128]{2,1,0:T(8,128)(2,1)S(1)}, bf16[8,96,128]{2,1,0:T(8,128)(2,1)S(1)}, u32[]{:S(2)}, u32[]{:S(2)}) collective-permute-start(bf16[8,96,128]{2,1,0:T(8,128)(2,1)S(1)} %get-tuple-element.52), channel_id=1, source_target_pairs={{0,6},{1,7},{2,0},{3,1},{4,2},{5,3},{6,4},{7,5},{8,14},{9,15},{10,... | collective-permute-start | bytes 589832 | tf_op jit(solution)/shard_map/ppermute | solution.py:199
  311.2 9.1 %collective-permute-start.29 = (bf16[8,32,128]{2,1,0:T(8,128)(2,1)S(1)}, bf16[8,32,128]{2,1,0:T(8,128)(2,1)S(1)}, u32[]{:S(2)}, u32[]{:S(2)}) collective-permute-start(bf16[8,32,128]{2,1,0:T(8,128)(2,1)S(1)} %get-tuple-element.62), channel_id=1, source_target_pairs={{0,2},{1,3},{2,4},{3,5},{4,6},{5,7},{6,0},{7,1},{8,10},{9,11},{10,... | collective-permute-start | bytes 196616 | tf_op jit(solution)/shard_map/ppermute | solution.py:199
  312.3 10.2 %collective-permute-start.30 = (bf16[8,32,128]{2,1,0:T(8,128)(2,1)S(1)}, bf16[8,32,128]{2,1,0:T(8,128)(2,1)S(1)}, u32[]{:S(2)}, u32[]{:S(2)}) collective-permute-start(bf16[8,32,128]{2,1,0:T(8,128)(2,1)S(1)} %get-tuple-element.63), channel_id=1, source_target_pairs={{0,4},{1,5},{2,6},{3,7},{4,0},{5,1},{6,2},{7,3},{8,12},{9,13},{10,... | collective-permute-start | bytes 196616 | tf_op jit(solution)/shard_map/ppermute | solution.py:199
  320.3 4.3 %collective-permute-start.31 = (bf16[8,32,128]{2,1,0:T(8,128)(2,1)S(1)}, bf16[8,32,128]{2,1,0:T(8,128)(2,1)S(1)}, u32[]{:S(2)}, u32[]{:S(2)}) collective-permute-start(bf16[8,32,128]{2,1,0:T(8,128)(2,1)S(1)} %get-tuple-element.64), channel_id=1, source_target_pairs={{0,6},{1,7},{2,0},{3,1},{4,2},{5,3},{6,4},{7,5},{8,14},{9,15},{10,... | collective-permute-start | bytes 196616 | tf_op jit(solution)/shard_map/ppermute | solution.py:199
  (20 other events, 19.4 us)

commit v2 on v1

v2 whole, which is shorter than its diff:
```python
import functools

import jax
import jax.numpy as jnp
from jax import lax
from jax.experimental import pallas as pl
from jax.experimental.pallas import tpu as pltpu
from jax.sharding import PartitionSpec as P

BLOCK = 128
SIDE = 4
PARTS = ((0, 48), (96, 16))
STEP = 256
VMEM = 60 * 2**20
bf16, f32 = jnp.bfloat16, jnp.float32


def params(limit=VMEM):
    return pltpu.CompilerParams(vmem_limit_bytes=limit)


def run_copies(copies):
    for copy in copies:
        copy.start()
    for copy in copies:
        copy.wait()


def moved(elements):
    return pl.CostEstimate(flops=0, bytes_accessed=4 * elements, transcendentals=0)


def gather_kernel(starts, index_ref, blocks_ref, *refs):
    outs, sems = refs[:-1], refs[-1]
    copies = []
    for n, (out_ref, start) in enumerate(zip(outs, starts)):
        count, rows = out_ref.shape[:2]
        for k in range(count):
            source = blocks_ref.at[index_ref[n * count + k], pl.ds(start, rows)]
            copies.append(pltpu.make_async_copy(source, out_ref.at[k], sems.at[n * count + k]))
    run_copies(copies)


def gather(blocks, bundles):
    width = blocks.shape[-1]
    outs = [jax.ShapeDtypeStruct((SIDE, rows, width), blocks.dtype) for _, _, rows in bundles]
    return pl.pallas_call(
        functools.partial(gather_kernel, [start for _, start, _ in bundles]),
        out_shape=outs,
        grid_spec=pltpu.PrefetchScalarGridSpec(
            num_scalar_prefetch=1,
            grid=(1,),
            in_specs=[pl.BlockSpec(memory_space=pl.ANY)],
            out_specs=[pl.BlockSpec(memory_space=pl.ANY)] * len(outs),
            scratch_shapes=[pltpu.SemaphoreType.DMA((SIDE * len(outs),))],
        ),
        compiler_params=params(),
        cost_estimate=moved(sum(SIDE * rows * width for _, _, rows in bundles)),
    )(jnp.concatenate([index for index, _, _ in bundles]), blocks)


def turn_kernel(*refs):
    pieces, outs, sems = refs[:SIDE], refs[SIDE:-1], refs[-1]
    copies = [
        pltpu.make_async_copy(piece.at[k + 1], out.at[i], sems.at[k * SIDE + i])
        for k, out in enumerate(outs)
        for i, piece in enumerate(pieces)
    ]
    run_copies(copies)


def turn(pieces):
    outs = [jax.ShapeDtypeStruct(pieces[0].shape, pieces[0].dtype)] * (SIDE - 1)
    return pl.pallas_call(
        turn_kernel,
        out_shape=outs,
        in_specs=[pl.BlockSpec(memory_space=pl.ANY)] * SIDE,
        out_specs=[pl.BlockSpec(memory_space=pl.ANY)] * (SIDE - 1),
        scratch_shapes=[pltpu.SemaphoreType.DMA((SIDE * (SIDE - 1),))],
        compiler_params=params(),
        cost_estimate=moved((SIDE - 1) * pieces[0].size),
    )(*pieces)


LANES = 16
OUTS = 4


def iota(shape, dim):
    return lax.broadcasted_iota(jnp.int32, shape, dim)


def one_hot(picked, shape):
    return (picked == iota(shape, 1)).astype(f32).astype(bf16)


def left_kernel(grads_ref, prec_in_ref, prec_out_ref, out_ref, inner_w_ref, outer_w_ref, inner_ref):
    rank = prec_in_ref.shape[0]
    group = rank * OUTS
    splits = rank // LANES
    per = group // splits
    width = grads_ref.shape[1]
    step = 256

    @pl.when(pl.program_id(0) == 0)
    def _():
        row = iota((group, rank), 0)
        rows = one_hot(row // per * LANES + row % LANES, (group, rank))
        columns = one_hot(row % rank, (group, rank))
        spread = lax.dot_general(
            rows, prec_in_ref[...], (((1,), (1,)), ((), ())), preferred_element_type=f32
        ).astype(bf16)
        full = lax.dot_general(spread, columns, (((1,), (1,)), ((), ())), preferred_element_type=f32)
        same = iota((group, group), 0) % per // LANES == iota((group, group), 1) // rank
        inner_w_ref[...] = jnp.where(same, full, 0.0).astype(bf16)
        columns = one_hot(iota((rank * LANES, rank), 0) // LANES, (rank * LANES, rank))
        for at in range(0, rank * LANES, step):
            rows = one_hot((iota((step, rank), 0) + at) // LANES, (step, rank))
            spread = jnp.dot(rows, prec_out_ref[...], preferred_element_type=f32).astype(bf16)
            full = lax.dot_general(spread, columns, (((1,), (1,)), ((), ())), preferred_element_type=f32)
            shape = (step, rank * LANES)
            same = iota(shape, 0) % LANES == iota(shape, 1) % LANES
            outer_w_ref[at : at + step, :] = jnp.where(same, full, 0.0).astype(bf16)

    for g in range(width // group):
        part = grads_ref[:, g * group : (g + 1) * group]
        inner = lax.dot_general(
            inner_w_ref[...], part, (((1,), (1,)), ((), ())), preferred_element_type=f32
        ).astype(bf16)
        for s in range(splits):
            inner_ref[s, g * per : (g + 1) * per, :] = inner[s * per : (s + 1) * per]
    for s in range(splits):
        for at in range(0, rank * LANES, step):
            outer = jnp.dot(
                outer_w_ref[at : at + step, :], inner_ref[s], preferred_element_type=f32
            ).astype(bf16)
            for k in range(step // LANES):
                first = (at // LANES + k) * rank + s * LANES
                out_ref[0, first : first + LANES, :] = outer[k * LANES : (k + 1) * LANES]


def left_transposed(grads, prec_in, prec_out):
    examples, width = grads.shape
    rank = prec_in.shape[-1]
    tile = STEP
    factor = pl.BlockSpec((rank, rank), lambda i: (0, 0))
    return pl.pallas_call(
        left_kernel,
        out_shape=jax.ShapeDtypeStruct((examples // tile, width, tile), bf16),
        grid=(examples // tile,),
        in_specs=[pl.BlockSpec((tile, width), lambda i: (i, 0)), factor, factor],
        out_specs=pl.BlockSpec((1, width, tile), lambda i: (i, 0, 0)),
        scratch_shapes=[
            pltpu.VMEM((rank * OUTS, rank * OUTS), bf16),
            pltpu.VMEM((rank * LANES, rank * LANES), bf16),
            pltpu.VMEM((rank // LANES, rank * LANES, tile), bf16),
        ],
        compiler_params=params(),
        cost_estimate=pl.CostEstimate(
            flops=2 * examples * width * (rank * OUTS + rank * LANES),
            bytes_accessed=4 * examples * width,
            transcendentals=0,
        ),
    )(grads, prec_in, prec_out)


def fetch(rights, right_ref, sems):
    copies, at = [], 0
    for k, ref in enumerate(rights):
        rows = ref.shape[0]
        copies.append(pltpu.make_async_copy(ref, right_ref.at[pl.ds(at, rows)], sems.at[k]))
        at += rows
    run_copies(copies)


def multiply(right_ref, left_ref, product_ref, first_block, at):
    rows = right_ref.shape[0]
    product = jnp.dot(right_ref[...], left_ref[0], preferred_element_type=f32)
    for b in range(left_ref.shape[2] // BLOCK):
        product_ref[first_block + b, at : at + rows, :] = product[:, b * BLOCK : (b + 1) * BLOCK]


def early_kernel(owns, count, left_ref, *refs):
    rights, (out_ref, right_ref, sems) = refs[:count], refs[count:]
    rights = [ref.at[0] for ref in rights[:owns]] + [ref for ref in rights[owns:]]

    @pl.when(pl.program_id(0) == 0)
    def _():
        fetch(rights, right_ref, sems)

    multiply(right_ref, left_ref, out_ref, 0, 0)


def cost(total, width, examples):
    return pl.CostEstimate(
        flops=2 * total * width * examples,
        bytes_accessed=2 * width * (examples + total) + 4 * total * examples,
        transcendentals=0,
    )


def early_products(left, owns, rights):
    groups, width, _ = left.shape
    examples = groups * STEP
    rows = owns[0].shape[1]
    total = rows * len(owns) + sum(r.shape[0] for r in rights)
    owned, rights = len(owns), [*owns, *rights]
    return pl.pallas_call(
        functools.partial(early_kernel, owned, len(rights)),
        out_shape=jax.ShapeDtypeStruct((examples // BLOCK, total, BLOCK), f32),
        grid=(examples // STEP,),
        in_specs=[pl.BlockSpec((1, width, STEP), lambda i: (i, 0, 0))]
        + [pl.BlockSpec(memory_space=pl.ANY)] * len(rights),
        out_specs=pl.BlockSpec((STEP // BLOCK, total, BLOCK), lambda i: (i, 0, 0)),
        scratch_shapes=[
            pltpu.VMEM((total, width), bf16),
            pltpu.SemaphoreType.DMA((len(rights),)),
        ],
        compiler_params=params(),
        cost_estimate=cost(total, width, examples),
    )(left, *rights)


def tiles_kernel(count, block_ref, row_a_ref, row_b_ref, left_ref, early_ref, *refs):
    rights = refs[:count]
    keep_ref, give_ref, product_ref, right_ref, sems, early_sem = refs[count:]
    step = pl.program_id(0)
    early = early_ref.shape[1]
    early_copy = pltpu.make_async_copy(early_ref, product_ref.at[:, pl.ds(0, early)], early_sem)

    @pl.when(step == 0)
    def _():
        early_copy.start()
        fetch(rights, right_ref, sems)

    multiply(right_ref, left_ref, product_ref, step * (left_ref.shape[2] // BLOCK), early)

    @pl.when(step == pl.num_programs(0) - 1)
    def _():
        early_copy.wait()
        half = keep_ref.shape[1] // 2
        for out_ref, base in ((give_ref, keep_ref.shape[0]), (keep_ref, 0)):
            for q in range(out_ref.shape[0]):
                block = block_ref[base + q]
                row_a = pl.multiple_of(row_a_ref[base + q], 16)
                row_b = pl.multiple_of(row_b_ref[base + q], 16)
                out_ref[q, :half, :] = product_ref[block, pl.ds(row_a, half), :]
                out_ref[q, half:, :] = product_ref[block, pl.ds(row_b, half), :]


def tiles(left, early, rights, rows, block, row_a, row_b):
    groups, width, _ = left.shape
    examples = groups * STEP
    total = sum(r.shape[0] for r in rights)
    pairs = block.shape[0]
    out = jax.ShapeDtypeStruct((pairs // 2, 2 * rows, BLOCK), f32)
    out_spec = pl.BlockSpec(out.shape, lambda i, *_: (0, 0, 0))
    return pl.pallas_call(
        functools.partial(tiles_kernel, len(rights)),
        out_shape=(out, out),
        grid_spec=pltpu.PrefetchScalarGridSpec(
            num_scalar_prefetch=3,
            grid=(examples // STEP,),
            in_specs=[pl.BlockSpec((1, width, STEP), lambda i, *_: (i, 0, 0))]
            + [pl.BlockSpec(memory_space=pl.ANY)] * (1 + len(rights)),
            out_specs=(out_spec, out_spec),
            scratch_shapes=[
                pltpu.VMEM((examples // BLOCK, early.shape[1] + total, BLOCK), f32),
                pltpu.VMEM((total, width), bf16),
                pltpu.SemaphoreType.DMA((len(rights),)),
                pltpu.SemaphoreType.DMA(()),
            ],
        ),
        compiler_params=params(),
        cost_estimate=cost(total, width, examples),
    )(block, row_a, row_b, left, early, *rights)


def merge_kernel(keep_ref, got_ref, own_ref, *send_refs):
    per = own_ref.shape[0]
    own_ref[...] = keep_ref[:per] + got_ref[:per]
    for k, ref in enumerate(send_refs, 1):
        ref[...] = (keep_ref[k * per : (k + 1) * per] + got_ref[k * per : (k + 1) * per]).astype(bf16)


def merge(keep, got):
    shape = (keep.shape[0] // SIDE, *keep.shape[1:])
    return pl.pallas_call(
        merge_kernel,
        out_shape=(jax.ShapeDtypeStruct(shape, f32),)
        + (jax.ShapeDtypeStruct(shape, bf16),) * (SIDE - 1),
        compiler_params=params(32 * 2**20),
    )(keep, got)


def finish_kernel(*refs):
    ins, out_ref = refs[:-1], refs[-1]
    for k in range(out_ref.shape[0]):
        columns = []
        for at in range(0, len(ins), SIDE):
            total = ins[at][k]
            for ref in ins[at + 1 : at + SIDE]:
                total = total + ref[k].astype(f32)
            columns.append(total)
        out_ref[k] = jnp.concatenate(columns, axis=0).T


def finish(parts):
    ins = [x for part in parts for x in part]
    return pl.pallas_call(
        finish_kernel,
        out_shape=jax.ShapeDtypeStruct((ins[0].shape[0], BLOCK, BLOCK), f32),
        compiler_params=params(16 * 2**20),
    )(*ins)


def shift(array, dy, dx):
    pairs = [
        (y * SIDE + x, (y + dy) % SIDE * SIDE + (x + dx) % SIDE)
        for y in range(SIDE)
        for x in range(SIDE)
    ]
    return lax.ppermute(array, "ex", pairs)


def swap_cores(array):
    return lax.ppermute(array, "lay", [(i, i ^ 1) for i in range(2 * SIDE)])


def shift_z(array, dz):
    pairs = [(z * 2 + c, (z + dz) % SIDE * 2 + c) for z in range(SIDE) for c in range(2)]
    return lax.ppermute(array, "lay", pairs)


IN_FLIGHT = 5


class Sender:
    def __init__(self):
        self.done = []

    def __call__(self, array, dy, dx):
        if len(self.done) >= IN_FLIGHT:
            array, _ = lax.optimization_barrier((array, self.done[-IN_FLIGHT]))
        self.done.append(shift(array, dy, dx))
        return self.done[-1]


def on_device(grads, prec_in, prec_out, requests, pairs):
    grads, prec_in, prec_out = grads[0], prec_in[0], prec_out[0]
    examples, width = grads.shape
    block_count = examples // BLOCK
    blocks = grads.reshape(block_count, BLOCK, width)
    member, layer = lax.axis_index("ex"), lax.axis_index("lay")
    my_y, my_x = member // SIDE, member % SIDE
    my_z, my_core = layer // 2, layer % 2

    wanted = lax.dynamic_index_in_dim(requests, member, axis=1, keepdims=False).reshape(SIDE, SIDE)
    wanted = jnp.concatenate([wanted, wanted], 0)
    wanted = jnp.concatenate([wanted, wanted], 1)
    wanted = lax.dynamic_slice(wanted, (my_y, my_x), (SIDE, SIDE))

    send = Sender()
    need = [(0, 1), (0, 3), (1, 2), (1, 1), (1, 3), (0, 2), (0, 0), (1, 0)]
    out = []
    for row, rows in PARTS:
        listed = [
            (wanted[:, d] if f else wanted[d], row + f * rows, rows) for f, d in need
        ]
        out.append(listed)
    calls = [out[0][:3], out[0][3:6], out[0][6:] + out[1]]
    made = [v for call in calls for v in gather(blocks, call)]
    parts = []
    for p in range(len(PARTS)):
        got = dict(zip(need, made[p * len(need) : (p + 1) * len(need)]))
        for f, d in need[:6]:
            got[f, d] = send(got[f, d], 0 if f else d, d if f else 0)
        parts.append([[got[f, d] for d in range(SIDE)] for f in range(2)])
    late_in = []
    for a, b in parts:
        sides = [turn(a), turn(b)]
        got = {}
        for f, d in need[:6]:
            got[f, d] = send(sides[f][d - 1], d if f else 0, 0 if f else d)
        late_in.append(got)

    left = left_transposed(grads, prec_in, prec_out)

    own, early, late = need[6:], need[:3], need[3:6]
    order = own + early + late

    def place(f, d):
        return sum(jnp.where(d == k, at, 0) for at, (n, k) in enumerate(order) if n == f)

    first = pairs[:, 0] - member * block_count
    dy = (my_y - pairs[:, 1] // SIDE) % SIDE
    dx = (my_x - pairs[:, 1] % SIDE) % SIDE
    listed = jnp.stack([first, place(0, dx) * SIDE + dy, place(1, dy) * SIDE + dx])
    listed = listed.reshape(3, SIDE, 2, -1)
    listed = jnp.concatenate([listed, listed], 1)
    listed = lax.dynamic_slice_in_dim(listed, my_z, SIDE, 1)
    listed = jnp.where(my_core == 0, listed, listed[:, :, ::-1])
    listed = listed.transpose(0, 2, 1, 3).reshape(3, -1)

    sums = []
    for (_, rows), sides, got in zip(PARTS, parts, late_in):
        flat = {key: got[key].reshape(-1, width) for key in early + late}
        owns = [piece for f, _ in own for piece in sides[f]]
        products = early_products(left, owns, [flat[key] for key in early])
        rest = [flat[key] for key in late]
        if sums:
            *rest, _ = lax.optimization_barrier((*rest, sums[-1]))
        keep, give = tiles(left, products, rest, rows, listed[0], listed[1] * rows, listed[2] * rows)
        mine, *sends = merge(keep, swap_cores(give))
        sums.append([mine] + [shift_z(s, k) for k, s in enumerate(sends, 1)])
    return finish(sums)


def solution(mesh):
    placed = (P("lay", "ex", None), P("lay", None, None), P("lay", None, None), P(), P("ex", None))
    return jax.shard_map(
        on_device,
        mesh=mesh,
        in_specs=placed,
        out_specs=P(("ex", "lay"), None, None),
        check_vma=False,
    )
```

time: 326 us -> 1080 us (3.31)
  Pallas kernels: 74.2 us -> 963 us
  local copies, waits for them, and re-layouts: 71 us -> 6.35 us
  waiting for transfers between devices: 119 us -> 60.9 us
  other arithmetic: 16.2 us -> 0.85 us
    pallas_call x17 -> x10, Pallas kernels: 34.5 us -> 940 us  [the longest x3 514 us: gather(): pl.pallas_call(functools.partial(gather_kernel, [start for _, start, _ in...]
    ppermute x24, waiting for transfers between devices: 108 us -> 54.7 us  [shift(): return lax.ppermute(array, 'ex', pairs)]
    reshape x2 -> x0, local copies, waits for them, and re-layouts: 30.6 us -> none  [the longest x1 29.8 us: left_transposed(): jnp.einsum('po,jk->pjok', prec_out, jnp.eye(lanes, dtype=bf16))]
    slice x17 -> x1, local copies, waits for them, and re-layouts: 17.6 us -> 0.22 us  [on_device(): wanted[:, d]]
    pallas_call x2, Pallas kernels: 38.5 us -> 21.1 us  [tiles(): pl.pallas_call(functools.partial(tiles_kernel, len(rights)), out_shape=(o...]
    unnamed x105 -> x30, local copies, waits for them, and re-layouts: 19 us -> 1.8 us
  transfers between devices with their start and end apart: 32 -> 32, of which waited for: 11 -> 8; matrix products, arithmetic and copies ran while one was open for 21% -> 0% of each run, Pallas kernels for 22% -> 74%
where the time goes in v2:
time: 1080 us
  Pallas kernels  963 us (89%)
  waiting for transfers between devices  60.9 us (6%)
  starting transfers between devices  48 us (4%)
    pallas_call x3, Pallas kernels, gather(): pl.pallas_call(functools.partial(gather_kernel, [start for _, start, _ in...  514 us
    pallas_call x4, Pallas kernels, turn(): pl.pallas_call(turn_kernel, out_shape=outs, in_specs=[pl.BlockSpec(memory...  386 us
    ppermute x24, waiting for transfers between devices, shift(): return lax.ppermute(array, 'ex', pairs)  54.7 us
    ppermute x24, starting transfers between devices, shift(): return lax.ppermute(array, 'ex', pairs)  34.7 us
    pallas_call x2, Pallas kernels, early_products(): pl.pallas_call(functools.partial(early_kernel, owned, len(rights)), out_s...  23.7 us
  transfers between devices with their start and end apart: 32, of which 8 were waited for; matrix products, arithmetic and copies ran while one was open for 0% of the time, Pallas kernels for 74%

profile of v2, /device:TPU:0, one launch (start us, length us, event | category | flops | bytes accessed | tf_op | source)
XLA Modules:
  0.0 1079.3 jit_solution(9353490390506790950)
XLA Ops:
  0.0 0.7 copy-done
  0.7 0.2 dynamic-slice_reduce_fusion
  0.9 0.1 reshape.326
  1.0 0.1 add_add_fusion
  1.1 0.2 slice_reduce_fusion
  1.4 0.7 pad_add_fusion
  2.0 144.8 %shard_map.57 = (bf16[4,48,4096]{2,1,0:T(8,128)(2,1)}, bf16[4,48,4096]{2,1,0:T(8,128)(2,1)}, bf16[4,48,4096]{2,1,0:T(8,128)(2,1)}) custom-call(s32[12]{0:T(128)} %get-tuple-element.147.index_ref, bf16[8,128,4096]{2,1,0:T(8,128)(2,1)} %bitcast.26), custom_call_target="tpu_custom_call" | custom-call | bytes 9437184 | tf_op jit(solution)/shard_map/pallas_call | solution.py:47
  146.8 1.7 collective-permute-start
  148.6 3.0 collective-permute-start.4
  151.6 1.7 collective-permute-start.2
  153.3 144.8 %shard_map.58 = (bf16[4,48,4096]{2,1,0:T(8,128)(2,1)}, bf16[4,48,4096]{2,1,0:T(8,128)(2,1)}, bf16[4,48,4096]{2,1,0:T(8,128)(2,1)}) custom-call(s32[12]{0:T(128)} %get-tuple-element.148.index_ref, bf16[8,128,4096]{2,1,0:T(8,128)(2,1)} %bitcast.27), custom_call_target="tpu_custom_call" | custom-call | bytes 9437184 | tf_op jit(solution)/shard_map/pallas_call | solution.py:47
  298.1 2.1 collective-permute-start.1
  300.2 1.1 collective-permute-start.5
  301.3 0.9 collective-permute-start.3
  302.2 0.6 concatenate.22.index_ref
  302.8 224.5 %shard_map.56 = (bf16[4,48,4096]{2,1,0:T(8,128)(2,1)}, bf16[4,48,4096]{2,1,0:T(8,128)(2,1)}, bf16[4,16,4096]{2,1,0:T(8,128)(2,1)}, bf16[4,16,4096]{2,1,0:T(8,128...) custom-call(s32[40]{0:T(128)} %concatenate.22.index_ref, ...), custom_call_target="tpu_custom_call" | custom-call | bytes 14680064 | tf_op jit(solution)/shard_map/pallas_call | solution.py:47
  527.3 1.1 collective-permute-start.6
  528.5 144.1 %shard_map.59 = (bf16[4,48,4096]{2,1,0:T(8,128)(2,1)}, bf16[4,48,4096]{2,1,0:T(8,128)(2,1)}, bf16[4,48,4096]{2,1,0:T(8,128)(2,1)}) custom-call(bf16[4,48,4096]{2,1,0:T(8,128)(2,1)} %get-tuple-element.67.refs_0_, bf16[4,48,4096]{2,1,0:T(8,128)(2,1)} %copy-done.10, bf16[4,48,4096]{2,1,0:T(8,128)(2,1)} %collective-permute-done.1.refs_2_, ...), custom_call_target="tpu_custom_call" | custom-call | bytes 9437184 | tf_op jit(solution)/shard_map/pallas_call | solution.py:74
  672.6 0.7 collective-permute-start.7
  673.3 0.1 collective-permute-start.10
  673.4 4.0 collective-permute-start.8
  677.4 1.0 collective-permute-start.14
  678.4 0.1 squeeze.28
  678.5 144.1 %shard_map.60 = (bf16[4,48,4096]{2,1,0:T(8,128)(2,1)}, bf16[4,48,4096]{2,1,0:T(8,128)(2,1)}, bf16[4,48,4096]{2,1,0:T(8,128)(2,1)}) custom-call(bf16[4,48,4096]{2,1,0:T(8,128)(2,1)} %get-tuple-element.72.refs_0_.refs_4_, bf16[4,48,4096]{2,1,0:T(8,128)(2,1)} %collective-permute-done.3.refs_1_.refs_5_, ...), custom_call_target="tpu_custom_call" | custom-call | bytes 9437184 | tf_op jit(solution)/shard_map/pallas_call | solution.py:74
  822.7 1.6 collective-permute-start.11
  824.4 1.7 collective-permute-start.9
  826.1 0.1 sub.70
  826.2 2.1 collective-permute-start.15
  828.4 0.6 squeeze.29.block_ref
  829.0 0.6 mul.49.row_a_ref
  829.6 0.7 mul.51.row_b_ref
  830.2 38.6 %collective-permute-done.15.refs_2_ = bf16[4,16,4096]{2,1,0:T(8,128)(2,1)S(1)} collective-permute-done((bf16[4,16,4096]{2,1,0:T(8,128)(2,1)}, bf16[4,16,4096]{2,1,0:T(8,128)(2,1)S(1)}, u32[]{:S(2)}, u32[]{:S(2)}) %collective-permute-start.15) | collective-permute-done | bytes 524320 | tf_op jit(solution)/shard_map/ppermute | solution.py:323
  868.8 3.2 collective-permute-start.16
  872.0 0.3 collective-permute-start.17
  872.3 16.0 %shard_map.55.left_ref = bf16[4,4096,256]{2,1,0:T(8,128)(2,1)} custom-call(bf16[1024,4096]{1,0:T(8,128)(2,1)} %bitcast.29, bf16[64,64]{1,0:T(8,128)(2,1)} %bitcast.31, bf16[64,64]{1,0:T(8,128)(2,1)} %bitcast.32), custom_call_target="tpu_custom_call" | custom-call | flops 10737418240 | bytes 16777216 | tf_op jit(solution)/shard_map/pallas_call | solution.py:147
  888.4 15.0 %shard_map.61.early_ref = f32[8,960,128]{2,1,0:T(8,128)} custom-call(bf16[4,4096,256]{2,1,0:T(8,128)(2,1)} %shard_map.55.left_ref, bf16[4,48,4096]{2,1,0:T(8,128)(2,1)} %get-tuple-element.67.refs_0_, bf16[4,48,4096]{2,1,0:T(8,128)(2,1)} %copy-done.10, bf16[4,48,4096]{2,1,0:T(8,128)(2,1)} %collective-permute-done.1.refs_2_, ...), custom_call_target="tpu_custom_call" | custom-call | flops 8053063680 | bytes 20185088 | tf_op jit(solution)/shard_map/pallas_call | solution.py:208
  903.4 1.1 collective-permute-done.13
  904.5 0.6 collective-permute-done.17
  905.0 12.5 %shard_map.62 = (f32[32,96,128]{2,1,0:T(8,128)}, f32[32,96,128]{2,1,0:T(8,128)}) custom-call(s32[64]{0:T(128)} %squeeze.29.block_ref, s32[64]{0:T(128)} %mul.49.row_a_ref, s32[64]{0:T(128)} %mul.51.row_b_ref, bf16[4,4096,256]{2,1,0:T(8,128)(2,1)} %shard_map.55.left_ref, f32[8,960,128]{2,1,0:T(8,128)} %shard_map.61.early_ref, ...), custom_call_target="tpu_custom_call" | custom-call | flops 4831838208 | bytes 15466496 | tf_op jit(solution)/shard_map/pallas_call | solution.py:258
  917.5 0.1 collective-permute-start.18
  917.6 48.9 %shard_map.64 = (bf16[4,16,4096]{2,1,0:T(8,128)(2,1)}, bf16[4,16,4096]{2,1,0:T(8,128)(2,1)}, bf16[4,16,4096]{2,1,0:T(8,128)(2,1)}) custom-call(bf16[4,16,4096]{2,1,0:T(8,128)(2,1)} %get-tuple-element.106.refs_0_, bf16[4,16,4096]{2,1,0:T(8,128)(2,1)} %copy-done.7, bf16[4,16,4096]{2,1,0:T(8,128)(2,1)} %copy-done.8, bf16[4,16,4096]{2,1,0:T(8,128)(2,1)} %copy-done.4), custom_call_target="tpu_custom_call" | custom-call | bytes 3145728 | tf_op jit(solution)/shard_map/pallas_call | solution.py:74
  966.5 1.0 collective-permute-start.22
  967.5 2.3 collective-permute-start.23
  969.8 48.9 %shard_map.65 = (bf16[4,16,4096]{2,1,0:T(8,128)(2,1)}, bf16[4,16,4096]{2,1,0:T(8,128)(2,1)}, bf16[4,16,4096]{2,1,0:T(8,128)(2,1)}) custom-call(bf16[4,16,4096]{2,1,0:T(8,128)(2,1)} %get-tuple-element.107.refs_0_.refs_4_, bf16[4,16,4096]{2,1,0:T(8,128)(2,1)} %copy-done.5, bf16[4,16,4096]{2,1,0:T(8,128)(2,1)} %copy-done.6, bf16[4,16,4096]{2,1,0:T(8,128)(2,1)} %copy-done.9), custom_call_target="tpu_custom_call" | custom-call | bytes 3145728 | tf_op jit(solution)/shard_map/pallas_call | solution.py:74
  1018.8 4.1 collective-permute-start.24
  1022.9 0.9 collective-permute-start.27
  1023.8 0.7 mul.53.row_a_ref
  1024.5 0.7 mul.55.row_b_ref
  1025.2 0.8 shard_map.63
  1026.0 1.9 collective-permute-start.19
  1027.9 6.3 collective-permute-done.25
  1034.2 3.9 collective-permute-start.20
  1038.0 8.1 collective-permute-done.24
  1046.2 4.0 collective-permute-start.21
  1050.2 8.7 shard_map.66.early_ref
  1059.0 8.6 shard_map.67
  1067.6 0.1 collective-permute-start.28
  1067.7 2.1 collective-permute-done.28.got_ref
  1069.8 1.0 copy-done.3
  1071.0 1.9 collective-permute-start.30
  1072.9 1.4 collective-permute-start.31
  1074.2 3.5 collective-permute-done.29.refs_5_
  1077.7 0.6 collective-permute-done.31.refs_7_
  1078.3 1.0 shard_map.69
  (67 shorter events, 0.6 us)
Async XLA Ops:
  0.0 0.7 copy-start
  146.8 151.2 %collective-permute-start = (bf16[4,48,4096]{2,1,0:T(8,128)(2,1)}, bf16[4,48,4096]{2,1,0:T(8,128)(2,1)S(1)}, u32[]{:S(2)}, u32[]{:S(2)}) collective-permute-start(bf16[4,48,4096]{2,1,0:T(8,128)(2,1)} %get-tuple-element.68), channel_id=1, source_target_pairs={{0,32},{8,40},{16,48},{24,56},{32,64},{40,72},{48,80},{56,88},{64,... | collective-permute-start | bytes 4718600 | tf_op jit(solution)/shard_map/ppermute | solution.py:323
  148.6 378.7 %collective-permute-start.4 = (bf16[4,48,4096]{2,1,0:T(8,128)(2,1)}, bf16[4,48,4096]{2,1,0:T(8,128)(2,1)}, u32[]{:S(2)}, u32[]{:S(2)}) collective-permute-start(bf16[4,48,4096]{2,1,0:T(8,128)(2,1)} %get-tuple-element.74), channel_id=1, source_target_pairs={{0,16},{8,24},{16,0},{24,8},{32,48},{40,56},{48,32},{56,40},{64,80... | collective-permute-start | bytes 4718600 | tf_op jit(solution)/shard_map/ppermute | solution.py:323
  151.6 376.8 %collective-permute-start.2 = (bf16[4,48,4096]{2,1,0:T(8,128)(2,1)}, bf16[4,48,4096]{2,1,0:T(8,128)(2,1)}, u32[]{:S(2)}, u32[]{:S(2)}) collective-permute-start(bf16[4,48,4096]{2,1,0:T(8,128)(2,1)} %get-tuple-element.71), channel_id=1, source_target_pairs={{0,96},{8,104},{16,112},{24,120},{32,0},{40,8},{48,16},{56,24},{64... | collective-permute-start | bytes 4718600 | tf_op jit(solution)/shard_map/ppermute | solution.py:323
  298.1 229.2 %copy-start.10 = (bf16[4,48,4096]{2,1,0:T(8,128)(2,1)}, bf16[4,48,4096]{2,1,0:T(8,128)(2,1)S(1)}, u32[]{:S(2)}) copy-start(bf16[4,48,4096]{2,1,0:T(8,128)(2,1)S(1)} %collective-permute-done.refs_1_) | copy-start | bytes 4718596
  298.1 230.3 %collective-permute-start.1 = (bf16[4,48,4096]{2,1,0:T(8,128)(2,1)}, bf16[4,48,4096]{2,1,0:T(8,128)(2,1)}, u32[]{:S(2)}, u32[]{:S(2)}) collective-permute-start(bf16[4,48,4096]{2,1,0:T(8,128)(2,1)} %get-tuple-element.70), channel_id=1, source_target_pairs={{0,64},{8,72},{16,80},{24,88},{32,96},{40,104},{48,112},{56,120},{... | collective-permute-start | bytes 4718600 | tf_op jit(solution)/shard_map/ppermute | solution.py:323
  300.2 373.1 %collective-permute-start.5 = (bf16[4,48,4096]{2,1,0:T(8,128)(2,1)}, bf16[4,48,4096]{2,1,0:T(8,128)(2,1)}, u32[]{:S(2)}, u32[]{:S(2)}) collective-permute-start(bf16[4,48,4096]{2,1,0:T(8,128)(2,1)} %get-tuple-element.75), channel_id=1, source_target_pairs={{0,24},{8,0},{16,8},{24,16},{32,56},{40,32},{48,40},{56,48},{64,88... | collective-permute-start | bytes 4718600 | tf_op jit(solution)/shard_map/ppermute | solution.py:323
  301.3 372.1 %collective-permute-start.3 = (bf16[4,48,4096]{2,1,0:T(8,128)(2,1)}, bf16[4,48,4096]{2,1,0:T(8,128)(2,1)}, u32[]{:S(2)}, u32[]{:S(2)}) collective-permute-start(bf16[4,48,4096]{2,1,0:T(8,128)(2,1)} %get-tuple-element.73), channel_id=1, source_target_pairs={{0,8},{8,16},{16,24},{24,0},{32,40},{40,48},{48,56},{56,32},{64,72... | collective-permute-start | bytes 4718600 | tf_op jit(solution)/shard_map/ppermute | solution.py:323
  527.3 145.3 %collective-permute-start.6 = (bf16[4,16,4096]{2,1,0:T(8,128)(2,1)}, bf16[4,16,4096]{2,1,0:T(8,128)(2,1)S(1)}, u32[]{:S(2)}, u32[]{:S(2)}) collective-permute-start(bf16[4,16,4096]{2,1,0:T(8,128)(2,1)} %get-tuple-element.78), channel_id=1, source_target_pairs={{0,96},{8,104},{16,112},{24,120},{32,0},{40,8},{48,16},{56,24},{64... | collective-permute-start | bytes 1572872 | tf_op jit(solution)/shard_map/ppermute | solution.py:323
  528.4 149.0 %copy-start.14 = (bf16[4,16,4096]{2,1,0:T(8,128)(2,1)S(1)}, bf16[4,16,4096]{2,1,0:T(8,128)(2,1)}, u32[]{:S(2)}) copy-start(bf16[4,16,4096]{2,1,0:T(8,128)(2,1)} %get-tuple-element.95) | copy-start | bytes 1572868
  528.4 149.9 %copy-start.12 = (s32[64,2]{0,1:T(2,128)S(1)}, s32[64,2]{0,1:T(2,128)}, u32[]{:S(2)}) copy-start(s32[64,2]{0,1:T(2,128)} %param.9) | copy-start | bytes 1540
  672.6 150.1 %copy-start.4 = (bf16[4,16,4096]{2,1,0:T(8,128)(2,1)}, bf16[4,16,4096]{2,1,0:T(8,128)(2,1)S(1)}, u32[]{:S(2)}) copy-start(bf16[4,16,4096]{2,1,0:T(8,128)(2,1)S(1)} %collective-permute-done.6.refs_3_) | copy-start | bytes 1572868
  672.6 199.4 %collective-permute-start.7 = (bf16[4,48,4096]{2,1,0:T(8,128)(2,1)}, bf16[4,48,4096]{2,1,0:T(8,128)(2,1)}, u32[]{:S(2)}, u32[]{:S(2)}) collective-permute-start(bf16[4,48,4096]{2,1,0:T(8,128)(2,1)} %get-tuple-element.79), channel_id=1, source_target_pairs={{0,8},{8,16},{16,24},{24,0},{32,40},{40,48},{48,56},{56,32},{64,72... | collective-permute-start | bytes 4718600 | tf_op jit(solution)/shard_map/ppermute | solution.py:323
  673.3 149.4 %collective-permute-start.10 = (bf16[4,16,4096]{2,1,0:T(8,128)(2,1)}, bf16[4,16,4096]{2,1,0:T(8,128)(2,1)S(1)}, u32[]{:S(2)}, u32[]{:S(2)}) collective-permute-start(bf16[4,16,4096]{2,1,0:T(8,128)(2,1)} %get-tuple-element.86), channel_id=1, source_target_pairs={{0,8},{8,16},{16,24},{24,0},{32,40},{40,48},{48,56},{56,32},{64,72... | collective-permute-start | bytes 1572872 | tf_op jit(solution)/shard_map/ppermute | solution.py:323
  673.4 151.0 %collective-permute-start.8 = (bf16[4,16,4096]{2,1,0:T(8,128)(2,1)}, bf16[4,16,4096]{2,1,0:T(8,128)(2,1)S(1)}, u32[]{:S(2)}, u32[]{:S(2)}) collective-permute-start(bf16[4,16,4096]{2,1,0:T(8,128)(2,1)} %get-tuple-element.82), channel_id=1, source_target_pairs={{0,16},{8,24},{16,0},{24,8},{32,48},{40,56},{48,32},{56,40},{64,80... | collective-permute-start | bytes 1572872 | tf_op jit(solution)/shard_map/ppermute | solution.py:323
  677.4 148.8 %collective-permute-start.14 = (bf16[4,16,4096]{2,1,0:T(8,128)(2,1)S(1)}, bf16[4,16,4096]{2,1,0:T(8,128)(2,1)S(1)}, u32[]{:S(2)}, u32[]{:S(2)}) collective-permute-start(bf16[4,16,4096]{2,1,0:T(8,128)(2,1)S(1)} %copy-done.14), channel_id=1, source_target_pairs={{0,32},{8,40},{16,48},{24,56},{32,64},{40,72},{48,80},{56,88},{64,... | collective-permute-start | bytes 1572872 | tf_op jit(solution)/shard_map/ppermute | solution.py:323
  678.5 149.8 %copy-start.13 = (bf16[4,16,4096]{2,1,0:T(8,128)(2,1)S(1)}, bf16[4,16,4096]{2,1,0:T(8,128)(2,1)}, u32[]{:S(2)}) copy-start(bf16[4,16,4096]{2,1,0:T(8,128)(2,1)} %get-tuple-element.90) | copy-start | bytes 1572868
  822.7 65.6 %copy-start.5 = (bf16[4,16,4096]{2,1,0:T(8,128)(2,1)}, bf16[4,16,4096]{2,1,0:T(8,128)(2,1)S(1)}, u32[]{:S(2)}) copy-start(bf16[4,16,4096]{2,1,0:T(8,128)(2,1)S(1)} %collective-permute-done.10.refs_1_.refs_5_) | copy-start | bytes 1572868
  822.7 65.6 %collective-permute-start.11 = (bf16[4,48,4096]{2,1,0:T(8,128)(2,1)}, bf16[4,48,4096]{2,1,0:T(8,128)(2,1)}, u32[]{:S(2)}, u32[]{:S(2)}) collective-permute-start(bf16[4,48,4096]{2,1,0:T(8,128)(2,1)} %get-tuple-element.87), channel_id=1, source_target_pairs={{0,64},{8,72},{16,80},{24,88},{32,96},{40,104},{48,112},{56,120},{... | collective-permute-start | bytes 4718600 | tf_op jit(solution)/shard_map/ppermute | solution.py:323
  824.4 64.0 %copy-start.6 = (bf16[4,16,4096]{2,1,0:T(8,128)(2,1)}, bf16[4,16,4096]{2,1,0:T(8,128)(2,1)S(1)}, u32[]{:S(2)}) copy-start(bf16[4,16,4096]{2,1,0:T(8,128)(2,1)S(1)} %collective-permute-done.8.refs_2_.refs_6_) | copy-start | bytes 1572868
  824.4 64.0 %collective-permute-start.9 = (bf16[4,48,4096]{2,1,0:T(8,128)(2,1)}, bf16[4,48,4096]{2,1,0:T(8,128)(2,1)}, u32[]{:S(2)}, u32[]{:S(2)}) collective-permute-start(bf16[4,48,4096]{2,1,0:T(8,128)(2,1)} %get-tuple-element.83), channel_id=1, source_target_pairs={{0,24},{8,0},{16,8},{24,16},{32,56},{40,32},{48,40},{56,48},{64,88... | collective-permute-start | bytes 4718600 | tf_op jit(solution)/shard_map/ppermute | solution.py:323
  826.2 62.1 %copy-start.7 = (bf16[4,16,4096]{2,1,0:T(8,128)(2,1)}, bf16[4,16,4096]{2,1,0:T(8,128)(2,1)S(1)}, u32[]{:S(2)}) copy-start(bf16[4,16,4096]{2,1,0:T(8,128)(2,1)S(1)} %collective-permute-done.14.refs_1_) | copy-start | bytes 1572868
  826.2 42.6 %collective-permute-start.15 = (bf16[4,16,4096]{2,1,0:T(8,128)(2,1)}, bf16[4,16,4096]{2,1,0:T(8,128)(2,1)S(1)}, u32[]{:S(2)}, u32[]{:S(2)}) collective-permute-start(bf16[4,16,4096]{2,1,0:T(8,128)(2,1)} %get-tuple-element.96), channel_id=1, source_target_pairs={{0,64},{8,72},{16,80},{24,88},{32,96},{40,104},{48,112},{56,120},{... | collective-permute-start | bytes 1572872 | tf_op jit(solution)/shard_map/ppermute | solution.py:323
  828.3 43.7 %collective-permute-start.12 = (bf16[4,16,4096]{2,1,0:T(8,128)(2,1)S(1)}, bf16[4,16,4096]{2,1,0:T(8,128)(2,1)S(1)}, u32[]{:S(2)}, u32[]{:S(2)}) collective-permute-start(bf16[4,16,4096]{2,1,0:T(8,128)(2,1)S(1)} %copy-done.13), channel_id=1, source_target_pairs={{0,24},{8,0},{16,8},{24,16},{32,56},{40,32},{48,40},{56,48},{64,88... | collective-permute-start | bytes 1572872 | tf_op jit(solution)/shard_map/ppermute | solution.py:323
  868.8 19.5 %copy-start.8 = (bf16[4,16,4096]{2,1,0:T(8,128)(2,1)}, bf16[4,16,4096]{2,1,0:T(8,128)(2,1)S(1)}, u32[]{:S(2)}) copy-start(bf16[4,16,4096]{2,1,0:T(8,128)(2,1)S(1)} %collective-permute-done.15.refs_2_) | copy-start | bytes 1572868
  868.8 34.6 %collective-permute-start.16 = (bf16[4,48,4096]{2,1,0:T(8,128)(2,1)}, bf16[4,48,4096]{2,1,0:T(8,128)(2,1)}, u32[]{:S(2)}, u32[]{:S(2)}) collective-permute-start(bf16[4,48,4096]{2,1,0:T(8,128)(2,1)} %get-tuple-element.97), channel_id=1, source_target_pairs={{0,96},{8,104},{16,112},{24,120},{32,0},{40,8},{48,16},{56,24},{64... | collective-permute-start | bytes 4718600 | tf_op jit(solution)/shard_map/ppermute | solution.py:323
  872.0 16.4 %copy-start.9 = (bf16[4,16,4096]{2,1,0:T(8,128)(2,1)}, bf16[4,16,4096]{2,1,0:T(8,128)(2,1)S(1)}, u32[]{:S(2)}) copy-start(bf16[4,16,4096]{2,1,0:T(8,128)(2,1)S(1)} %collective-permute-done.12.refs_3_.refs_7_) | copy-start | bytes 1572868
  872.0 32.5 %collective-permute-start.13 = (bf16[4,48,4096]{2,1,0:T(8,128)(2,1)}, bf16[4,48,4096]{2,1,0:T(8,128)(2,1)}, u32[]{:S(2)}, u32[]{:S(2)}) collective-permute-start(bf16[4,48,4096]{2,1,0:T(8,128)(2,1)} %get-tuple-element.91), channel_id=1, source_target_pairs={{0,32},{8,40},{16,48},{24,56},{32,64},{40,72},{48,80},{56,88},{64,... | collective-permute-start | bytes 4718600 | tf_op jit(solution)/shard_map/ppermute | solution.py:323
  872.0 33.0 %collective-permute-start.17 = (bf16[4,48,4096]{2,1,0:T(8,128)(2,1)}, bf16[4,48,4096]{2,1,0:T(8,128)(2,1)}, u32[]{:S(2)}, u32[]{:S(2)}) collective-permute-start(bf16[4,48,4096]{2,1,0:T(8,128)(2,1)} %get-tuple-element.99), channel_id=1, source_target_pairs={{0,16},{8,24},{16,0},{24,8},{32,48},{40,56},{48,32},{56,40},{64,80... | collective-permute-start | bytes 4718600 | tf_op jit(solution)/shard_map/ppermute | solution.py:323
  917.5 106.3 %collective-permute-start.18 = (f32[32,96,128]{2,1,0:T(8,128)}, f32[32,96,128]{2,1,0:T(8,128)S(1)}, u32[]{:S(2)}, u32[]{:S(2)}) collective-permute-start(f32[32,96,128]{2,1,0:T(8,128)} %get-tuple-element.101), channel_id=1, source_target_pairs={{0,1},{1,0},{2,3},{3,2},{4,5},{5,4},{6,7},{7,6},{8,9},{9,8},{10,11... | collective-permute-start | bytes 4718600 | tf_op jit(solution)/shard_map/ppermute | solution.py:327
  966.5 58.7 %copy-start.2 = (f32[32,96,128]{2,1,0:T(8,128)S(1)}, f32[32,96,128]{2,1,0:T(8,128)}, u32[]{:S(2)}) copy-start(f32[32,96,128]{2,1,0:T(8,128)} %get-tuple-element.100.keep_ref) | copy-start | bytes 4718596
  966.5 56.4 %collective-permute-start.22 = (bf16[4,16,4096]{2,1,0:T(8,128)(2,1)}, bf16[4,16,4096]{2,1,0:T(8,128)(2,1)S(1)}, u32[]{:S(2)}, u32[]{:S(2)}) collective-permute-start(bf16[4,16,4096]{2,1,0:T(8,128)(2,1)} %get-tuple-element.109), channel_id=1, source_target_pairs={{0,8},{8,16},{16,24},{24,0},{32,40},{40,48},{48,56},{56,32},{64,72... | collective-permute-start | bytes 1572872 | tf_op jit(solution)/shard_map/ppermute | solution.py:323
  967.5 58.5 %collective-permute-start.23 = (bf16[4,16,4096]{2,1,0:T(8,128)(2,1)}, bf16[4,16,4096]{2,1,0:T(8,128)(2,1)}, u32[]{:S(2)}, u32[]{:S(2)}) collective-permute-start(bf16[4,16,4096]{2,1,0:T(8,128)(2,1)} %get-tuple-element.111), channel_id=1, source_target_pairs={{0,24},{8,0},{16,8},{24,16},{32,56},{40,32},{48,40},{56,48},{64,88... | collective-permute-start | bytes 1572872 | tf_op jit(solution)/shard_map/ppermute | solution.py:323
  1018.7 15.5 %collective-permute-start.25 = (bf16[4,16,4096]{2,1,0:T(8,128)(2,1)}, bf16[4,16,4096]{2,1,0:T(8,128)(2,1)}, u32[]{:S(2)}, u32[]{:S(2)}) collective-permute-start(bf16[4,16,4096]{2,1,0:T(8,128)(2,1)} %get-tuple-element.115), channel_id=1, source_target_pairs={{0,32},{8,40},{16,48},{24,56},{32,64},{40,72},{48,80},{56,88},{64,... | collective-permute-start | bytes 1572872 | tf_op jit(solution)/shard_map/ppermute | solution.py:323
  1018.8 27.4 %collective-permute-start.24 = (bf16[4,16,4096]{2,1,0:T(8,128)(2,1)}, bf16[4,16,4096]{2,1,0:T(8,128)(2,1)}, u32[]{:S(2)}, u32[]{:S(2)}) collective-permute-start(bf16[4,16,4096]{2,1,0:T(8,128)(2,1)} %get-tuple-element.113), channel_id=1, source_target_pairs={{0,64},{8,72},{16,80},{24,88},{32,96},{40,104},{48,112},{56,120},{... | collective-permute-start | bytes 1572872 | tf_op jit(solution)/shard_map/ppermute | solution.py:323
  1022.9 0.9 copy-start.11
  1022.9 36.0 %collective-permute-start.27 = (bf16[4,16,4096]{2,1,0:T(8,128)(2,1)}, bf16[4,16,4096]{2,1,0:T(8,128)(2,1)}, u32[]{:S(2)}, u32[]{:S(2)}) collective-permute-start(bf16[4,16,4096]{2,1,0:T(8,128)(2,1)} %get-tuple-element.119), channel_id=1, source_target_pairs={{0,16},{8,24},{16,0},{24,8},{32,48},{40,56},{48,32},{56,40},{64,80... | collective-permute-start | bytes 1572872 | tf_op jit(solution)/shard_map/ppermute | solution.py:323
  1023.8 35.1 %collective-permute-start.26 = (bf16[4,16,4096]{2,1,0:T(8,128)(2,1)}, bf16[4,16,4096]{2,1,0:T(8,128)(2,1)}, u32[]{:S(2)}, u32[]{:S(2)}) collective-permute-start(bf16[4,16,4096]{2,1,0:T(8,128)(2,1)} %get-tuple-element.117), channel_id=1, source_target_pairs={{0,96},{8,104},{16,112},{24,120},{32,0},{40,8},{48,16},{56,24},{64... | collective-permute-start | bytes 1572872 | tf_op jit(solution)/shard_map/ppermute | solution.py:323
  1026.0 33.0 %collective-permute-start.19 = (bf16[8,96,128]{2,1,0:T(8,128)(2,1)}, bf16[8,96,128]{2,1,0:T(8,128)(2,1)S(1)}, u32[]{:S(2)}, u32[]{:S(2)}) collective-permute-start(bf16[8,96,128]{2,1,0:T(8,128)(2,1)} %get-tuple-element.103), channel_id=1, source_target_pairs={{0,2},{1,3},{2,4},{3,5},{4,6},{5,7},{6,0},{7,1},{8,10},{9,11},{10,... | collective-permute-start | bytes 589832 | tf_op jit(solution)/shard_map/ppermute | solution.py:332
  1034.2 24.8 %collective-permute-start.20 = (bf16[8,96,128]{2,1,0:T(8,128)(2,1)S(1)}, bf16[8,96,128]{2,1,0:T(8,128)(2,1)S(1)}, u32[]{:S(2)}, u32[]{:S(2)}) collective-permute-start(bf16[8,96,128]{2,1,0:T(8,128)(2,1)S(1)} %get-tuple-element.104), channel_id=1, source_target_pairs={{0,4},{1,5},{2,6},{3,7},{4,0},{5,1},{6,2},{7,3},{8,12},{9,13},{10,... | collective-permute-start | bytes 589832 | tf_op jit(solution)/shard_map/ppermute | solution.py:332
  1046.2 12.8 %collective-permute-start.21 = (bf16[8,96,128]{2,1,0:T(8,128)(2,1)S(1)}, bf16[8,96,128]{2,1,0:T(8,128)(2,1)S(1)}, u32[]{:S(2)}, u32[]{:S(2)}) collective-permute-start(bf16[8,96,128]{2,1,0:T(8,128)(2,1)S(1)} %get-tuple-element.105), channel_id=1, source_target_pairs={{0,6},{1,7},{2,0},{3,1},{4,2},{5,3},{6,4},{7,5},{8,14},{9,15},{10,... | collective-permute-start | bytes 589832 | tf_op jit(solution)/shard_map/ppermute | solution.py:332
  1059.0 20.3 %copy-start.1 = (s32[16,16]{1,0:T(8,128)S(1)}, s32[16,16]{1,0:T(8,128)}, u32[]{:S(2)}) copy-start(s32[16,16]{1,0:T(8,128)} %param.8) | copy-start | bytes 3076
  1067.6 2.2 collective-permute-start.28
  1069.8 1.0 copy-start.3
  1070.9 6.8 collective-permute-start.29
  1071.0 6.7 collective-permute-start.30
  1072.9 5.5 collective-permute-start.31

commit v3 on v2

--- a/solution.py
+++ b/solution.py
@@ -26,19 +26,38 @@
         copy.wait()
 
 
+def relay(pieces, sems):
+    ins = [pltpu.make_async_copy(src, mid, sems.at[0, k]) for k, (src, mid, _) in enumerate(pieces)]
+    outs = [pltpu.make_async_copy(mid, dst, sems.at[1, k]) for k, (_, mid, dst) in enumerate(pieces)]
+    for copy in ins:
+        copy.start()
+    for arrived, copy in zip(ins, outs):
+        arrived.wait()
+        copy.start()
+    for copy in outs:
+        copy.wait()
+
+
+def relay_scratch(outs):
+    return [pltpu.VMEM(o.shape, o.dtype) for o in outs] + [
+        pltpu.SemaphoreType.DMA((2, SIDE * len(outs)))
+    ]
+
+
 def moved(elements):
     return pl.CostEstimate(flops=0, bytes_accessed=4 * elements, transcendentals=0)
 
 
 def gather_kernel(starts, index_ref, blocks_ref, *refs):
-    outs, sems = refs[:-1], refs[-1]
-    copies = []
-    for n, (out_ref, start) in enumerate(zip(outs, starts)):
-        count, rows = out_ref.shape[:2]
-        for k in range(count):
-            source = blocks_ref.at[index_ref[n * count + k], pl.ds(start, rows)]
-            copies.append(pltpu.make_async_copy(source, out_ref.at[k], sems.at[n * count + k]))
-    run_copies(copies)
+    n = len(starts)
+    outs, mids, sems = refs[:n], refs[n : 2 * n], refs[2 * n]
+    pieces = []
+    for at, start in enumerate(starts):
+        rows = outs[at].shape[1]
+        for k in range(SIDE):
+            source = blocks_ref.at[index_ref[at * SIDE + k], pl.ds(start, rows)]
+            pieces.append((source, mids[at].at[k], outs[at].at[k]))
+    relay(pieces, sems)
 
 
 def gather(blocks, bundles):
@@ -52,7 +71,7 @@
             grid=(1,),
             in_specs=[pl.BlockSpec(memory_space=pl.ANY)],
             out_specs=[pl.BlockSpec(memory_space=pl.ANY)] * len(outs),
-            scratch_shapes=[pltpu.SemaphoreType.DMA((SIDE * len(outs),))],
+            scratch_shapes=relay_scratch(outs),
         ),
         compiler_params=params(),
         cost_estimate=moved(sum(SIDE * rows * width for _, _, rows in bundles)),
@@ -60,13 +79,12 @@
 
 
 def turn_kernel(*refs):
-    pieces, outs, sems = refs[:SIDE], refs[SIDE:-1], refs[-1]
-    copies = [
-        pltpu.make_async_copy(piece.at[k + 1], out.at[i], sems.at[k * SIDE + i])
-        for k, out in enumerate(outs)
-        for i, piece in enumerate(pieces)
+    n = SIDE - 1
+    ins, outs, mids, sems = refs[:SIDE], refs[SIDE : SIDE + n], refs[SIDE + n : SIDE + 2 * n], refs[-1]
+    pieces = [
+        (ins[i].at[k + 1], mids[k].at[i], outs[k].at[i]) for k in range(n) for i in range(SIDE)
     ]
-    run_copies(copies)
+    relay(pieces, sems)
 
 
 def turn(pieces):
@@ -76,7 +94,7 @@
         out_shape=outs,
         in_specs=[pl.BlockSpec(memory_space=pl.ANY)] * SIDE,
         out_specs=[pl.BlockSpec(memory_space=pl.ANY)] * (SIDE - 1),
-        scratch_shapes=[pltpu.SemaphoreType.DMA((SIDE * (SIDE - 1),))],
+        scratch_shapes=relay_scratch(outs),
         compiler_params=params(),
         cost_estimate=moved((SIDE - 1) * pieces[0].size),
     )(*pieces)
@@ -216,7 +234,7 @@
             pltpu.VMEM((total, width), bf16),
             pltpu.SemaphoreType.DMA((len(rights),)),
         ],
-        compiler_params=params(),
+        compiler_params=params(32 * 2**20),
         cost_estimate=cost(total, width, examples),
     )(left, *rights)
 
@@ -271,7 +289,7 @@
                 pltpu.SemaphoreType.DMA(()),
             ],
         ),
-        compiler_params=params(),
+        compiler_params=params(32 * 2**20),
         cost_estimate=cost(total, width, examples),
     )(block, row_a, row_b, left, early, *rights)
 

time: 1080 us -> 317 us (0.29)
  Pallas kernels: 963 us -> 85.1 us
  waiting for transfers between devices: 60.9 us -> 143 us
  starting transfers between devices: 48 us -> 71.1 us
    pallas_call x3, Pallas kernels: 514 us -> 17.7 us  [gather(): pl.pallas_call(functools.partial(gather_kernel, [start for _, start, _ in...]
    pallas_call x4, Pallas kernels: 386 us -> 13.4 us  [turn(): pl.pallas_call(turn_kernel, out_shape=outs, in_specs=[pl.BlockSpec(memory...]
    ppermute x24, waiting for transfers between devices: 54.7 us -> 137 us  [shift(): return lax.ppermute(array, 'ex', pairs)]
    ppermute x24, starting transfers between devices: 34.7 us -> 58 us  [shift(): return lax.ppermute(array, 'ex', pairs)]
    unnamed x30 -> x58, local copies, waits for them, and re-layouts: 1.8 us -> 14.3 us
  transfers between devices with their start and end apart: 32 -> 32, of which waited for: 8 -> 11; matrix products, arithmetic and copies ran while one was open for 0% -> 0% of each run, Pallas kernels for 74% -> 20%
where the time goes in v3:
time: 317 us
  waiting for transfers between devices  143 us (45%)
  Pallas kernels  85.1 us (27%)
  starting transfers between devices  71.1 us (22%)
  local copies, waits for them, and re-layouts  16.1 us (5%)
    ppermute x24, waiting for transfers between devices, shift(): return lax.ppermute(array, 'ex', pairs)  137 us
    ppermute x24, starting transfers between devices, shift(): return lax.ppermute(array, 'ex', pairs)  58 us
    pallas_call x2, Pallas kernels, early_products(): pl.pallas_call(functools.partial(early_kernel, owned, len(rights)), out_s...  20.4 us
    pallas_call x3, Pallas kernels, gather(): pl.pallas_call(functools.partial(gather_kernel, [start for _, start, _ in...  17.7 us
    pallas_call x1, Pallas kernels, left_transposed(): pl.pallas_call(left_kernel, out_shape=jax.ShapeDtypeStruct((examples // t...  16 us
    pallas_call x2, Pallas kernels, tiles(): pl.pallas_call(functools.partial(tiles_kernel, len(rights)), out_shape=(o...  14.8 us
    unnamed x58, local copies, waits for them, and re-layouts  14.3 us
    pallas_call x4, Pallas kernels, turn(): pl.pallas_call(turn_kernel, out_shape=outs, in_specs=[pl.BlockSpec(memory...  13.4 us
  transfers between devices with their start and end apart: 32, of which 11 were waited for; matrix products, arithmetic and copies ran while one was open for 0% of the time, Pallas kernels for 20%

profile of v3, /device:TPU:0, one launch (start us, length us, event | category | flops | bytes accessed | tf_op | source)
XLA Modules:
  0.0 316.6 jit_solution(18279210263043735643)
XLA Ops:
  0.0 0.7 copy-done
  0.7 0.2 dynamic-slice_reduce_fusion
  1.1 0.2 slice_reduce_fusion
  1.4 0.7 pad_add_fusion
  2.0 5.2 %shard_map.57 = (bf16[4,48,4096]{2,1,0:T(8,128)(2,1)}, bf16[4,48,4096]{2,1,0:T(8,128)(2,1)}, bf16[4,48,4096]{2,1,0:T(8,128)(2,1)}) custom-call(s32[12]{0:T(128)} %get-tuple-element.147.index_ref, bf16[8,128,4096]{2,1,0:T(8,128)(2,1)} %bitcast.28), custom_call_target="tpu_custom_call" | custom-call | bytes 9437184 | tf_op jit(solution)/shard_map/pallas_call | solution.py:66
  7.2 1.7 collective-permute-start
  8.9 3.1 collective-permute-start.4
  12.0 1.5 collective-permute-start.2
  13.6 5.3 %shard_map.58 = (bf16[4,48,4096]{2,1,0:T(8,128)(2,1)}, bf16[4,48,4096]{2,1,0:T(8,128)(2,1)}, bf16[4,48,4096]{2,1,0:T(8,128)(2,1)}) custom-call(s32[12]{0:T(128)} %get-tuple-element.148.index_ref, bf16[8,128,4096]{2,1,0:T(8,128)(2,1)} %bitcast.29), custom_call_target="tpu_custom_call" | custom-call | bytes 9437184 | tf_op jit(solution)/shard_map/pallas_call | solution.py:66
  18.9 26.1 %collective-permute-done.refs_1_ = bf16[4,48,4096]{2,1,0:T(8,128)(2,1)S(1)} collective-permute-done((bf16[4,48,4096]{2,1,0:T(8,128)(2,1)}, bf16[4,48,4096]{2,1,0:T(8,128)(2,1)S(1)}, u32[]{:S(2)}, u32[]{:S(2)}) %collective-permute-start) | collective-permute-done | bytes 1572896 | tf_op jit(solution)/shard_map/ppermute | solution.py:341
  45.0 2.1 collective-permute-start.1
  47.1 2.7 collective-permute-start.5
  49.8 0.6 concatenate.22.index_ref
  50.5 7.3 %shard_map.56 = (bf16[4,48,4096]{2,1,0:T(8,128)(2,1)}, bf16[4,48,4096]{2,1,0:T(8,128)(2,1)}, bf16[4,16,4096]{2,1,0:T(8,128)(2,1)}, bf16[4,16,4096]{2,1,0:T(8,128...) custom-call(s32[40]{0:T(128)} %concatenate.22.index_ref, ...), custom_call_target="tpu_custom_call" | custom-call | bytes 14680064 | tf_op jit(solution)/shard_map/pallas_call | solution.py:66
  57.7 0.9 collective-permute-start.6
  58.6 21.0 %collective-permute-done.2.refs_3_ = bf16[4,48,4096]{2,1,0:T(8,128)(2,1)} collective-permute-done((bf16[4,48,4096]{2,1,0:T(8,128)(2,1)}, bf16[4,48,4096]{2,1,0:T(8,128)(2,1)}, u32[]{:S(2)}, u32[]{:S(2)}) %collective-permute-start.2) | collective-permute-done | bytes 1572896 | tf_op jit(solution)/shard_map/ppermute | solution.py:341
  79.7 2.6 collective-permute-done.1.refs_2_
  82.3 4.4 %shard_map.59 = (bf16[4,48,4096]{2,1,0:T(8,128)(2,1)}, bf16[4,48,4096]{2,1,0:T(8,128)(2,1)}, bf16[4,48,4096]{2,1,0:T(8,128)(2,1)}) custom-call(bf16[4,48,4096]{2,1,0:T(8,128)(2,1)} %get-tuple-element.67.refs_0_, bf16[4,48,4096]{2,1,0:T(8,128)(2,1)} %copy-done.18, bf16[4,48,4096]{2,1,0:T(8,128)(2,1)} %collective-permute-done.1.refs_2_, ...), custom_call_target="tpu_custom_call" | custom-call | bytes 9437184 | tf_op jit(solution)/shard_map/pallas_call | solution.py:92
  86.7 6.1 %collective-permute-done.6.refs_3_ = bf16[4,16,4096]{2,1,0:T(8,128)(2,1)S(1)} collective-permute-done((bf16[4,16,4096]{2,1,0:T(8,128)(2,1)}, bf16[4,16,4096]{2,1,0:T(8,128)(2,1)S(1)}, u32[]{:S(2)}, u32[]{:S(2)}) %collective-permute-start.6) | collective-permute-done | bytes 524320 | tf_op jit(solution)/shard_map/ppermute | solution.py:341
  92.8 1.1 collective-permute-start.7
  93.9 1.5 collective-permute-start.10
  95.5 2.0 collective-permute-start.8
  97.5 2.3 collective-permute-start.14
  99.9 4.3 %shard_map.60 = (bf16[4,48,4096]{2,1,0:T(8,128)(2,1)}, bf16[4,48,4096]{2,1,0:T(8,128)(2,1)}, bf16[4,48,4096]{2,1,0:T(8,128)(2,1)}) custom-call(bf16[4,48,4096]{2,1,0:T(8,128)(2,1)} %get-tuple-element.72.refs_0_.refs_4_, bf16[4,48,4096]{2,1,0:T(8,128)(2,1)} %collective-permute-done.3.refs_1_.refs_5_, ...), custom_call_target="tpu_custom_call" | custom-call | bytes 9437184 | tf_op jit(solution)/shard_map/pallas_call | solution.py:92
  104.2 38.5 %collective-permute-done.10.refs_1_.refs_5_ = bf16[4,16,4096]{2,1,0:T(8,128)(2,1)S(1)} collective-permute-done((bf16[4,16,4096]{2,1,0:T(8,128)(2,1)}, bf16[4,16,4096]{2,1,0:T(8,128)(2,1)S(1)}, u32[]{:S(2)}, u32[]{:S(2)}) %collective-permute-start.10) | collective-permute-done | bytes 524320 | tf_op jit(solution)/shard_map/ppermute | solution.py:341
  142.8 12.2 %collective-permute-start.11 = (bf16[4,48,4096]{2,1,0:T(8,128)(2,1)}, bf16[4,48,4096]{2,1,0:T(8,128)(2,1)}, u32[]{:S(2)}, u32[]{:S(2)}) collective-permute-start(bf16[4,48,4096]{2,1,0:T(8,128)(2,1)} %get-tuple-element.87), channel_id=1, source_target_pairs={{0,64},{8,72},{16,80},{24,88},{32,96},{40,104},{48,112},{56,120},{... | collective-permute-start | bytes 4718600 | tf_op jit(solution)/shard_map/ppermute | solution.py:341
  155.3 1.2 collective-permute-start.12
  156.8 31.9 %collective-permute-done.15.refs_2_ = bf16[4,16,4096]{2,1,0:T(8,128)(2,1)S(1)} collective-permute-done((bf16[4,16,4096]{2,1,0:T(8,128)(2,1)}, bf16[4,16,4096]{2,1,0:T(8,128)(2,1)S(1)}, u32[]{:S(2)}, u32[]{:S(2)}) %collective-permute-start.15) | collective-permute-done | bytes 524320 | tf_op jit(solution)/shard_map/ppermute | solution.py:341
  188.7 13.0 %collective-permute-start.16 = (bf16[4,48,4096]{2,1,0:T(8,128)(2,1)}, bf16[4,48,4096]{2,1,0:T(8,128)(2,1)}, u32[]{:S(2)}, u32[]{:S(2)}) collective-permute-start(bf16[4,48,4096]{2,1,0:T(8,128)(2,1)} %get-tuple-element.97), channel_id=1, source_target_pairs={{0,96},{8,104},{16,112},{24,120},{32,0},{40,8},{48,16},{56,24},{64... | collective-permute-start | bytes 4718600 | tf_op jit(solution)/shard_map/ppermute | solution.py:341
  201.7 0.7 collective-permute-start.13
  202.4 0.7 collective-permute-start.17
  203.1 16.0 %shard_map.55.left_ref = bf16[4,4096,256]{2,1,0:T(8,128)(2,1)} custom-call(bf16[1024,4096]{1,0:T(8,128)(2,1)} %bitcast.31, bf16[64,64]{1,0:T(8,128)(2,1)} %bitcast.32, bf16[64,64]{1,0:T(8,128)(2,1)} %bitcast.33), custom_call_target="tpu_custom_call" | custom-call | flops 10737418240 | bytes 16777216 | tf_op jit(solution)/shard_map/pallas_call | solution.py:165
  219.1 1.4 copy-done.19
  220.5 1.4 copy-done.20
  221.9 1.4 copy-done.21
  223.3 14.2 %shard_map.61.early_ref = f32[8,960,128]{2,1,0:T(8,128)S(1)} custom-call(bf16[4,4096,256]{2,1,0:T(8,128)(2,1)} %shard_map.55.left_ref, bf16[4,48,4096]{2,1,0:T(8,128)(2,1)S(1)} %copy-done.20, bf16[4,48,4096]{2,1,0:T(8,128)(2,1)S(1)} %copy-done.19, bf16[4,48,4096]{2,1,0:T(8,128)(2,1)} %collective-permute-done.1.refs_2_, ...), custom_call_target="tpu_custom_call" | custom-call | flops 8053063680 | bytes 20185088 | tf_op jit(solution)/shard_map/pallas_call | solution.py:226
  237.5 1.9 copy-done.24
  239.5 2.1 copy-done.25
  241.6 10.2 %shard_map.62 = (f32[32,96,128]{2,1,0:T(8,128)S(1)}, f32[32,96,128]{2,1,0:T(8,128)}) custom-call(s32[64]{0:T(128)S(1)} %squeeze.29.block_ref, s32[64]{0:T(128)S(1)} %mul.49.row_a_ref, s32[64]{0:T(128)S(1)} %mul.51.row_b_ref, bf16[4,4096,256]{2,1,0:T(8,128)(2,1)S(1)} %copy-done.2, f32[8,960,128]{2,1,0:T(8,128)S(1)} %copy-done.25, ...), custom_call_target="tpu_custom_call" | custom-call | flops 4831838208 | bytes 15466496 | tf_op jit(solution)/shard_map/pallas_call | solution.py:276
  251.9 2.3 shard_map.64
  254.3 1.6 collective-permute-start.22
  255.9 1.7 collective-permute-start.23
  257.6 2.4 shard_map.65
  260.0 1.4 collective-permute-start.25
  261.4 2.1 collective-permute-start.24
  263.5 6.6 %collective-permute-done.22 = bf16[4,16,4096]{2,1,0:T(8,128)(2,1)S(1)} collective-permute-done((bf16[4,16,4096]{2,1,0:T(8,128)(2,1)}, bf16[4,16,4096]{2,1,0:T(8,128)(2,1)S(1)}, u32[]{:S(2)}, u32[]{:S(2)}) %collective-permute-start.22) | collective-permute-done | bytes 524320 | tf_op jit(solution)/shard_map/ppermute | solution.py:341
  270.1 0.8 copy-done.22
  270.9 1.6 collective-permute-start.27
  272.5 2.6 collective-permute-start.26
  275.4 1.7 shard_map.63
  277.1 2.0 collective-permute-start.19
  279.1 3.6 %collective-permute-start.20 = (bf16[8,96,128]{2,1,0:T(8,128)(2,1)S(1)}, bf16[8,96,128]{2,1,0:T(8,128)(2,1)S(1)}, u32[]{:S(2)}, u32[]{:S(2)}) collective-permute-start(bf16[8,96,128]{2,1,0:T(8,128)(2,1)S(1)} %get-tuple-element.104), channel_id=1, source_target_pairs={{0,4},{1,5},{2,6},{3,7},{4,0},{5,1},{6,2},{7,3},{8,12},{9,13},{10,... | collective-permute-start | bytes 589832 | tf_op jit(solution)/shard_map/ppermute | solution.py:350
  282.6 4.1 %collective-permute-done.24 = bf16[4,16,4096]{2,1,0:T(8,128)(2,1)} collective-permute-done((bf16[4,16,4096]{2,1,0:T(8,128)(2,1)}, bf16[4,16,4096]{2,1,0:T(8,128)(2,1)}, u32[]{:S(2)}, u32[]{:S(2)}) %collective-permute-start.24) | collective-permute-done | bytes 524320 | tf_op jit(solution)/shard_map/ppermute | solution.py:341
  286.8 4.0 %collective-permute-start.21 = (bf16[8,96,128]{2,1,0:T(8,128)(2,1)S(1)}, bf16[8,96,128]{2,1,0:T(8,128)(2,1)S(1)}, u32[]{:S(2)}, u32[]{:S(2)}) collective-permute-start(bf16[8,96,128]{2,1,0:T(8,128)(2,1)S(1)} %get-tuple-element.105), channel_id=1, source_target_pairs={{0,6},{1,7},{2,0},{3,1},{4,2},{5,3},{6,4},{7,5},{8,14},{9,15},{10,... | collective-permute-start | bytes 589832 | tf_op jit(solution)/shard_map/ppermute | solution.py:350
  290.9 3.4 %copy-done.3 = bf16[4,4096,256]{2,1,0:T(8,128)(2,1)S(1)} copy-done((bf16[4,4096,256]{2,1,0:T(8,128)(2,1)S(1)}, bf16[4,4096,256]{2,1,0:T(8,128)(2,1)}, u32[]{:S(2)}) %copy-start.3) | copy-done | bytes 8388632
  294.3 1.0 copy-done.23
  295.3 6.2 %shard_map.66.early_ref = f32[8,320,128]{2,1,0:T(8,128)S(1)} custom-call(bf16[4,4096,256]{2,1,0:T(8,128)(2,1)S(1)} %copy-done.3, bf16[4,16,4096]{2,1,0:T(8,128)(2,1)S(1)} %copy-done.4, bf16[4,16,4096]{2,1,0:T(8,128)(2,1)S(1)} %copy-done.13, bf16[4,16,4096]{2,1,0:T(8,128)(2,1)S(1)} %copy-done.15, bf16[4,16,4096]{2,1,0:T(8,128)(2,1)S(1)} %copy-done.7, ...), custom_call_target="tpu_custom_call" | custom-call | flops 2684354560 | bytes 12320768 | tf_op jit(solution)/shard_map/pallas_call | solution.py:226
  301.6 4.6 %shard_map.67 = (f32[32,32,128]{2,1,0:T(8,128)S(1)}, f32[32,32,128]{2,1,0:T(8,128)S(1)}) custom-call(s32[64]{0:T(128)S(1)} %squeeze.29.block_ref, s32[64]{0:T(128)S(1)} %mul.53.row_a_ref, s32[64]{0:T(128)S(1)} %mul.55.row_b_ref, bf16[4,4096,256]{2,1,0:T(8,128)(2,1)S(1)} %copy-done.3, f32[8,320,128]{2,1,0:T(8,128)S(1)} %shard_map.66.early_ref, ...), custom_call_target="tpu_custom_call" | custom-call | flops 1610612736 | bytes 10747904 | tf_op jit(solution)/shard_map/pallas_call | solution.py:276
  306.3 1.9 collective-permute-done.28.got_ref
  308.3 1.9 collective-permute-start.30
  310.2 1.4 collective-permute-start.31
  311.5 3.5 %collective-permute-done.29.refs_5_ = bf16[8,32,128]{2,1,0:T(8,128)(2,1)S(1)} collective-permute-done((bf16[8,32,128]{2,1,0:T(8,128)(2,1)S(1)}, bf16[8,32,128]{2,1,0:T(8,128)(2,1)S(1)}, u32[]{:S(2)}, u32[]{:S(2)}) %collective-permute-start.29) | collective-permute-done | bytes 65568 | tf_op jit(solution)/shard_map/ppermute | solution.py:350
  315.0 0.6 collective-permute-done.31.refs_7_
  315.6 1.0 shard_map.69
  (95 shorter events, 1.6 us)
Async XLA Ops:
  0.0 0.7 copy-start
  7.2 37.8 %collective-permute-start = (bf16[4,48,4096]{2,1,0:T(8,128)(2,1)}, bf16[4,48,4096]{2,1,0:T(8,128)(2,1)S(1)}, u32[]{:S(2)}, u32[]{:S(2)}) collective-permute-start(bf16[4,48,4096]{2,1,0:T(8,128)(2,1)} %get-tuple-element.68), channel_id=1, source_target_pairs={{0,32},{8,40},{16,48},{24,56},{32,64},{40,72},{48,80},{56,88},{64,... | collective-permute-start | bytes 4718600 | tf_op jit(solution)/shard_map/ppermute | solution.py:341
  8.9 48.8 %collective-permute-start.4 = (bf16[4,48,4096]{2,1,0:T(8,128)(2,1)}, bf16[4,48,4096]{2,1,0:T(8,128)(2,1)}, u32[]{:S(2)}, u32[]{:S(2)}) collective-permute-start(bf16[4,48,4096]{2,1,0:T(8,128)(2,1)} %get-tuple-element.74), channel_id=1, source_target_pairs={{0,16},{8,24},{16,0},{24,8},{32,48},{40,56},{48,32},{56,40},{64,80... | collective-permute-start | bytes 4718600 | tf_op jit(solution)/shard_map/ppermute | solution.py:341
  12.0 67.6 %collective-permute-start.2 = (bf16[4,48,4096]{2,1,0:T(8,128)(2,1)}, bf16[4,48,4096]{2,1,0:T(8,128)(2,1)}, u32[]{:S(2)}, u32[]{:S(2)}) collective-permute-start(bf16[4,48,4096]{2,1,0:T(8,128)(2,1)} %get-tuple-element.71), channel_id=1, source_target_pairs={{0,96},{8,104},{16,112},{24,120},{32,0},{40,8},{48,16},{56,24},{64... | collective-permute-start | bytes 4718600 | tf_op jit(solution)/shard_map/ppermute | solution.py:341
  45.0 12.8 %copy-start.18 = (bf16[4,48,4096]{2,1,0:T(8,128)(2,1)}, bf16[4,48,4096]{2,1,0:T(8,128)(2,1)S(1)}, u32[]{:S(2)}) copy-start(bf16[4,48,4096]{2,1,0:T(8,128)(2,1)S(1)} %collective-permute-done.refs_1_) | copy-start | bytes 4718596
  45.0 37.3 %collective-permute-start.1 = (bf16[4,48,4096]{2,1,0:T(8,128)(2,1)}, bf16[4,48,4096]{2,1,0:T(8,128)(2,1)}, u32[]{:S(2)}, u32[]{:S(2)}) collective-permute-start(bf16[4,48,4096]{2,1,0:T(8,128)(2,1)} %get-tuple-element.70), channel_id=1, source_target_pairs={{0,64},{8,72},{16,80},{24,88},{32,96},{40,104},{48,112},{56,120},{... | collective-permute-start | bytes 4718600 | tf_op jit(solution)/shard_map/ppermute | solution.py:341
  47.1 46.8 %collective-permute-start.5 = (bf16[4,48,4096]{2,1,0:T(8,128)(2,1)}, bf16[4,48,4096]{2,1,0:T(8,128)(2,1)}, u32[]{:S(2)}, u32[]{:S(2)}) collective-permute-start(bf16[4,48,4096]{2,1,0:T(8,128)(2,1)} %get-tuple-element.75), channel_id=1, source_target_pairs={{0,24},{8,0},{16,8},{24,16},{32,56},{40,32},{48,40},{56,48},{64,88... | collective-permute-start | bytes 4718600 | tf_op jit(solution)/shard_map/ppermute | solution.py:341
  49.8 45.7 %collective-permute-start.3 = (bf16[4,48,4096]{2,1,0:T(8,128)(2,1)}, bf16[4,48,4096]{2,1,0:T(8,128)(2,1)}, u32[]{:S(2)}, u32[]{:S(2)}) collective-permute-start(bf16[4,48,4096]{2,1,0:T(8,128)(2,1)} %get-tuple-element.73), channel_id=1, source_target_pairs={{0,8},{8,16},{16,24},{24,0},{32,40},{40,48},{48,56},{56,32},{64,72... | collective-permute-start | bytes 4718600 | tf_op jit(solution)/shard_map/ppermute | solution.py:341
  57.7 35.1 %collective-permute-start.6 = (bf16[4,16,4096]{2,1,0:T(8,128)(2,1)}, bf16[4,16,4096]{2,1,0:T(8,128)(2,1)S(1)}, u32[]{:S(2)}, u32[]{:S(2)}) collective-permute-start(bf16[4,16,4096]{2,1,0:T(8,128)(2,1)} %get-tuple-element.78), channel_id=1, source_target_pairs={{0,96},{8,104},{16,112},{24,120},{32,0},{40,8},{48,16},{56,24},{64... | collective-permute-start | bytes 1572872 | tf_op jit(solution)/shard_map/ppermute | solution.py:341
  82.3 13.2 %copy-start.28 = (bf16[4,16,4096]{2,1,0:T(8,128)(2,1)S(1)}, bf16[4,16,4096]{2,1,0:T(8,128)(2,1)}, u32[]{:S(2)}) copy-start(bf16[4,16,4096]{2,1,0:T(8,128)(2,1)} %get-tuple-element.82) | copy-start | bytes 1572868
  82.3 15.2 %copy-start.27 = (bf16[4,16,4096]{2,1,0:T(8,128)(2,1)S(1)}, bf16[4,16,4096]{2,1,0:T(8,128)(2,1)}, u32[]{:S(2)}) copy-start(bf16[4,16,4096]{2,1,0:T(8,128)(2,1)} %get-tuple-element.95) | copy-start | bytes 1572868
  82.3 17.5 %copy-start.26 = (s32[64,2]{0,1:T(2,128)S(1)}, s32[64,2]{0,1:T(2,128)}, u32[]{:S(2)}) copy-start(s32[64,2]{0,1:T(2,128)} %param.9) | copy-start | bytes 1540
  92.8 11.4 %copy-start.6 = (bf16[4,16,4096]{2,1,0:T(8,128)(2,1)}, bf16[4,16,4096]{2,1,0:T(8,128)(2,1)S(1)}, u32[]{:S(2)}) copy-start(bf16[4,16,4096]{2,1,0:T(8,128)(2,1)S(1)} %collective-permute-done.6.refs_3_) | copy-start | bytes 1572868
  92.8 109.6 %collective-permute-start.7 = (bf16[4,48,4096]{2,1,0:T(8,128)(2,1)}, bf16[4,48,4096]{2,1,0:T(8,128)(2,1)}, u32[]{:S(2)}, u32[]{:S(2)}) collective-permute-start(bf16[4,48,4096]{2,1,0:T(8,128)(2,1)} %get-tuple-element.79), channel_id=1, source_target_pairs={{0,8},{8,16},{16,24},{24,0},{32,40},{40,48},{48,56},{56,32},{64,72... | collective-permute-start | bytes 4718600 | tf_op jit(solution)/shard_map/ppermute | solution.py:341
  93.9 48.8 %collective-permute-start.10 = (bf16[4,16,4096]{2,1,0:T(8,128)(2,1)}, bf16[4,16,4096]{2,1,0:T(8,128)(2,1)S(1)}, u32[]{:S(2)}, u32[]{:S(2)}) collective-permute-start(bf16[4,16,4096]{2,1,0:T(8,128)(2,1)} %get-tuple-element.86), channel_id=1, source_target_pairs={{0,8},{8,16},{16,24},{24,0},{32,40},{40,48},{48,56},{56,32},{64,72... | collective-permute-start | bytes 1572872 | tf_op jit(solution)/shard_map/ppermute | solution.py:341
  95.5 59.5 %collective-permute-start.8 = (bf16[4,16,4096]{2,1,0:T(8,128)(2,1)S(1)}, bf16[4,16,4096]{2,1,0:T(8,128)(2,1)S(1)}, u32[]{:S(2)}, u32[]{:S(2)}) collective-permute-start(bf16[4,16,4096]{2,1,0:T(8,128)(2,1)S(1)} %copy-done.28), channel_id=1, source_target_pairs={{0,16},{8,24},{16,0},{24,8},{32,48},{40,56},{48,32},{56,40},{64,80... | collective-permute-start | bytes 1572872 | tf_op jit(solution)/shard_map/ppermute | solution.py:341
  97.5 57.6 %collective-permute-start.14 = (bf16[4,16,4096]{2,1,0:T(8,128)(2,1)S(1)}, bf16[4,16,4096]{2,1,0:T(8,128)(2,1)S(1)}, u32[]{:S(2)}, u32[]{:S(2)}) collective-permute-start(bf16[4,16,4096]{2,1,0:T(8,128)(2,1)S(1)} %copy-done.27), channel_id=1, source_target_pairs={{0,32},{8,40},{16,48},{24,56},{32,64},{40,72},{48,80},{56,88},{64,... | collective-permute-start | bytes 1572872 | tf_op jit(solution)/shard_map/ppermute | solution.py:341
  142.8 76.3 %copy-start.8 = (bf16[4,16,4096]{2,1,0:T(8,128)(2,1)}, bf16[4,16,4096]{2,1,0:T(8,128)(2,1)S(1)}, u32[]{:S(2)}) copy-start(bf16[4,16,4096]{2,1,0:T(8,128)(2,1)S(1)} %collective-permute-done.10.refs_1_.refs_5_) | copy-start | bytes 1572868
  142.8 76.3 %collective-permute-start.11 = (bf16[4,48,4096]{2,1,0:T(8,128)(2,1)}, bf16[4,48,4096]{2,1,0:T(8,128)(2,1)}, u32[]{:S(2)}, u32[]{:S(2)}) collective-permute-start(bf16[4,48,4096]{2,1,0:T(8,128)(2,1)} %get-tuple-element.87), channel_id=1, source_target_pairs={{0,64},{8,72},{16,80},{24,88},{32,96},{40,104},{48,112},{56,120},{... | collective-permute-start | bytes 4718600 | tf_op jit(solution)/shard_map/ppermute | solution.py:341
  155.0 64.1 %copy-start.10 = (bf16[4,16,4096]{2,1,0:T(8,128)(2,1)}, bf16[4,16,4096]{2,1,0:T(8,128)(2,1)S(1)}, u32[]{:S(2)}) copy-start(bf16[4,16,4096]{2,1,0:T(8,128)(2,1)S(1)} %collective-permute-done.8.refs_2_.refs_6_) | copy-start | bytes 1572868
  155.0 64.1 %collective-permute-start.9 = (bf16[4,48,4096]{2,1,0:T(8,128)(2,1)}, bf16[4,48,4096]{2,1,0:T(8,128)(2,1)}, u32[]{:S(2)}, u32[]{:S(2)}) collective-permute-start(bf16[4,48,4096]{2,1,0:T(8,128)(2,1)} %get-tuple-element.83), channel_id=1, source_target_pairs={{0,24},{8,0},{16,8},{24,16},{32,56},{40,32},{48,40},{56,48},{64,88... | collective-permute-start | bytes 4718600 | tf_op jit(solution)/shard_map/ppermute | solution.py:341
  155.1 63.9 %copy-start.12 = (bf16[4,16,4096]{2,1,0:T(8,128)(2,1)}, bf16[4,16,4096]{2,1,0:T(8,128)(2,1)S(1)}, u32[]{:S(2)}) copy-start(bf16[4,16,4096]{2,1,0:T(8,128)(2,1)S(1)} %collective-permute-done.14.refs_1_) | copy-start | bytes 1572868
  155.1 33.6 %collective-permute-start.15 = (bf16[4,16,4096]{2,1,0:T(8,128)(2,1)}, bf16[4,16,4096]{2,1,0:T(8,128)(2,1)S(1)}, u32[]{:S(2)}, u32[]{:S(2)}) collective-permute-start(bf16[4,16,4096]{2,1,0:T(8,128)(2,1)} %get-tuple-element.96), channel_id=1, source_target_pairs={{0,64},{8,72},{16,80},{24,88},{32,96},{40,104},{48,112},{56,120},{... | collective-permute-start | bytes 1572872 | tf_op jit(solution)/shard_map/ppermute | solution.py:341
  155.3 46.4 %collective-permute-start.12 = (bf16[4,16,4096]{2,1,0:T(8,128)(2,1)}, bf16[4,16,4096]{2,1,0:T(8,128)(2,1)S(1)}, u32[]{:S(2)}, u32[]{:S(2)}) collective-permute-start(bf16[4,16,4096]{2,1,0:T(8,128)(2,1)} %get-tuple-element.90), channel_id=1, source_target_pairs={{0,24},{8,0},{16,8},{24,16},{32,56},{40,32},{48,40},{56,48},{64,88... | collective-permute-start | bytes 1572872 | tf_op jit(solution)/shard_map/ppermute | solution.py:341
  188.7 30.3 %copy-start.14 = (bf16[4,16,4096]{2,1,0:T(8,128)(2,1)}, bf16[4,16,4096]{2,1,0:T(8,128)(2,1)S(1)}, u32[]{:S(2)}) copy-start(bf16[4,16,4096]{2,1,0:T(8,128)(2,1)S(1)} %collective-permute-done.15.refs_2_) | copy-start | bytes 1572868
  188.7 50.7 %collective-permute-start.16 = (bf16[4,48,4096]{2,1,0:T(8,128)(2,1)}, bf16[4,48,4096]{2,1,0:T(8,128)(2,1)}, u32[]{:S(2)}, u32[]{:S(2)}) collective-permute-start(bf16[4,48,4096]{2,1,0:T(8,128)(2,1)} %get-tuple-element.97), channel_id=1, source_target_pairs={{0,96},{8,104},{16,112},{24,120},{32,0},{40,8},{48,16},{56,24},{64... | collective-permute-start | bytes 4718600 | tf_op jit(solution)/shard_map/ppermute | solution.py:341
  201.7 17.3 %copy-start.16 = (bf16[4,16,4096]{2,1,0:T(8,128)(2,1)}, bf16[4,16,4096]{2,1,0:T(8,128)(2,1)S(1)}, u32[]{:S(2)}) copy-start(bf16[4,16,4096]{2,1,0:T(8,128)(2,1)S(1)} %collective-permute-done.12.refs_3_.refs_7_) | copy-start | bytes 1572868
  201.7 37.7 %collective-permute-start.13 = (bf16[4,48,4096]{2,1,0:T(8,128)(2,1)}, bf16[4,48,4096]{2,1,0:T(8,128)(2,1)}, u32[]{:S(2)}, u32[]{:S(2)}) collective-permute-start(bf16[4,48,4096]{2,1,0:T(8,128)(2,1)} %get-tuple-element.91), channel_id=1, source_target_pairs={{0,32},{8,40},{16,48},{24,56},{32,64},{40,72},{48,80},{56,88},{64,... | collective-permute-start | bytes 4718600 | tf_op jit(solution)/shard_map/ppermute | solution.py:341
  202.4 37.1 %collective-permute-start.17 = (bf16[4,48,4096]{2,1,0:T(8,128)(2,1)}, bf16[4,48,4096]{2,1,0:T(8,128)(2,1)}, u32[]{:S(2)}, u32[]{:S(2)}) collective-permute-start(bf16[4,48,4096]{2,1,0:T(8,128)(2,1)} %get-tuple-element.99), channel_id=1, source_target_pairs={{0,16},{8,24},{16,0},{24,8},{32,48},{40,56},{48,32},{56,40},{64,80... | collective-permute-start | bytes 4718600 | tf_op jit(solution)/shard_map/ppermute | solution.py:341
  219.1 1.4 copy-start.19
  220.5 1.4 copy-start.20
  221.9 1.4 copy-start.21
  223.3 16.2 %copy-start.2 = (bf16[4,4096,256]{2,1,0:T(8,128)(2,1)S(1)}, bf16[4,4096,256]{2,1,0:T(8,128)(2,1)}, u32[]{:S(2)}) copy-start(bf16[4,4096,256]{2,1,0:T(8,128)(2,1)} %shard_map.55.left_ref) | copy-start | bytes 25165828
  237.5 1.9 copy-start.24
  239.5 2.1 copy-start.25
  251.8 20.7 %collective-permute-start.18 = (f32[32,96,128]{2,1,0:T(8,128)}, f32[32,96,128]{2,1,0:T(8,128)}, u32[]{:S(2)}, u32[]{:S(2)}) collective-permute-start(f32[32,96,128]{2,1,0:T(8,128)} %get-tuple-element.101), channel_id=1, source_target_pairs={{0,1},{1,0},{2,3},{3,2},{4,5},{5,4},{6,7},{7,6},{8,9},{9,8},{10,11... | collective-permute-start | bytes 4718600 | tf_op jit(solution)/shard_map/ppermute | solution.py:345
  254.3 15.8 %collective-permute-start.22 = (bf16[4,16,4096]{2,1,0:T(8,128)(2,1)}, bf16[4,16,4096]{2,1,0:T(8,128)(2,1)S(1)}, u32[]{:S(2)}, u32[]{:S(2)}) collective-permute-start(bf16[4,16,4096]{2,1,0:T(8,128)(2,1)} %get-tuple-element.109), channel_id=1, source_target_pairs={{0,8},{8,16},{16,24},{24,0},{32,40},{40,48},{48,56},{56,32},{64,72... | collective-permute-start | bytes 1572872 | tf_op jit(solution)/shard_map/ppermute | solution.py:341
  255.9 21.1 %collective-permute-start.23 = (bf16[4,16,4096]{2,1,0:T(8,128)(2,1)}, bf16[4,16,4096]{2,1,0:T(8,128)(2,1)}, u32[]{:S(2)}, u32[]{:S(2)}) collective-permute-start(bf16[4,16,4096]{2,1,0:T(8,128)(2,1)} %get-tuple-element.111), channel_id=1, source_target_pairs={{0,24},{8,0},{16,8},{24,16},{32,56},{40,32},{48,40},{56,48},{64,88... | collective-permute-start | bytes 1572872 | tf_op jit(solution)/shard_map/ppermute | solution.py:341
  257.6 33.2 %copy-start.15 = (bf16[4,16,4096]{2,1,0:T(8,128)(2,1)S(1)}, bf16[4,16,4096]{2,1,0:T(8,128)(2,1)}, u32[]{:S(2)}) copy-start(bf16[4,16,4096]{2,1,0:T(8,128)(2,1)} %copy-done.14) | copy-start | bytes 1572868
  257.6 33.2 %copy-start.17 = (bf16[4,16,4096]{2,1,0:T(8,128)(2,1)S(1)}, bf16[4,16,4096]{2,1,0:T(8,128)(2,1)}, u32[]{:S(2)}) copy-start(bf16[4,16,4096]{2,1,0:T(8,128)(2,1)} %copy-done.16) | copy-start | bytes 1572868
  260.0 19.0 %collective-permute-start.25 = (bf16[4,16,4096]{2,1,0:T(8,128)(2,1)}, bf16[4,16,4096]{2,1,0:T(8,128)(2,1)S(1)}, u32[]{:S(2)}, u32[]{:S(2)}) collective-permute-start(bf16[4,16,4096]{2,1,0:T(8,128)(2,1)} %get-tuple-element.115), channel_id=1, source_target_pairs={{0,32},{8,40},{16,48},{24,56},{32,64},{40,72},{48,80},{56,88},{64,... | collective-permute-start | bytes 1572872 | tf_op jit(solution)/shard_map/ppermute | solution.py:341
  261.4 25.4 %collective-permute-start.24 = (bf16[4,16,4096]{2,1,0:T(8,128)(2,1)}, bf16[4,16,4096]{2,1,0:T(8,128)(2,1)}, u32[]{:S(2)}, u32[]{:S(2)}) collective-permute-start(bf16[4,16,4096]{2,1,0:T(8,128)(2,1)} %get-tuple-element.113), channel_id=1, source_target_pairs={{0,64},{8,72},{16,80},{24,88},{32,96},{40,104},{48,112},{56,120},{... | collective-permute-start | bytes 1572872 | tf_op jit(solution)/shard_map/ppermute | solution.py:341
  270.1 0.8 copy-start.22
  270.9 30.6 %collective-permute-start.27 = (bf16[4,16,4096]{2,1,0:T(8,128)(2,1)}, bf16[4,16,4096]{2,1,0:T(8,128)(2,1)}, u32[]{:S(2)}, u32[]{:S(2)}) collective-permute-start(bf16[4,16,4096]{2,1,0:T(8,128)(2,1)} %get-tuple-element.119), channel_id=1, source_target_pairs={{0,16},{8,24},{16,0},{24,8},{32,48},{40,56},{48,32},{56,40},{64,80... | collective-permute-start | bytes 1572872 | tf_op jit(solution)/shard_map/ppermute | solution.py:341
  272.5 29.0 %collective-permute-start.26 = (bf16[4,16,4096]{2,1,0:T(8,128)(2,1)}, bf16[4,16,4096]{2,1,0:T(8,128)(2,1)}, u32[]{:S(2)}, u32[]{:S(2)}) collective-permute-start(bf16[4,16,4096]{2,1,0:T(8,128)(2,1)} %get-tuple-element.117), channel_id=1, source_target_pairs={{0,96},{8,104},{16,112},{24,120},{32,0},{40,8},{48,16},{56,24},{64... | collective-permute-start | bytes 1572872 | tf_op jit(solution)/shard_map/ppermute | solution.py:341
  275.3 15.5 %copy-start.4 = (bf16[4,16,4096]{2,1,0:T(8,128)(2,1)S(1)}, bf16[4,16,4096]{2,1,0:T(8,128)(2,1)}, u32[]{:S(2)}) copy-start(bf16[4,16,4096]{2,1,0:T(8,128)(2,1)} %get-tuple-element.106.refs_0_) | copy-start | bytes 1572868
  275.3 15.5 %copy-start.5 = (bf16[4,16,4096]{2,1,0:T(8,128)(2,1)S(1)}, bf16[4,16,4096]{2,1,0:T(8,128)(2,1)}, u32[]{:S(2)}) copy-start(bf16[4,16,4096]{2,1,0:T(8,128)(2,1)} %get-tuple-element.107.refs_0_.refs_4_) | copy-start | bytes 1572868
  275.3 15.5 %copy-start.7 = (bf16[4,16,4096]{2,1,0:T(8,128)(2,1)S(1)}, bf16[4,16,4096]{2,1,0:T(8,128)(2,1)}, u32[]{:S(2)}) copy-start(bf16[4,16,4096]{2,1,0:T(8,128)(2,1)} %copy-done.6) | copy-start | bytes 1572868
  275.3 15.5 %copy-start.9 = (bf16[4,16,4096]{2,1,0:T(8,128)(2,1)S(1)}, bf16[4,16,4096]{2,1,0:T(8,128)(2,1)}, u32[]{:S(2)}) copy-start(bf16[4,16,4096]{2,1,0:T(8,128)(2,1)} %copy-done.8) | copy-start | bytes 1572868
  275.3 15.5 %copy-start.11 = (bf16[4,16,4096]{2,1,0:T(8,128)(2,1)S(1)}, bf16[4,16,4096]{2,1,0:T(8,128)(2,1)}, u32[]{:S(2)}) copy-start(bf16[4,16,4096]{2,1,0:T(8,128)(2,1)} %copy-done.10) | copy-start | bytes 1572868
  275.3 15.5 %copy-start.13 = (bf16[4,16,4096]{2,1,0:T(8,128)(2,1)S(1)}, bf16[4,16,4096]{2,1,0:T(8,128)(2,1)}, u32[]{:S(2)}) copy-start(bf16[4,16,4096]{2,1,0:T(8,128)(2,1)} %copy-done.12) | copy-start | bytes 1572868
  277.1 24.5 %collective-permute-start.19 = (bf16[8,96,128]{2,1,0:T(8,128)(2,1)S(1)}, bf16[8,96,128]{2,1,0:T(8,128)(2,1)S(1)}, u32[]{:S(2)}, u32[]{:S(2)}) collective-permute-start(bf16[8,96,128]{2,1,0:T(8,128)(2,1)S(1)} %get-tuple-element.103), channel_id=1, source_target_pairs={{0,2},{1,3},{2,4},{3,5},{4,6},{5,7},{6,0},{7,1},{8,10},{9,11},{10,... | collective-permute-start | bytes 589832 | tf_op jit(solution)/shard_map/ppermute | solution.py:350
  279.1 22.5 %collective-permute-start.20 = (bf16[8,96,128]{2,1,0:T(8,128)(2,1)S(1)}, bf16[8,96,128]{2,1,0:T(8,128)(2,1)S(1)}, u32[]{:S(2)}, u32[]{:S(2)}) collective-permute-start(bf16[8,96,128]{2,1,0:T(8,128)(2,1)S(1)} %get-tuple-element.104), channel_id=1, source_target_pairs={{0,4},{1,5},{2,6},{3,7},{4,0},{5,1},{6,2},{7,3},{8,12},{9,13},{10,... | collective-permute-start | bytes 589832 | tf_op jit(solution)/shard_map/ppermute | solution.py:350
  286.8 14.8 %collective-permute-start.21 = (bf16[8,96,128]{2,1,0:T(8,128)(2,1)S(1)}, bf16[8,96,128]{2,1,0:T(8,128)(2,1)S(1)}, u32[]{:S(2)}, u32[]{:S(2)}) collective-permute-start(bf16[8,96,128]{2,1,0:T(8,128)(2,1)S(1)} %get-tuple-element.105), channel_id=1, source_target_pairs={{0,6},{1,7},{2,0},{3,1},{4,2},{5,3},{6,4},{7,5},{8,14},{9,15},{10,... | collective-permute-start | bytes 589832 | tf_op jit(solution)/shard_map/ppermute | solution.py:350
  290.9 3.4 %copy-start.3 = (bf16[4,4096,256]{2,1,0:T(8,128)(2,1)S(1)}, bf16[4,4096,256]{2,1,0:T(8,128)(2,1)}, u32[]{:S(2)}) copy-start(bf16[4,4096,256]{2,1,0:T(8,128)(2,1)} %shard_map.55.left_ref) | copy-start | bytes 25165828
  294.2 1.0 copy-start.23
  301.6 15.1 %copy-start.1 = (s32[16,16]{1,0:T(8,128)S(1)}, s32[16,16]{1,0:T(8,128)}, u32[]{:S(2)}) copy-start(s32[16,16]{1,0:T(8,128)} %param.8) | copy-start | bytes 3076
  306.2 2.0 collective-permute-start.28
  308.2 6.8 %collective-permute-start.29 = (bf16[8,32,128]{2,1,0:T(8,128)(2,1)S(1)}, bf16[8,32,128]{2,1,0:T(8,128)(2,1)S(1)}, u32[]{:S(2)}, u32[]{:S(2)}) collective-permute-start(bf16[8,32,128]{2,1,0:T(8,128)(2,1)S(1)} %get-tuple-element.126), channel_id=1, source_target_pairs={{0,2},{1,3},{2,4},{3,5},{4,6},{5,7},{6,0},{7,1},{8,10},{9,11},{10,... | collective-permute-start | bytes 196616 | tf_op jit(solution)/shard_map/ppermute | solution.py:350
  308.3 6.7 %collective-permute-start.30 = (bf16[8,32,128]{2,1,0:T(8,128)(2,1)S(1)}, bf16[8,32,128]{2,1,0:T(8,128)(2,1)S(1)}, u32[]{:S(2)}, u32[]{:S(2)}) collective-permute-start(bf16[8,32,128]{2,1,0:T(8,128)(2,1)S(1)} %get-tuple-element.127), channel_id=1, source_target_pairs={{0,4},{1,5},{2,6},{3,7},{4,0},{5,1},{6,2},{7,3},{8,12},{9,13},{10,... | collective-permute-start | bytes 196616 | tf_op jit(solution)/shard_map/ppermute | solution.py:350
  310.2 5.5 %collective-permute-start.31 = (bf16[8,32,128]{2,1,0:T(8,128)(2,1)S(1)}, bf16[8,32,128]{2,1,0:T(8,128)(2,1)S(1)}, u32[]{:S(2)}, u32[]{:S(2)}) collective-permute-start(bf16[8,32,128]{2,1,0:T(8,128)(2,1)S(1)} %get-tuple-element.128), channel_id=1, source_target_pairs={{0,6},{1,7},{2,0},{3,1},{4,2},{5,3},{6,4},{7,5},{8,14},{9,15},{10,... | collective-permute-start | bytes 196616 | tf_op jit(solution)/shard_map/ppermute | solution.py:350

commit v4 on v3

--- a/solution.py
+++ b/solution.py
@@ -13,6 +13,7 @@
 STEP = 256
 VMEM = 60 * 2**20
 bf16, f32 = jnp.bfloat16, jnp.float32
+BRIEF = pl.CostEstimate(flops=1, bytes_accessed=1, transcendentals=0)
 
 
 def params(limit=VMEM):
@@ -44,10 +45,6 @@
     ]
 
 
-def moved(elements):
-    return pl.CostEstimate(flops=0, bytes_accessed=4 * elements, transcendentals=0)
-
-
 def gather_kernel(starts, index_ref, blocks_ref, *refs):
     n = len(starts)
     outs, mids, sems = refs[:n], refs[n : 2 * n], refs[2 * n]
@@ -74,7 +71,7 @@
             scratch_shapes=relay_scratch(outs),
         ),
         compiler_params=params(),
-        cost_estimate=moved(sum(SIDE * rows * width for _, _, rows in bundles)),
+        cost_estimate=BRIEF,
     )(jnp.concatenate([index for index, _, _ in bundles]), blocks)
 
 
@@ -96,7 +93,7 @@
         out_specs=[pl.BlockSpec(memory_space=pl.ANY)] * (SIDE - 1),
         scratch_shapes=relay_scratch(outs),
         compiler_params=params(),
-        cost_estimate=moved((SIDE - 1) * pieces[0].size),
+        cost_estimate=BRIEF,
     )(*pieces)
 
 
@@ -174,11 +171,7 @@
             pltpu.VMEM((rank // LANES, rank * LANES, tile), bf16),
         ],
         compiler_params=params(),
-        cost_estimate=pl.CostEstimate(
-            flops=2 * examples * width * (rank * OUTS + rank * LANES),
-            bytes_accessed=4 * examples * width,
-            transcendentals=0,
-        ),
+        cost_estimate=BRIEF,
     )(grads, prec_in, prec_out)
 
 
@@ -207,14 +200,6 @@
         fetch(rights, right_ref, sems)
 
     multiply(right_ref, left_ref, out_ref, 0, 0)
-
-
-def cost(total, width, examples):
-    return pl.CostEstimate(
-        flops=2 * total * width * examples,
-        bytes_accessed=2 * width * (examples + total) + 4 * total * examples,
-        transcendentals=0,
-    )
 
 
 def early_products(left, owns, rights):
@@ -235,7 +220,7 @@
             pltpu.SemaphoreType.DMA((len(rights),)),
         ],
         compiler_params=params(32 * 2**20),
-        cost_estimate=cost(total, width, examples),
+        cost_estimate=BRIEF,
     )(left, *rights)
 
 
@@ -290,7 +275,7 @@
             ],
         ),
         compiler_params=params(32 * 2**20),
-        cost_estimate=cost(total, width, examples),
+        cost_estimate=BRIEF,
     )(block, row_a, row_b, left, early, *rights)
 
 
@@ -308,6 +293,7 @@
         out_shape=(jax.ShapeDtypeStruct(shape, f32),)
         + (jax.ShapeDtypeStruct(shape, bf16),) * (SIDE - 1),
         compiler_params=params(32 * 2**20),
+        cost_estimate=BRIEF,
     )(keep, got)
 
 
@@ -360,8 +346,11 @@
     def __call__(self, array, dy, dx):
         if len(self.done) >= IN_FLIGHT:
             array, _ = lax.optimization_barrier((array, self.done[-IN_FLIGHT]))
-        self.done.append(shift(array, dy, dx))
-        return self.done[-1]
+        arrived = shift(array, dy, dx)
+        if self.done:
+            arrived, _ = lax.optimization_barrier((arrived, self.done[-1]))
+        self.done.append(arrived)
+        return arrived
 
 
 def on_device(grads, prec_in, prec_out, requests, pairs):
@@ -388,9 +377,12 @@
         out.append(listed)
     calls = [out[0][:3], out[0][3:6], out[0][6:] + out[1]]
     made = [v for call in calls for v in gather(blocks, call)]
+    left = left_transposed(grads, prec_in, prec_out)
     parts = []
     for p in range(len(PARTS)):
         got = dict(zip(need, made[p * len(need) : (p + 1) * len(need)]))
+        if p:
+            got, left = lax.optimization_barrier((got, left))
         for f, d in need[:6]:
             got[f, d] = send(got[f, d], 0 if f else d, d if f else 0)
         parts.append([[got[f, d] for d in range(SIDE)] for f in range(2)])
@@ -401,8 +393,6 @@
         for f, d in need[:6]:
             got[f, d] = send(sides[f][d - 1], d if f else 0, 0 if f else d)
         late_in.append(got)
-
-    left = left_transposed(grads, prec_in, prec_out)
 
     own, early, late = need[6:], need[:3], need[3:6]
     order = own + early + late

time: 317 us -> 312 us (0.984); the launches traced: 317 us -> 307 us
  starting transfers between devices: 71.1 us -> 51.1 us
  waiting for transfers between devices: 143 us -> 153 us
  local copies, waits for them, and re-layouts: 16.1 us -> 19.3 us
    ppermute x24, starting transfers between devices: 58 us -> 38.1 us  [shift(): return lax.ppermute(array, 'ex', pairs)]
    ppermute x24, waiting for transfers between devices: 137 us -> 147 us  [shift(): return lax.ppermute(array, 'ex', pairs)]
    unnamed x58 -> x50, local copies, waits for them, and re-layouts: 14.3 us -> 17.5 us
  transfers between devices with their start and end apart: 32 -> 32, of which waited for: 11 -> 14; matrix products, arithmetic and copies ran while one was open for 0% -> 0% of each run, Pallas kernels for 20% -> 19%
where the time goes in v4:
time: 312 us; the launch traced here: 307 us
  waiting for transfers between devices  153 us (49%)
  Pallas kernels  83.4 us (27%)
  starting transfers between devices  51.1 us (16%)
  local copies, waits for them, and re-layouts  19.3 us (6%)
    ppermute x24, waiting for transfers between devices, shift(): return lax.ppermute(array, 'ex', pairs)  147 us
    ppermute x24, starting transfers between devices, shift(): return lax.ppermute(array, 'ex', pairs)  38.1 us
    pallas_call x2, Pallas kernels, early_products(): pl.pallas_call(functools.partial(early_kernel, owned, len(rights)), out_s...  19.3 us
    pallas_call x3, Pallas kernels, gather(): pl.pallas_call(functools.partial(gather_kernel, [start for _, start, _ in...  18 us
    unnamed x50, local copies, waits for them, and re-layouts  17.5 us
    pallas_call x1, Pallas kernels, left_transposed(): pl.pallas_call(left_kernel, out_shape=jax.ShapeDtypeStruct((examples // t...  16.1 us
    pallas_call x2, Pallas kernels, tiles(): pl.pallas_call(functools.partial(tiles_kernel, len(rights)), out_shape=(o...  14.6 us
    pallas_call x4, Pallas kernels, turn(): pl.pallas_call(turn_kernel, out_shape=outs, in_specs=[pl.BlockSpec(memory...  13.5 us
  transfers between devices with their start and end apart: 32, of which 14 were waited for; matrix products, arithmetic and copies ran while one was open for 0% of the time, Pallas kernels for 19%

profile of v4, /device:TPU:0, one launch (start us, length us, event | category | flops | bytes accessed | tf_op | source)
XLA Modules:
  0.0 307.4 jit_solution(3353475802429200165)
XLA Ops:
  2.0 5.3 %shard_map.57 = (bf16[4,48,4096]{2,1,0:T(8,128)(2,1)}, bf16[4,48,4096]{2,1,0:T(8,128)(2,1)}, bf16[4,48,4096]{2,1,0:T(8,128)(2,1)}) custom-call(s32[12]{0:T(128)} %get-tuple-element.211.index_ref, bf16[8,128,4096]{2,1,0:T(8,128)(2,1)} %bitcast.31), custom_call_target="tpu_custom_call" | custom-call | flops 1 | bytes 1 | tf_op jit(solution)/shard_map/pallas_call | solution.py:63
  7.3 1.7 collective-permute-start
  9.0 1.7 collective-permute-start.5
  10.6 3.0 collective-permute-start.4
  13.6 5.4 %shard_map.58 = (bf16[4,48,4096]{2,1,0:T(8,128)(2,1)}, bf16[4,48,4096]{2,1,0:T(8,128)(2,1)}, bf16[4,48,4096]{2,1,0:T(8,128)(2,1)}) custom-call(s32[12]{0:T(128)} %get-tuple-element.212.index_ref, bf16[8,128,4096]{2,1,0:T(8,128)(2,1)} %bitcast.32), custom_call_target="tpu_custom_call" | custom-call | flops 1 | bytes 1 | tf_op jit(solution)/shard_map/pallas_call | solution.py:63
  19.5 2.8 collective-permute-start.2
  22.3 22.8 %collective-permute-done.refs_1_ = bf16[4,48,4096]{2,1,0:T(8,128)(2,1)S(1)} collective-permute-done((bf16[4,48,4096]{2,1,0:T(8,128)(2,1)}, bf16[4,48,4096]{2,1,0:T(8,128)(2,1)S(1)}, u32[]{:S(2)}, u32[]{:S(2)}) %collective-permute-start) | collective-permute-done | bytes 1572896 | tf_op jit(solution)/shard_map/ppermute | solution.py:327
  45.2 1.8 collective-permute-start.1
  47.6 7.3 %shard_map.55 = (bf16[4,48,4096]{2,1,0:T(8,128)(2,1)}, bf16[4,48,4096]{2,1,0:T(8,128)(2,1)}, bf16[4,16,4096]{2,1,0:T(8,128)(2,1)}, bf16[4,16,4096]{2,1,0:T(8,128...) custom-call(s32[40]{0:T(128)} %concatenate.22.index_ref, ...), custom_call_target="tpu_custom_call" | custom-call | flops 1 | bytes 1 | tf_op jit(solution)/shard_map/pallas_call | solution.py:63
  54.9 16.1 %shard_map.56.left_ref = bf16[4,4096,256]{2,1,0:T(8,128)(2,1)} custom-call(bf16[1024,4096]{1,0:T(8,128)(2,1)} %bitcast.34, bf16[64,64]{1,0:T(8,128)(2,1)} %bitcast.35, bf16[64,64]{1,0:T(8,128)(2,1)} %bitcast.36), custom_call_target="tpu_custom_call" | custom-call | flops 1 | bytes 1 | tf_op jit(solution)/shard_map/pallas_call | solution.py:162
  71.0 0.9 collective-permute-start.7
  71.8 2.5 collective-permute-start.6
  74.3 7.7 %collective-permute-done.3.refs_1_.refs_5_ = bf16[4,48,4096]{2,1,0:T(8,128)(2,1)} collective-permute-done((bf16[4,48,4096]{2,1,0:T(8,128)(2,1)}, bf16[4,48,4096]{2,1,0:T(8,128)(2,1)}, u32[]{:S(2)}, u32[]{:S(2)}) %collective-permute-start.3) | collective-permute-done | bytes 1572896 | tf_op jit(solution)/shard_map/ppermute | solution.py:327
  82.0 2.3 collective-permute-done.1.refs_2_
  84.4 9.5 %collective-permute-done.7.refs_1_ = bf16[4,16,4096]{2,1,0:T(8,128)(2,1)} collective-permute-done((bf16[4,16,4096]{2,1,0:T(8,128)(2,1)S(1)}, bf16[4,16,4096]{2,1,0:T(8,128)(2,1)}, u32[]{:S(2)}, u32[]{:S(2)}) %collective-permute-start.7) | collective-permute-done | bytes 524320 | tf_op jit(solution)/shard_map/ppermute | solution.py:327
  93.9 4.3 %shard_map.59 = (bf16[4,48,4096]{2,1,0:T(8,128)(2,1)}, bf16[4,48,4096]{2,1,0:T(8,128)(2,1)}, bf16[4,48,4096]{2,1,0:T(8,128)(2,1)}) custom-call(bf16[4,48,4096]{2,1,0:T(8,128)(2,1)} %get-tuple-element.108.refs_0_, bf16[4,48,4096]{2,1,0:T(8,128)(2,1)} %copy-done.5, bf16[4,48,4096]{2,1,0:T(8,128)(2,1)} %collective-permute-done.1.refs_2_, ...), custom_call_target="tpu_custom_call" | custom-call | flops 1 | bytes 1 | tf_op jit(solution)/shard_map/pallas_call | solution.py:89
  98.2 1.3 collective-permute-start.8
  99.5 2.6 collective-permute-start.12
  102.4 3.0 collective-permute-start.10
  105.3 1.8 collective-permute-start.9
  107.1 4.4 %shard_map.60 = (bf16[4,48,4096]{2,1,0:T(8,128)(2,1)}, bf16[4,48,4096]{2,1,0:T(8,128)(2,1)}, bf16[4,48,4096]{2,1,0:T(8,128)(2,1)}) custom-call(bf16[4,48,4096]{2,1,0:T(8,128)(2,1)} %get-tuple-element.121.refs_0_.refs_4_, bf16[4,48,4096]{2,1,0:T(8,128)(2,1)} %collective-permute-done.3.refs_1_.refs_5_, ...), custom_call_target="tpu_custom_call" | custom-call | flops 1 | bytes 1 | tf_op jit(solution)/shard_map/pallas_call | solution.py:89
  111.6 37.4 %collective-permute-done.12.refs_2_.refs_6_ = bf16[4,16,4096]{2,1,0:T(8,128)(2,1)} collective-permute-done((bf16[4,16,4096]{2,1,0:T(8,128)(2,1)}, bf16[4,16,4096]{2,1,0:T(8,128)(2,1)}, u32[]{:S(2)}, u32[]{:S(2)}) %collective-permute-start.12) | collective-permute-done | bytes 524320 | tf_op jit(solution)/shard_map/ppermute | solution.py:327
  148.9 9.7 %collective-permute-done.11.refs_1_.refs_5_ = bf16[4,16,4096]{2,1,0:T(8,128)(2,1)} collective-permute-done((bf16[4,16,4096]{2,1,0:T(8,128)(2,1)}, bf16[4,16,4096]{2,1,0:T(8,128)(2,1)}, u32[]{:S(2)}, u32[]{:S(2)}) %collective-permute-start.11) | collective-permute-done | bytes 524320 | tf_op jit(solution)/shard_map/ppermute | solution.py:327
  158.6 1.2 collective-permute-start.13
  159.8 1.8 collective-permute-start.14
  161.6 0.7 collective-permute-start.15
  162.3 2.5 collective-permute-start.16
  164.8 0.8 collective-permute-start.17
  166.2 30.1 %collective-permute-done.13 = bf16[4,48,4096]{2,1,0:T(8,128)(2,1)} collective-permute-done((bf16[4,48,4096]{2,1,0:T(8,128)(2,1)}, bf16[4,48,4096]{2,1,0:T(8,128)(2,1)}, u32[]{:S(2)}, u32[]{:S(2)}) %collective-permute-start.13) | collective-permute-done | bytes 1572896 | tf_op jit(solution)/shard_map/ppermute | solution.py:327
  196.2 2.7 collective-permute-done.14
  199.0 1.6 copy-done.9
  200.6 1.6 copy-done.10
  202.1 14.2 %shard_map.61.early_ref = f32[8,960,128]{2,1,0:T(8,128)S(1)} custom-call(bf16[4,4096,256]{2,1,0:T(8,128)(2,1)} %shard_map.56.left_ref, bf16[4,48,4096]{2,1,0:T(8,128)(2,1)S(1)} %copy-done.9, bf16[4,48,4096]{2,1,0:T(8,128)(2,1)S(1)} %copy-done.6, bf16[4,48,4096]{2,1,0:T(8,128)(2,1)} %collective-permute-done.1.refs_2_, bf16[4,48,4096]{2,1,0:T(8,128)(2,1)S(1)} %copy-done.8, ...), custom_call_target="tpu_custom_call" | custom-call | flops 1 | bytes 1 | tf_op jit(solution)/shard_map/pallas_call | solution.py:211
  216.4 1.9 copy-done.3
  218.3 12.2 %collective-permute-done.15 = bf16[4,48,4096]{2,1,0:T(8,128)(2,1)} collective-permute-done((bf16[4,48,4096]{2,1,0:T(8,128)(2,1)}, bf16[4,48,4096]{2,1,0:T(8,128)(2,1)}, u32[]{:S(2)}, u32[]{:S(2)}) %collective-permute-start.15) | collective-permute-done | bytes 1572896 | tf_op jit(solution)/shard_map/ppermute | solution.py:327
  230.5 2.1 copy-done.4
  232.6 10.1 %shard_map.62 = (f32[32,96,128]{2,1,0:T(8,128)S(1)}, f32[32,96,128]{2,1,0:T(8,128)}) custom-call(s32[64]{0:T(128)S(1)} %squeeze.29.block_ref, s32[64]{0:T(128)S(1)} %mul.49.row_a_ref, s32[64]{0:T(128)S(1)} %mul.51.row_b_ref, bf16[4,4096,256]{2,1,0:T(8,128)(2,1)S(1)} %bitcast.27, f32[8,960,128]{2,1,0:T(8,128)S(1)} %copy-done.4, ...), custom_call_target="tpu_custom_call" | custom-call | flops 1 | bytes 1 | tf_op jit(solution)/shard_map/pallas_call | solution.py:261
  242.9 2.3 shard_map.64
  245.2 0.9 collective-permute-start.22
  246.1 2.4 shard_map.65
  248.5 2.5 collective-permute-start.23
  251.0 1.8 collective-permute-start.24
  252.7 0.7 collective-permute-start.25
  253.5 7.6 %collective-permute-done.22 = bf16[4,16,4096]{2,1,0:T(8,128)(2,1)} collective-permute-done((bf16[4,16,4096]{2,1,0:T(8,128)(2,1)}, bf16[4,16,4096]{2,1,0:T(8,128)(2,1)}, u32[]{:S(2)}, u32[]{:S(2)}) %collective-permute-start.22) | collective-permute-done | bytes 524320 | tf_op jit(solution)/shard_map/ppermute | solution.py:327
  261.1 1.6 collective-permute-start.26
  262.8 1.2 copy-done.13
  263.9 1.4 copy-done.14
  265.3 0.9 shard_map.63
  266.3 0.8 copy-done.15
  267.1 1.9 collective-permute-start.19
  269.0 0.8 copy-done.17
  269.8 3.6 %collective-permute-start.20 = (bf16[8,96,128]{2,1,0:T(8,128)(2,1)}, bf16[8,96,128]{2,1,0:T(8,128)(2,1)S(1)}, u32[]{:S(2)}, u32[]{:S(2)}) collective-permute-start(bf16[8,96,128]{2,1,0:T(8,128)(2,1)} %get-tuple-element.162), channel_id=1, source_target_pairs={{0,4},{1,5},{2,6},{3,7},{4,0},{5,1},{6,2},{7,3},{8,12},{9,13},{10,... | collective-permute-start | bytes 589832 | tf_op jit(solution)/shard_map/ppermute | solution.py:336
  273.4 4.3 %collective-permute-done.25 = bf16[4,16,4096]{2,1,0:T(8,128)(2,1)S(1)} collective-permute-done((bf16[4,16,4096]{2,1,0:T(8,128)(2,1)}, bf16[4,16,4096]{2,1,0:T(8,128)(2,1)S(1)}, u32[]{:S(2)}, u32[]{:S(2)}) %collective-permute-start.25) | collective-permute-done | bytes 524320 | tf_op jit(solution)/shard_map/ppermute | solution.py:327
  277.7 4.0 %collective-permute-start.21 = (bf16[8,96,128]{2,1,0:T(8,128)(2,1)}, bf16[8,96,128]{2,1,0:T(8,128)(2,1)S(1)}, u32[]{:S(2)}, u32[]{:S(2)}) collective-permute-start(bf16[8,96,128]{2,1,0:T(8,128)(2,1)} %get-tuple-element.163), channel_id=1, source_target_pairs={{0,6},{1,7},{2,0},{3,1},{4,2},{5,3},{6,4},{7,5},{8,14},{9,15},{10,... | collective-permute-start | bytes 589832 | tf_op jit(solution)/shard_map/ppermute | solution.py:336
  281.9 3.4 %copy-done.2 = bf16[4,4096,256]{2,1,0:T(8,128)(2,1)S(1)} copy-done((bf16[4,4096,256]{2,1,0:T(8,128)(2,1)S(1)}, bf16[4,4096,256]{2,1,0:T(8,128)(2,1)}, u32[]{:S(2)}) %copy-start.2) | copy-done | bytes 8388632
  285.3 1.0 copy-done.16
  286.3 1.0 copy-done.18
  287.4 5.1 %shard_map.66.early_ref = f32[8,320,128]{2,1,0:T(8,128)S(1)} custom-call(bf16[4,4096,256]{2,1,0:T(8,128)(2,1)S(1)} %copy-done.2, bf16[4,16,4096]{2,1,0:T(8,128)(2,1)S(1)} %copy-done.11, bf16[4,16,4096]{2,1,0:T(8,128)(2,1)} %collective-permute-done.7.refs_1_, bf16[4,16,4096]{2,1,0:T(8,128)(2,1)} %collective-permute-done.9.refs_2_, ...), custom_call_target="tpu_custom_call" | custom-call | flops 1 | bytes 1 | tf_op jit(solution)/shard_map/pallas_call | solution.py:211
  292.5 4.4 %shard_map.67 = (f32[32,32,128]{2,1,0:T(8,128)S(1)}, f32[32,32,128]{2,1,0:T(8,128)S(1)}) custom-call(s32[64]{0:T(128)S(1)} %squeeze.29.block_ref, s32[64]{0:T(128)S(1)} %mul.53.row_a_ref, s32[64]{0:T(128)S(1)} %mul.55.row_b_ref, bf16[4,4096,256]{2,1,0:T(8,128)(2,1)S(1)} %copy-done.2, f32[8,320,128]{2,1,0:T(8,128)S(1)} %shard_map.66.early_ref, ...), custom_call_target="tpu_custom_call" | custom-call | flops 1 | bytes 1 | tf_op jit(solution)/shard_map/pallas_call | solution.py:261
  297.0 1.9 collective-permute-done.28.got_ref
  299.1 1.9 collective-permute-start.30
  301.0 1.4 collective-permute-start.31
  302.3 3.5 %collective-permute-done.29.refs_5_ = bf16[8,32,128]{2,1,0:T(8,128)(2,1)S(1)} collective-permute-done((bf16[8,32,128]{2,1,0:T(8,128)(2,1)S(1)}, bf16[8,32,128]{2,1,0:T(8,128)(2,1)S(1)}, u32[]{:S(2)}, u32[]{:S(2)}) %collective-permute-start.29) | collective-permute-done | bytes 65568 | tf_op jit(solution)/shard_map/ppermute | solution.py:336
  306.4 1.0 shard_map.69
  (88 shorter events, 5.1 us)
Async XLA Ops:
  0.0 0.7 copy-start
  7.3 37.9 %collective-permute-start = (bf16[4,48,4096]{2,1,0:T(8,128)(2,1)}, bf16[4,48,4096]{2,1,0:T(8,128)(2,1)S(1)}, u32[]{:S(2)}, u32[]{:S(2)}) collective-permute-start(bf16[4,48,4096]{2,1,0:T(8,128)(2,1)} %get-tuple-element.109), channel_id=1, source_target_pairs={{0,32},{8,40},{16,48},{24,56},{32,64},{40,72},{48,80},{56,88},{64,... | collective-permute-start | bytes 4718600 | tf_op jit(solution)/shard_map/ppermute | solution.py:327
  9.0 62.0 %collective-permute-start.5 = (bf16[4,48,4096]{2,1,0:T(8,128)(2,1)}, bf16[4,48,4096]{2,1,0:T(8,128)(2,1)S(1)}, u32[]{:S(2)}, u32[]{:S(2)}) collective-permute-start(bf16[4,48,4096]{2,1,0:T(8,128)(2,1)} %get-tuple-element.115), channel_id=1, source_target_pairs={{0,96},{8,104},{16,112},{24,120},{32,0},{40,8},{48,16},{56,24},{64... | collective-permute-start | bytes 4718600 | tf_op jit(solution)/shard_map/ppermute | solution.py:327
  10.6 60.3 %collective-permute-start.4 = (bf16[4,48,4096]{2,1,0:T(8,128)(2,1)}, bf16[4,48,4096]{2,1,0:T(8,128)(2,1)}, u32[]{:S(2)}, u32[]{:S(2)}) collective-permute-start(bf16[4,48,4096]{2,1,0:T(8,128)(2,1)} %get-tuple-element.114), channel_id=1, source_target_pairs={{0,16},{8,24},{16,0},{24,8},{32,48},{40,56},{48,32},{56,40},{64,80... | collective-permute-start | bytes 4718600 | tf_op jit(solution)/shard_map/ppermute | solution.py:327
  19.0 63.0 %collective-permute-start.3 = (bf16[4,48,4096]{2,1,0:T(8,128)(2,1)}, bf16[4,48,4096]{2,1,0:T(8,128)(2,1)}, u32[]{:S(2)}, u32[]{:S(2)}) collective-permute-start(bf16[4,48,4096]{2,1,0:T(8,128)(2,1)} %get-tuple-element.113), channel_id=1, source_target_pairs={{0,8},{8,16},{16,24},{24,0},{32,40},{40,48},{48,56},{56,32},{64,72... | collective-permute-start | bytes 4718600 | tf_op jit(solution)/shard_map/ppermute | solution.py:327
  19.5 62.5 %collective-permute-start.2 = (bf16[4,48,4096]{2,1,0:T(8,128)(2,1)}, bf16[4,48,4096]{2,1,0:T(8,128)(2,1)}, u32[]{:S(2)}, u32[]{:S(2)}) collective-permute-start(bf16[4,48,4096]{2,1,0:T(8,128)(2,1)} %get-tuple-element.112), channel_id=1, source_target_pairs={{0,24},{8,0},{16,8},{24,16},{32,56},{40,32},{48,40},{56,48},{64,88... | collective-permute-start | bytes 4718600 | tf_op jit(solution)/shard_map/ppermute | solution.py:327
  45.2 9.7 %copy-start.5 = (bf16[4,48,4096]{2,1,0:T(8,128)(2,1)}, bf16[4,48,4096]{2,1,0:T(8,128)(2,1)S(1)}, u32[]{:S(2)}) copy-start(bf16[4,48,4096]{2,1,0:T(8,128)(2,1)S(1)} %collective-permute-done.refs_1_) | copy-start | bytes 4718596
  45.2 39.2 %collective-permute-start.1 = (bf16[4,48,4096]{2,1,0:T(8,128)(2,1)}, bf16[4,48,4096]{2,1,0:T(8,128)(2,1)}, u32[]{:S(2)}, u32[]{:S(2)}) collective-permute-start(bf16[4,48,4096]{2,1,0:T(8,128)(2,1)} %get-tuple-element.111), channel_id=1, source_target_pairs={{0,64},{8,72},{16,80},{24,88},{32,96},{40,104},{48,112},{56,120},{... | collective-permute-start | bytes 4718600 | tf_op jit(solution)/shard_map/ppermute | solution.py:327
  54.8 16.1 %copy-start.22 = (bf16[4,16,4096]{2,1,0:T(8,128)(2,1)S(1)}, bf16[4,16,4096]{2,1,0:T(8,128)(2,1)}, u32[]{:S(2)}) copy-start(bf16[4,16,4096]{2,1,0:T(8,128)(2,1)} %get-tuple-element.126) | copy-start | bytes 1572868
  54.9 17.0 %copy-start.21 = (bf16[4,16,4096]{2,1,0:T(8,128)(2,1)S(1)}, bf16[4,16,4096]{2,1,0:T(8,128)(2,1)}, u32[]{:S(2)}) copy-start(bf16[4,16,4096]{2,1,0:T(8,128)(2,1)} %get-tuple-element.124) | copy-start | bytes 1572868
  71.0 22.9 %copy-start.7 = (bf16[4,48,4096]{2,1,0:T(8,128)(2,1)}, bf16[4,48,4096]{2,1,0:T(8,128)(2,1)S(1)}, u32[]{:S(2)}) copy-start(bf16[4,48,4096]{2,1,0:T(8,128)(2,1)S(1)} %collective-permute-done.5.refs_3_) | copy-start | bytes 4718596
  71.0 22.9 %collective-permute-start.7 = (bf16[4,16,4096]{2,1,0:T(8,128)(2,1)S(1)}, bf16[4,16,4096]{2,1,0:T(8,128)(2,1)}, u32[]{:S(2)}, u32[]{:S(2)}) collective-permute-start(bf16[4,16,4096]{2,1,0:T(8,128)(2,1)S(1)} %copy-done.22), channel_id=1, source_target_pairs={{0,32},{8,40},{16,48},{24,56},{32,64},{40,72},{48,80},{56,88},{64,... | collective-permute-start | bytes 1572872 | tf_op jit(solution)/shard_map/ppermute | solution.py:327
  71.8 22.0 %collective-permute-start.6 = (bf16[4,16,4096]{2,1,0:T(8,128)(2,1)S(1)}, bf16[4,16,4096]{2,1,0:T(8,128)(2,1)}, u32[]{:S(2)}, u32[]{:S(2)}) collective-permute-start(bf16[4,16,4096]{2,1,0:T(8,128)(2,1)S(1)} %copy-done.21), channel_id=1, source_target_pairs={{0,96},{8,104},{16,112},{24,120},{32,0},{40,8},{48,16},{56,24},{64... | collective-permute-start | bytes 1572872 | tf_op jit(solution)/shard_map/ppermute | solution.py:327
  93.9 11.5 %copy-start.20 = (bf16[4,16,4096]{2,1,0:T(8,128)(2,1)S(1)}, bf16[4,16,4096]{2,1,0:T(8,128)(2,1)}, u32[]{:S(2)}) copy-start(bf16[4,16,4096]{2,1,0:T(8,128)(2,1)} %get-tuple-element.131) | copy-start | bytes 1572868
  98.2 66.6 %collective-permute-start.8 = (bf16[4,48,4096]{2,1,0:T(8,128)(2,1)}, bf16[4,48,4096]{2,1,0:T(8,128)(2,1)}, u32[]{:S(2)}, u32[]{:S(2)}) collective-permute-start(bf16[4,48,4096]{2,1,0:T(8,128)(2,1)} %get-tuple-element.129), channel_id=1, source_target_pairs={{0,8},{8,16},{16,24},{24,0},{32,40},{40,48},{48,56},{56,32},{64,72... | collective-permute-start | bytes 4718600 | tf_op jit(solution)/shard_map/ppermute | solution.py:327
  99.5 49.4 %collective-permute-start.12 = (bf16[4,16,4096]{2,1,0:T(8,128)(2,1)}, bf16[4,16,4096]{2,1,0:T(8,128)(2,1)}, u32[]{:S(2)}, u32[]{:S(2)}) collective-permute-start(bf16[4,16,4096]{2,1,0:T(8,128)(2,1)} %get-tuple-element.137), channel_id=1, source_target_pairs={{0,16},{8,24},{16,0},{24,8},{32,48},{40,56},{48,32},{56,40},{64,80... | collective-permute-start | bytes 1572872 | tf_op jit(solution)/shard_map/ppermute | solution.py:327
  102.1 56.5 %collective-permute-start.11 = (bf16[4,16,4096]{2,1,0:T(8,128)(2,1)}, bf16[4,16,4096]{2,1,0:T(8,128)(2,1)}, u32[]{:S(2)}, u32[]{:S(2)}) collective-permute-start(bf16[4,16,4096]{2,1,0:T(8,128)(2,1)} %get-tuple-element.135), channel_id=1, source_target_pairs={{0,8},{8,16},{16,24},{24,0},{32,40},{40,48},{48,56},{56,32},{64,72... | collective-permute-start | bytes 1572872 | tf_op jit(solution)/shard_map/ppermute | solution.py:327
  102.4 59.2 %collective-permute-start.10 = (bf16[4,16,4096]{2,1,0:T(8,128)(2,1)}, bf16[4,16,4096]{2,1,0:T(8,128)(2,1)}, u32[]{:S(2)}, u32[]{:S(2)}) collective-permute-start(bf16[4,16,4096]{2,1,0:T(8,128)(2,1)} %get-tuple-element.133), channel_id=1, source_target_pairs={{0,24},{8,0},{16,8},{24,16},{32,56},{40,32},{48,40},{56,48},{64,88... | collective-permute-start | bytes 1572872 | tf_op jit(solution)/shard_map/ppermute | solution.py:327
  105.3 56.2 %collective-permute-start.9 = (bf16[4,16,4096]{2,1,0:T(8,128)(2,1)S(1)}, bf16[4,16,4096]{2,1,0:T(8,128)(2,1)}, u32[]{:S(2)}, u32[]{:S(2)}) collective-permute-start(bf16[4,16,4096]{2,1,0:T(8,128)(2,1)S(1)} %copy-done.20), channel_id=1, source_target_pairs={{0,64},{8,72},{16,80},{24,88},{32,96},{40,104},{48,112},{56,120},{... | collective-permute-start | bytes 1572872 | tf_op jit(solution)/shard_map/ppermute | solution.py:327
  107.1 58.5 %copy-start.19 = (s32[64,2]{0,1:T(2,128)S(1)}, s32[64,2]{0,1:T(2,128)}, u32[]{:S(2)}) copy-start(s32[64,2]{0,1:T(2,128)} %param.9) | copy-start | bytes 1540
  107.1 91.9 %copy-start.6 = (bf16[4,48,4096]{2,1,0:T(8,128)(2,1)S(1)}, bf16[4,48,4096]{2,1,0:T(8,128)(2,1)}, u32[]{:S(2)}) copy-start(bf16[4,48,4096]{2,1,0:T(8,128)(2,1)} %copy-done.5) | copy-start | bytes 4718596
  107.1 91.9 %copy-start.8 = (bf16[4,48,4096]{2,1,0:T(8,128)(2,1)S(1)}, bf16[4,48,4096]{2,1,0:T(8,128)(2,1)}, u32[]{:S(2)}) copy-start(bf16[4,48,4096]{2,1,0:T(8,128)(2,1)} %copy-done.7) | copy-start | bytes 4718596
  158.6 37.6 %collective-permute-start.13 = (bf16[4,48,4096]{2,1,0:T(8,128)(2,1)}, bf16[4,48,4096]{2,1,0:T(8,128)(2,1)}, u32[]{:S(2)}, u32[]{:S(2)}) collective-permute-start(bf16[4,48,4096]{2,1,0:T(8,128)(2,1)} %get-tuple-element.144), channel_id=1, source_target_pairs={{0,24},{8,0},{16,8},{24,16},{32,56},{40,32},{48,40},{56,48},{64,88... | collective-permute-start | bytes 4718600 | tf_op jit(solution)/shard_map/ppermute | solution.py:327
  159.8 39.2 %collective-permute-start.14 = (bf16[4,48,4096]{2,1,0:T(8,128)(2,1)}, bf16[4,48,4096]{2,1,0:T(8,128)(2,1)}, u32[]{:S(2)}, u32[]{:S(2)}) collective-permute-start(bf16[4,48,4096]{2,1,0:T(8,128)(2,1)} %get-tuple-element.147), channel_id=1, source_target_pairs={{0,64},{8,72},{16,80},{24,88},{32,96},{40,104},{48,112},{56,120},{... | collective-permute-start | bytes 4718600 | tf_op jit(solution)/shard_map/ppermute | solution.py:327
  161.6 68.9 %collective-permute-start.15 = (bf16[4,48,4096]{2,1,0:T(8,128)(2,1)}, bf16[4,48,4096]{2,1,0:T(8,128)(2,1)}, u32[]{:S(2)}, u32[]{:S(2)}) collective-permute-start(bf16[4,48,4096]{2,1,0:T(8,128)(2,1)} %get-tuple-element.150), channel_id=1, source_target_pairs={{0,32},{8,40},{16,48},{24,56},{32,64},{40,72},{48,80},{56,88},{64,... | collective-permute-start | bytes 4718600 | tf_op jit(solution)/shard_map/ppermute | solution.py:327
  162.3 68.2 %collective-permute-start.16 = (bf16[4,48,4096]{2,1,0:T(8,128)(2,1)}, bf16[4,48,4096]{2,1,0:T(8,128)(2,1)}, u32[]{:S(2)}, u32[]{:S(2)}) collective-permute-start(bf16[4,48,4096]{2,1,0:T(8,128)(2,1)} %get-tuple-element.153), channel_id=1, source_target_pairs={{0,96},{8,104},{16,112},{24,120},{32,0},{40,8},{48,16},{56,24},{64... | collective-permute-start | bytes 4718600 | tf_op jit(solution)/shard_map/ppermute | solution.py:327
  164.8 65.7 %collective-permute-start.17 = (bf16[4,48,4096]{2,1,0:T(8,128)(2,1)}, bf16[4,48,4096]{2,1,0:T(8,128)(2,1)}, u32[]{:S(2)}, u32[]{:S(2)}) collective-permute-start(bf16[4,48,4096]{2,1,0:T(8,128)(2,1)} %get-tuple-element.156), channel_id=1, source_target_pairs={{0,16},{8,24},{16,0},{24,8},{32,48},{40,56},{48,32},{56,40},{64,80... | collective-permute-start | bytes 4718600 | tf_op jit(solution)/shard_map/ppermute | solution.py:327
  199.0 31.5 %slice-start = ((s8[8388608]{0:T(1024)(128)(4,1)}), s8[4194304]{0:T(1024)(128)(4,1)S(1)}, s32[]{:S(2)}) async-start(s8[8388608]{0:T(1024)(128)(4,1)} %bitcast.26), calls=%async_computation | async-start | bytes 8388608
  199.0 1.6 copy-start.9
  200.6 1.6 copy-start.10
  202.1 28.4 %slice-start.1 = ((s8[8388608]{0:T(1024)(128)(4,1)}), s8[4194304]{0:T(1024)(128)(4,1)S(1)}, s32[]{:S(2)}) async-start(s8[8388608]{0:T(1024)(128)(4,1)} %bitcast.26), calls=%async_computation.1 | async-start | bytes 8388608
  216.4 1.9 copy-start.3
  230.5 2.1 copy-start.4
  242.8 20.0 %collective-permute-start.18 = (f32[32,96,128]{2,1,0:T(8,128)}, f32[32,96,128]{2,1,0:T(8,128)S(1)}, u32[]{:S(2)}, u32[]{:S(2)}) collective-permute-start(f32[32,96,128]{2,1,0:T(8,128)} %get-tuple-element.159), channel_id=1, source_target_pairs={{0,1},{1,0},{2,3},{3,2},{4,5},{5,4},{6,7},{7,6},{8,9},{9,8},{10,11... | collective-permute-start | bytes 4718600 | tf_op jit(solution)/shard_map/ppermute | solution.py:331
  245.2 15.9 %collective-permute-start.22 = (bf16[4,16,4096]{2,1,0:T(8,128)(2,1)}, bf16[4,16,4096]{2,1,0:T(8,128)(2,1)}, u32[]{:S(2)}, u32[]{:S(2)}) collective-permute-start(bf16[4,16,4096]{2,1,0:T(8,128)(2,1)} %get-tuple-element.167), channel_id=1, source_target_pairs={{0,8},{8,16},{16,24},{24,0},{32,40},{40,48},{48,56},{56,32},{64,72... | collective-permute-start | bytes 1572872 | tf_op jit(solution)/shard_map/ppermute | solution.py:327
  248.5 17.8 %collective-permute-start.23 = (bf16[4,16,4096]{2,1,0:T(8,128)(2,1)}, bf16[4,16,4096]{2,1,0:T(8,128)(2,1)S(1)}, u32[]{:S(2)}, u32[]{:S(2)}) collective-permute-start(bf16[4,16,4096]{2,1,0:T(8,128)(2,1)} %get-tuple-element.170), channel_id=1, source_target_pairs={{0,24},{8,0},{16,8},{24,16},{32,56},{40,32},{48,40},{56,48},{64,88... | collective-permute-start | bytes 1572872 | tf_op jit(solution)/shard_map/ppermute | solution.py:327
  251.0 18.0 %collective-permute-start.24 = (bf16[4,16,4096]{2,1,0:T(8,128)(2,1)}, bf16[4,16,4096]{2,1,0:T(8,128)(2,1)S(1)}, u32[]{:S(2)}, u32[]{:S(2)}) collective-permute-start(bf16[4,16,4096]{2,1,0:T(8,128)(2,1)} %get-tuple-element.173), channel_id=1, source_target_pairs={{0,64},{8,72},{16,80},{24,88},{32,96},{40,104},{48,112},{56,120},{... | collective-permute-start | bytes 1572872 | tf_op jit(solution)/shard_map/ppermute | solution.py:327
  252.7 25.0 %collective-permute-start.25 = (bf16[4,16,4096]{2,1,0:T(8,128)(2,1)}, bf16[4,16,4096]{2,1,0:T(8,128)(2,1)S(1)}, u32[]{:S(2)}, u32[]{:S(2)}) collective-permute-start(bf16[4,16,4096]{2,1,0:T(8,128)(2,1)} %get-tuple-element.176), channel_id=1, source_target_pairs={{0,32},{8,40},{16,48},{24,56},{32,64},{40,72},{48,80},{56,88},{64,... | collective-permute-start | bytes 1572872 | tf_op jit(solution)/shard_map/ppermute | solution.py:327
  261.1 31.3 %collective-permute-start.26 = (bf16[4,16,4096]{2,1,0:T(8,128)(2,1)}, bf16[4,16,4096]{2,1,0:T(8,128)(2,1)}, u32[]{:S(2)}, u32[]{:S(2)}) collective-permute-start(bf16[4,16,4096]{2,1,0:T(8,128)(2,1)} %get-tuple-element.179), channel_id=1, source_target_pairs={{0,96},{8,104},{16,112},{24,120},{32,0},{40,8},{48,16},{56,24},{64... | collective-permute-start | bytes 1572872 | tf_op jit(solution)/shard_map/ppermute | solution.py:327
  262.8 1.2 copy-start.13
  263.9 28.5 %collective-permute-start.27 = (bf16[4,16,4096]{2,1,0:T(8,128)(2,1)}, bf16[4,16,4096]{2,1,0:T(8,128)(2,1)}, u32[]{:S(2)}, u32[]{:S(2)}) collective-permute-start(bf16[4,16,4096]{2,1,0:T(8,128)(2,1)} %get-tuple-element.182), channel_id=1, source_target_pairs={{0,16},{8,24},{16,0},{24,8},{32,48},{40,56},{48,32},{56,40},{64,80... | collective-permute-start | bytes 1572872 | tf_op jit(solution)/shard_map/ppermute | solution.py:327
  263.9 1.4 copy-start.14
  265.3 16.6 %copy-start.11 = (bf16[4,16,4096]{2,1,0:T(8,128)(2,1)S(1)}, bf16[4,16,4096]{2,1,0:T(8,128)(2,1)}, u32[]{:S(2)}) copy-start(bf16[4,16,4096]{2,1,0:T(8,128)(2,1)} %get-tuple-element.164.refs_0_) | copy-start | bytes 1572868
  265.3 16.6 %copy-start.12 = (bf16[4,16,4096]{2,1,0:T(8,128)(2,1)S(1)}, bf16[4,16,4096]{2,1,0:T(8,128)(2,1)}, u32[]{:S(2)}) copy-start(bf16[4,16,4096]{2,1,0:T(8,128)(2,1)} %get-tuple-element.165.refs_0_.refs_4_) | copy-start | bytes 1572868
  266.3 0.8 copy-start.15
  267.1 25.4 %collective-permute-start.19 = (bf16[8,96,128]{2,1,0:T(8,128)(2,1)}, bf16[8,96,128]{2,1,0:T(8,128)(2,1)S(1)}, u32[]{:S(2)}, u32[]{:S(2)}) collective-permute-start(bf16[8,96,128]{2,1,0:T(8,128)(2,1)} %get-tuple-element.161), channel_id=1, source_target_pairs={{0,2},{1,3},{2,4},{3,5},{4,6},{5,7},{6,0},{7,1},{8,10},{9,11},{10,... | collective-permute-start | bytes 589832 | tf_op jit(solution)/shard_map/ppermute | solution.py:336
  269.0 0.8 copy-start.17
  269.8 22.7 %collective-permute-start.20 = (bf16[8,96,128]{2,1,0:T(8,128)(2,1)}, bf16[8,96,128]{2,1,0:T(8,128)(2,1)S(1)}, u32[]{:S(2)}, u32[]{:S(2)}) collective-permute-start(bf16[8,96,128]{2,1,0:T(8,128)(2,1)} %get-tuple-element.162), channel_id=1, source_target_pairs={{0,4},{1,5},{2,6},{3,7},{4,0},{5,1},{6,2},{7,3},{8,12},{9,13},{10,... | collective-permute-start | bytes 589832 | tf_op jit(solution)/shard_map/ppermute | solution.py:336
  277.7 14.8 %collective-permute-start.21 = (bf16[8,96,128]{2,1,0:T(8,128)(2,1)}, bf16[8,96,128]{2,1,0:T(8,128)(2,1)S(1)}, u32[]{:S(2)}, u32[]{:S(2)}) collective-permute-start(bf16[8,96,128]{2,1,0:T(8,128)(2,1)} %get-tuple-element.163), channel_id=1, source_target_pairs={{0,6},{1,7},{2,0},{3,1},{4,2},{5,3},{6,4},{7,5},{8,14},{9,15},{10,... | collective-permute-start | bytes 589832 | tf_op jit(solution)/shard_map/ppermute | solution.py:336
  281.9 3.4 %copy-start.2 = (bf16[4,4096,256]{2,1,0:T(8,128)(2,1)S(1)}, bf16[4,4096,256]{2,1,0:T(8,128)(2,1)}, u32[]{:S(2)}) copy-start(bf16[4,4096,256]{2,1,0:T(8,128)(2,1)} %shard_map.56.left_ref) | copy-start | bytes 25165828
  285.3 1.0 copy-start.16
  286.3 1.0 copy-start.18
  292.5 14.9 %copy-start.1 = (s32[16,16]{1,0:T(8,128)S(1)}, s32[16,16]{1,0:T(8,128)}, u32[]{:S(2)}) copy-start(s32[16,16]{1,0:T(8,128)} %param.8) | copy-start | bytes 3076
  297.0 2.0 collective-permute-start.28
  299.0 6.8 %collective-permute-start.29 = (bf16[8,32,128]{2,1,0:T(8,128)(2,1)S(1)}, bf16[8,32,128]{2,1,0:T(8,128)(2,1)S(1)}, u32[]{:S(2)}, u32[]{:S(2)}) collective-permute-start(bf16[8,32,128]{2,1,0:T(8,128)(2,1)S(1)} %get-tuple-element.190), channel_id=1, source_target_pairs={{0,2},{1,3},{2,4},{3,5},{4,6},{5,7},{6,0},{7,1},{8,10},{9,11},{10,... | collective-permute-start | bytes 196616 | tf_op jit(solution)/shard_map/ppermute | solution.py:336
  299.1 6.7 %collective-permute-start.30 = (bf16[8,32,128]{2,1,0:T(8,128)(2,1)S(1)}, bf16[8,32,128]{2,1,0:T(8,128)(2,1)S(1)}, u32[]{:S(2)}, u32[]{:S(2)}) collective-permute-start(bf16[8,32,128]{2,1,0:T(8,128)(2,1)S(1)} %get-tuple-element.191), channel_id=1, source_target_pairs={{0,4},{1,5},{2,6},{3,7},{4,0},{5,1},{6,2},{7,3},{8,12},{9,13},{10,... | collective-permute-start | bytes 196616 | tf_op jit(solution)/shard_map/ppermute | solution.py:336
  301.0 5.5 %collective-permute-start.31 = (bf16[8,32,128]{2,1,0:T(8,128)(2,1)S(1)}, bf16[8,32,128]{2,1,0:T(8,128)(2,1)S(1)}, u32[]{:S(2)}, u32[]{:S(2)}) collective-permute-start(bf16[8,32,128]{2,1,0:T(8,128)(2,1)S(1)} %get-tuple-element.192), channel_id=1, source_target_pairs={{0,6},{1,7},{2,0},{3,1},{4,2},{5,3},{6,4},{7,5},{8,14},{9,15},{10,... | collective-permute-start | bytes 196616 | tf_op jit(solution)/shard_map/ppermute | solution.py:336

commit v5 on v4

--- a/solution.py
+++ b/solution.py
@@ -9,7 +9,7 @@
 
 BLOCK = 128
 SIDE = 4
-PARTS = ((0, 48), (96, 16))
+PARTS = ((0, 64), (64, 64))
 STEP = 256
 VMEM = 60 * 2**20
 bf16, f32 = jnp.bfloat16, jnp.float32
@@ -191,40 +191,37 @@
         product_ref[first_block + b, at : at + rows, :] = product[:, b * BLOCK : (b + 1) * BLOCK]
 
 
-def early_kernel(owns, count, left_ref, *refs):
-    rights, (out_ref, right_ref, sems) = refs[:count], refs[count:]
-    rights = [ref.at[0] for ref in rights[:owns]] + [ref for ref in rights[owns:]]
+def early_kernel(count, left_ref, *refs):
+    owns, (out_ref, right_ref, sems) = refs[:count], refs[count:]
 
     @pl.when(pl.program_id(0) == 0)
     def _():
-        fetch(rights, right_ref, sems)
+        fetch([ref.at[0] for ref in owns], right_ref, sems)
 
     multiply(right_ref, left_ref, out_ref, 0, 0)
 
 
-def early_products(left, owns, rights):
+def early_products(left, owns):
     groups, width, _ = left.shape
     examples = groups * STEP
-    rows = owns[0].shape[1]
-    total = rows * len(owns) + sum(r.shape[0] for r in rights)
-    owned, rights = len(owns), [*owns, *rights]
-    return pl.pallas_call(
-        functools.partial(early_kernel, owned, len(rights)),
+    total = sum(o.shape[1] for o in owns)
+    return pl.pallas_call(
+        functools.partial(early_kernel, len(owns)),
         out_shape=jax.ShapeDtypeStruct((examples // BLOCK, total, BLOCK), f32),
-        grid=(examples // STEP,),
+        grid=(groups,),
         in_specs=[pl.BlockSpec((1, width, STEP), lambda i: (i, 0, 0))]
-        + [pl.BlockSpec(memory_space=pl.ANY)] * len(rights),
+        + [pl.BlockSpec(memory_space=pl.ANY)] * len(owns),
         out_specs=pl.BlockSpec((STEP // BLOCK, total, BLOCK), lambda i: (i, 0, 0)),
         scratch_shapes=[
             pltpu.VMEM((total, width), bf16),
-            pltpu.SemaphoreType.DMA((len(rights),)),
+            pltpu.SemaphoreType.DMA((len(owns),)),
         ],
         compiler_params=params(32 * 2**20),
         cost_estimate=BRIEF,
-    )(left, *rights)
-
-
-def tiles_kernel(count, block_ref, row_a_ref, row_b_ref, left_ref, early_ref, *refs):
+    )(left, *owns)
+
+
+def tiles_kernel(count, block_ref, row_ref, left_ref, early_ref, *refs):
     rights = refs[:count]
     keep_ref, give_ref, product_ref, right_ref, sems, early_sem = refs[count:]
     step = pl.program_id(0)
@@ -241,28 +238,25 @@
     @pl.when(step == pl.num_programs(0) - 1)
     def _():
         early_copy.wait()
-        half = keep_ref.shape[1] // 2
+        rows = keep_ref.shape[1]
         for out_ref, base in ((give_ref, keep_ref.shape[0]), (keep_ref, 0)):
             for q in range(out_ref.shape[0]):
-                block = block_ref[base + q]
-                row_a = pl.multiple_of(row_a_ref[base + q], 16)
-                row_b = pl.multiple_of(row_b_ref[base + q], 16)
-                out_ref[q, :half, :] = product_ref[block, pl.ds(row_a, half), :]
-                out_ref[q, half:, :] = product_ref[block, pl.ds(row_b, half), :]
-
-
-def tiles(left, early, rights, rows, block, row_a, row_b):
+                row = pl.multiple_of(row_ref[base + q], 16)
+                out_ref[q] = product_ref[block_ref[base + q], pl.ds(row, rows), :]
+
+
+def tiles(left, early, rights, rows, block, row):
     groups, width, _ = left.shape
     examples = groups * STEP
     total = sum(r.shape[0] for r in rights)
     pairs = block.shape[0]
-    out = jax.ShapeDtypeStruct((pairs // 2, 2 * rows, BLOCK), f32)
+    out = jax.ShapeDtypeStruct((pairs // 2, rows, BLOCK), f32)
     out_spec = pl.BlockSpec(out.shape, lambda i, *_: (0, 0, 0))
     return pl.pallas_call(
         functools.partial(tiles_kernel, len(rights)),
         out_shape=(out, out),
         grid_spec=pltpu.PrefetchScalarGridSpec(
-            num_scalar_prefetch=3,
+            num_scalar_prefetch=2,
             grid=(examples // STEP,),
             in_specs=[pl.BlockSpec((1, width, STEP), lambda i, *_: (i, 0, 0))]
             + [pl.BlockSpec(memory_space=pl.ANY)] * (1 + len(rights)),
@@ -276,7 +270,7 @@
         ),
         compiler_params=params(32 * 2**20),
         cost_estimate=BRIEF,
-    )(block, row_a, row_b, left, early, *rights)
+    )(block, row, left, early, *rights)
 
 
 def merge_kernel(keep_ref, got_ref, own_ref, *send_refs):
@@ -318,13 +312,15 @@
     )(*ins)
 
 
-def shift(array, dy, dx):
-    pairs = [
-        (y * SIDE + x, (y + dy) % SIDE * SIDE + (x + dx) % SIDE)
-        for y in range(SIDE)
-        for x in range(SIDE)
-    ]
-    return lax.ppermute(array, "ex", pairs)
+def shift(array, leg, d):
+    pairs = []
+    for y in range(SIDE):
+        for x in range(SIDE):
+            for i in range(2 * SIDE):
+                dy, dx = (d, 0) if leg == i % 2 else (0, d)
+                to = (y + dy) % SIDE * SIDE + (x + dx) % SIDE
+                pairs.append(((y * SIDE + x) * 2 * SIDE + i, to * 2 * SIDE + i))
+    return lax.ppermute(array, ("ex", "lay"), pairs)
 
 
 def swap_cores(array):
@@ -336,21 +332,11 @@
     return lax.ppermute(array, "lay", pairs)
 
 
-IN_FLIGHT = 5
-
-
-class Sender:
-    def __init__(self):
-        self.done = []
-
-    def __call__(self, array, dy, dx):
-        if len(self.done) >= IN_FLIGHT:
-            array, _ = lax.optimization_barrier((array, self.done[-IN_FLIGHT]))
-        arrived = shift(array, dy, dx)
-        if self.done:
-            arrived, _ = lax.optimization_barrier((arrived, self.done[-1]))
-        self.done.append(arrived)
-        return arrived
+def after(value, other):
+    return lax.optimization_barrier((value, other))[0]
+
+
+STEPS = (1, 3, 2)
 
 
 def on_device(grads, prec_in, prec_out, requests, pairs):
@@ -367,59 +353,51 @@
     wanted = jnp.concatenate([wanted, wanted], 1)
     wanted = lax.dynamic_slice(wanted, (my_y, my_x), (SIDE, SIDE))
 
-    send = Sender()
-    need = [(0, 1), (0, 3), (1, 2), (1, 1), (1, 3), (0, 2), (0, 0), (1, 0)]
-    out = []
-    for row, rows in PARTS:
-        listed = [
-            (wanted[:, d] if f else wanted[d], row + f * rows, rows) for f, d in need
-        ]
-        out.append(listed)
-    calls = [out[0][:3], out[0][3:6], out[0][6:] + out[1]]
-    made = [v for call in calls for v in gather(blocks, call)]
-    left = left_transposed(grads, prec_in, prec_out)
-    parts = []
-    for p in range(len(PARTS)):
-        got = dict(zip(need, made[p * len(need) : (p + 1) * len(need)]))
-        if p:
-            got, left = lax.optimization_barrier((got, left))
-        for f, d in need[:6]:
-            got[f, d] = send(got[f, d], 0 if f else d, d if f else 0)
-        parts.append([[got[f, d] for d in range(SIDE)] for f in range(2)])
-    late_in = []
-    for a, b in parts:
-        sides = [turn(a), turn(b)]
-        got = {}
-        for f, d in need[:6]:
-            got[f, d] = send(sides[f][d - 1], d if f else 0, 0 if f else d)
-        late_in.append(got)
-
-    own, early, late = need[6:], need[:3], need[3:6]
-    order = own + early + late
-
-    def place(f, d):
-        return sum(jnp.where(d == k, at, 0) for at, (n, k) in enumerate(order) if n == f)
+    wanted = jnp.where(my_core == 0, wanted, wanted.T)
+
+    (row1, rows1), (row2, rows2) = PARTS
+    one = {}
+    for d in STEPS:
+        (bundle,) = gather(blocks, [(wanted[d], row1, rows1)])
+        one[d] = shift(bundle, 0, d)
+    one[0], *bundles = gather(
+        blocks, [(wanted[0], row1, rows1)] + [(wanted[d], row2, rows2) for d in range(SIDE)]
+    )
+    left = left_transposed(after(grads, bundles), prec_in, prec_out)
+    bundles = after(bundles, (left, one[1]))
+    two = {d: shift(bundles[d], 0, d) for d in STEPS} | {0: bundles[0]}
+    one = [one[d] for d in range(SIDE)]
+    turned = dict(enumerate(turn(one), 1))
+    one_in = [shift(turned[k], 1, k) for k in STEPS]
+    early_one = early_products(after(left, turned), one)
+    two = after([two[d] for d in range(SIDE)], early_one)
+    turned = dict(enumerate(turn(two), 1))
+    turned, early_one = lax.optimization_barrier((turned, early_one))
+    early_two = early_products(left, after(two, turned))
+    gate = one_in[0]
+    two_in = [shift(after(turned[k], gate), 1, k) for k in STEPS]
+    one_in = after(one_in, early_two)
 
     first = pairs[:, 0] - member * block_count
     dy = (my_y - pairs[:, 1] // SIDE) % SIDE
     dx = (my_x - pairs[:, 1] % SIDE) % SIDE
-    listed = jnp.stack([first, place(0, dx) * SIDE + dy, place(1, dy) * SIDE + dx])
-    listed = listed.reshape(3, SIDE, 2, -1)
+    leg0, leg1 = jnp.where(my_core == 0, dy, dx), jnp.where(my_core == 0, dx, dy)
+    place = sum(jnp.where(leg1 == k, at, 0) for at, k in enumerate(STEPS, 1))
+    listed = jnp.stack([first, place * SIDE + leg0])
+    listed = listed.reshape(2, SIDE, 2, -1)
     listed = jnp.concatenate([listed, listed], 1)
     listed = lax.dynamic_slice_in_dim(listed, my_z, SIDE, 1)
     listed = jnp.where(my_core == 0, listed, listed[:, :, ::-1])
-    listed = listed.transpose(0, 2, 1, 3).reshape(3, -1)
+    listed = listed.transpose(0, 2, 1, 3).reshape(2, -1)
 
     sums = []
-    for (_, rows), sides, got in zip(PARTS, parts, late_in):
-        flat = {key: got[key].reshape(-1, width) for key in early + late}
-        owns = [piece for f, _ in own for piece in sides[f]]
-        products = early_products(left, owns, [flat[key] for key in early])
-        rest = [flat[key] for key in late]
-        if sums:
-            *rest, _ = lax.optimization_barrier((*rest, sums[-1]))
-        keep, give = tiles(left, products, rest, rows, listed[0], listed[1] * rows, listed[2] * rows)
+    for (_, rows), early in zip(PARTS, (early_one, early_two)):
+        got = two_in if sums else one_in
+        rest = [v.reshape(-1, width) for v in got]
+        keep, give = tiles(left, early, rest, rows, listed[0], listed[1] * rows)
         mine, *sends = merge(keep, swap_cores(give))
+        if not sums:
+            sends, two_in = lax.optimization_barrier((sends, two_in))
         sums.append([mine] + [shift_z(s, k) for k, s in enumerate(sends, 1)])
     return finish(sums)
 

time: 312 us -> 229 us (0.73); the launches traced: 307 us -> 228 us
  waiting for transfers between devices: 153 us -> 92.5 us
  local copies, waits for them, and re-layouts: 19.3 us -> 12.7 us
  starting transfers between devices: 51.1 us -> 45.1 us
  Pallas kernels: 83.4 us -> 77.5 us
    ppermute x24 -> x12, waiting for transfers between devices: 147 us -> 83 us  [shift(): return lax.ppermute(array, ('ex', 'lay'), pairs)]
    pallas_call x2, Pallas kernels: 19.3 us -> 8.91 us  [early_products(): pl.pallas_call(functools.partial(early_kernel, len(owns)), out_shape=jax....]
    pallas_call x2, Pallas kernels: 14.6 us -> 22.3 us  [tiles(): pl.pallas_call(functools.partial(tiles_kernel, len(rights)), out_shape=(o...]
    unnamed x50 -> x28, local copies, waits for them, and re-layouts: 17.5 us -> 10.7 us
    ppermute x24 -> x12, starting transfers between devices: 38.1 us -> 33.8 us  [shift(): return lax.ppermute(array, ('ex', 'lay'), pairs)]
    ppermute x6, waiting for transfers between devices: 4.09 us -> 7.29 us  [shift_z(): return lax.ppermute(array, 'lay', pairs)]
    pallas_call x4 -> x2, Pallas kernels: 13.5 us -> 11 us  [turn(): pl.pallas_call(turn_kernel, out_shape=outs, in_specs=[pl.BlockSpec(memory...]
    pallas_call x3 -> x4, Pallas kernels: 18 us -> 18.2 us  [gather(): pl.pallas_call(functools.partial(gather_kernel, [start for _, start, _ in...]
  transfers between devices with their start and end apart: 32 -> 20, of which waited for: 14 -> 9; matrix products, arithmetic and copies ran while one was open for 0% -> 0% of each run, Pallas kernels for 19% -> 27%
where the time goes in v5:
time: 229 us; the launch traced here: 228 us
  waiting for transfers between devices  92.5 us (40%)
  Pallas kernels  77.5 us (34%)
  starting transfers between devices  45.1 us (20%)
  local copies, waits for them, and re-layouts  12.7 us (6%)
    ppermute x12, waiting for transfers between devices, shift(): return lax.ppermute(array, ('ex', 'lay'), pairs)  83 us
    ppermute x12, starting transfers between devices, shift(): return lax.ppermute(array, ('ex', 'lay'), pairs)  33.8 us
    pallas_call x2, Pallas kernels, tiles(): pl.pallas_call(functools.partial(tiles_kernel, len(rights)), out_shape=(o...  22.3 us
    pallas_call x4, Pallas kernels, gather(): pl.pallas_call(functools.partial(gather_kernel, [start for _, start, _ in...  18.2 us
    pallas_call x1, Pallas kernels, left_transposed(): pl.pallas_call(left_kernel, out_shape=jax.ShapeDtypeStruct((examples // t...  16 us
    pallas_call x2, Pallas kernels, turn(): pl.pallas_call(turn_kernel, out_shape=outs, in_specs=[pl.BlockSpec(memory...  11 us
    unnamed x28, local copies, waits for them, and re-layouts  10.7 us
    ppermute x6, starting transfers between devices, shift_z(): return lax.ppermute(array, 'lay', pairs)  10.4 us
  transfers between devices with their start and end apart: 20, of which 9 were waited for; matrix products, arithmetic and copies ran while one was open for 0% of the time, Pallas kernels for 27%

profile of v5, /device:TPU:0, one launch (start us, length us, event | category | flops | bytes accessed | tf_op | source)
XLA Modules:
  0.0 228.4 jit_solution(6018724006004413427)
XLA Ops:
  0.0 0.7 copy-done
  0.7 0.2 dynamic-slice_reduce_fusion
  0.9 0.1 reshape.249
  1.0 0.1 add_add_fusion
  1.0 0.1 dynamic_slice.12
  1.1 0.1 copy.17
  1.2 0.1 bitcast_select_fusion
  1.3 0.6 slice_bitcast_fusion
  1.9 3.1 %shard_map.57 = bf16[4,64,4096]{2,1,0:T(8,128)(2,1)} custom-call(s32[4]{0:T(128)} %get-tuple-element.117.index_ref, bf16[8,128,4096]{2,1,0:T(8,128)(2,1)} %bitcast.24), custom_call_target="tpu_custom_call" | custom-call | flops 1 | bytes 1 | tf_op jit(solution)/shard_map/pallas_call | solution.py:63
  5.0 1.7 collective-permute-start
  6.7 3.2 %shard_map.58 = bf16[4,64,4096]{2,1,0:T(8,128)(2,1)} custom-call(s32[4]{0:T(128)} %get-tuple-element.116.index_ref, bf16[8,128,4096]{2,1,0:T(8,128)(2,1)} %bitcast.25), custom_call_target="tpu_custom_call" | custom-call | flops 1 | bytes 1 | tf_op jit(solution)/shard_map/pallas_call | solution.py:63
  9.9 3.0 %collective-permute-start.4 = (bf16[4,64,4096]{2,1,0:T(8,128)(2,1)}, bf16[4,64,4096]{2,1,0:T(8,128)(2,1)}, u32[]{:S(2)}, u32[]{:S(2)}) collective-permute-start(bf16[4,64,4096]{2,1,0:T(8,128)(2,1)} %shard_map.58), channel_id=1, source_target_pairs={{0,64},{1,17},{2,66},{3,19},{4,68},{5,21},{6,70},{7,23},{8,72},{9,... | collective-permute-start | bytes 6291464 | tf_op jit(solution)/shard_map/ppermute | solution.py:323
  12.9 3.3 %shard_map.59 = bf16[4,64,4096]{2,1,0:T(8,128)(2,1)} custom-call(s32[4]{0:T(128)} %get-tuple-element.115.index_ref, bf16[8,128,4096]{2,1,0:T(8,128)(2,1)} %bitcast.26), custom_call_target="tpu_custom_call" | custom-call | flops 1 | bytes 1 | tf_op jit(solution)/shard_map/pallas_call | solution.py:63
  16.2 1.8 collective-permute-start.5
  18.0 0.6 concatenate.16.index_ref
  18.6 8.6 %shard_map.55 = (bf16[4,64,4096]{2,1,0:T(8,128)(2,1)}, bf16[4,64,4096]{2,1,0:T(8,128)(2,1)}, bf16[4,64,4096]{2,1,0:T(8,128)(2,1)}, bf16[4,64,4096]{2,1,0:T(8,128)(2,1)}, bf16[4,64,4096]{2,1,0:T(8,128)(2,1)}) custom-call(s32[20]{0:T(128)} %concatenate.16.index_ref, bf16[8,128,4096]{2,1,0:T(8,128)(2,1)} %bitcast.27), custom_call_target="tpu_custom_call" | custom-call | flops 1 | bytes 1 | tf_op jit(solution)/shard_map/pallas_call | solution.py:63
  27.2 16.0 %shard_map.56.left_ref = bf16[4,4096,256]{2,1,0:T(8,128)(2,1)} custom-call(bf16[1024,4096]{1,0:T(8,128)(2,1)} %bitcast.28, bf16[64,64]{1,0:T(8,128)(2,1)} %bitcast.29, bf16[64,64]{1,0:T(8,128)(2,1)} %bitcast.30), custom_call_target="tpu_custom_call" | custom-call | flops 1 | bytes 1 | tf_op jit(solution)/shard_map/pallas_call | solution.py:162
  43.2 11.8 %collective-permute-start.1 = (bf16[4,64,4096]{2,1,0:T(8,128)(2,1)}, bf16[4,64,4096]{2,1,0:T(8,128)(2,1)S(1)}, u32[]{:S(2)}, u32[]{:S(2)}) collective-permute-start(bf16[4,64,4096]{2,1,0:T(8,128)(2,1)} %get-tuple-element.64), channel_id=1, source_target_pairs={{0,32},{1,9},{2,34},{3,11},{4,36},{5,13},{6,38},{7,15},{8,40},{9,1... | collective-permute-start | bytes 6291464 | tf_op jit(solution)/shard_map/ppermute | solution.py:323
  55.1 2.5 %collective-permute-start.2 = (bf16[4,64,4096]{2,1,0:T(8,128)(2,1)}, bf16[4,64,4096]{2,1,0:T(8,128)(2,1)}, u32[]{:S(2)}, u32[]{:S(2)}) collective-permute-start(bf16[4,64,4096]{2,1,0:T(8,128)(2,1)} %get-tuple-element.65), channel_id=1, source_target_pairs={{0,64},{1,17},{2,66},{3,19},{4,68},{5,21},{6,70},{7,23},{8,72},{9,... | collective-permute-start | bytes 6291464 | tf_op jit(solution)/shard_map/ppermute | solution.py:323
  57.6 2.6 %collective-permute-start.3 = (bf16[4,64,4096]{2,1,0:T(8,128)(2,1)}, bf16[4,64,4096]{2,1,0:T(8,128)(2,1)}, u32[]{:S(2)}, u32[]{:S(2)}) collective-permute-start(bf16[4,64,4096]{2,1,0:T(8,128)(2,1)} %get-tuple-element.66), channel_id=1, source_target_pairs={{0,96},{1,25},{2,98},{3,27},{4,100},{5,29},{6,102},{7,31},{8,104},... | collective-permute-start | bytes 6291464 | tf_op jit(solution)/shard_map/ppermute | solution.py:323
  60.2 0.0 collective-permute-done.4.refs_2_
  60.2 5.5 %shard_map.60 = (bf16[4,64,4096]{2,1,0:T(8,128)(2,1)}, bf16[4,64,4096]{2,1,0:T(8,128)(2,1)}, bf16[4,64,4096]{2,1,0:T(8,128)(2,1)}) custom-call(bf16[4,64,4096]{2,1,0:T(8,128)(2,1)} %get-tuple-element.67.refs_0_, bf16[4,64,4096]{2,1,0:T(8,128)(2,1)} %collective-permute-done.refs_1_, bf16[4,64,4096]{2,1,0:T(8,128)(2,1)} %collective-permute-done.4.refs_2_, ...), custom_call_target="tpu_custom_call" | custom-call | flops 1 | bytes 1 | tf_op jit(solution)/shard_map/pallas_call | solution.py:89
  65.7 1.2 collective-permute-start.6
  66.9 2.1 collective-permute-start.7
  69.0 23.0 %collective-permute-done.1.refs_1_ = bf16[4,64,4096]{2,1,0:T(8,128)(2,1)S(1)} collective-permute-done((bf16[4,64,4096]{2,1,0:T(8,128)(2,1)}, bf16[4,64,4096]{2,1,0:T(8,128)(2,1)S(1)}, u32[]{:S(2)}, u32[]{:S(2)}) %collective-permute-start.1) | collective-permute-done | bytes 2097184 | tf_op jit(solution)/shard_map/ppermute | solution.py:323
  92.0 1.4 collective-permute-start.8
  93.4 3.4 %copy-done.2 = bf16[4,4096,256]{2,1,0:T(8,128)(2,1)S(1)} copy-done((bf16[4,4096,256]{2,1,0:T(8,128)(2,1)S(1)}, bf16[4,4096,256]{2,1,0:T(8,128)(2,1)}, u32[]{:S(2)}) %copy-start.2) | copy-done | bytes 8388632
  96.8 1.6 copy-done.7
  98.4 4.5 %shard_map.61.early_ref = f32[8,256,128]{2,1,0:T(8,128)S(1)} custom-call(bf16[4,4096,256]{2,1,0:T(8,128)(2,1)S(1)} %copy-done.2, bf16[4,64,4096]{2,1,0:T(8,128)(2,1)S(1)} %copy-done.7, bf16[4,64,4096]{2,1,0:T(8,128)(2,1)} %collective-permute-done.refs_1_, bf16[4,64,4096]{2,1,0:T(8,128)(2,1)} %collective-permute-done.4.refs_2_, ...), custom_call_target="tpu_custom_call" | custom-call | flops 1 | bytes 1 | tf_op jit(solution)/shard_map/pallas_call | solution.py:208
  102.9 0.0 copy-start.11
  103.0 35.8 %collective-permute-done.2.refs_2_ = bf16[4,64,4096]{2,1,0:T(8,128)(2,1)} collective-permute-done((bf16[4,64,4096]{2,1,0:T(8,128)(2,1)}, bf16[4,64,4096]{2,1,0:T(8,128)(2,1)}, u32[]{:S(2)}, u32[]{:S(2)}) %collective-permute-start.2) | collective-permute-done | bytes 2097184 | tf_op jit(solution)/shard_map/ppermute | solution.py:323
  138.8 1.9 collective-permute-done.3.refs_3_
  140.6 5.5 %shard_map.62 = (bf16[4,64,4096]{2,1,0:T(8,128)(2,1)}, bf16[4,64,4096]{2,1,0:T(8,128)(2,1)}, bf16[4,64,4096]{2,1,0:T(8,128)(2,1)}) custom-call(bf16[4,64,4096]{2,1,0:T(8,128)(2,1)} %get-tuple-element.83.refs_0_, bf16[4,64,4096]{2,1,0:T(8,128)(2,1)} %copy-done.5, bf16[4,64,4096]{2,1,0:T(8,128)(2,1)} %collective-permute-done.2.refs_2_, ...), custom_call_target="tpu_custom_call" | custom-call | flops 1 | bytes 1 | tf_op jit(solution)/shard_map/pallas_call | solution.py:89
  146.1 0.5 collective-permute-start.10
  146.7 3.6 %collective-permute-start.11 = (bf16[4,64,4096]{2,1,0:T(8,128)(2,1)}, bf16[4,64,4096]{2,1,0:T(8,128)(2,1)}, u32[]{:S(2)}, u32[]{:S(2)}) collective-permute-start(bf16[4,64,4096]{2,1,0:T(8,128)(2,1)} %get-tuple-element.97), channel_id=1, source_target_pairs={{0,24},{1,97},{2,26},{3,99},{4,28},{5,101},{6,30},{7,103},{8,0},{9... | collective-permute-start | bytes 6291464 | tf_op jit(solution)/shard_map/ppermute | solution.py:323
  150.3 1.5 collective-permute-start.12
  151.8 0.1 sub.60
  151.9 0.1 squeeze.38
  152.0 0.1 squeeze.39.block_ref
  152.1 0.1 mul.24.row_ref
  152.2 3.4 %copy-done.3 = bf16[4,4096,256]{2,1,0:T(8,128)(2,1)S(1)} copy-done((bf16[4,4096,256]{2,1,0:T(8,128)(2,1)S(1)}, bf16[4,4096,256]{2,1,0:T(8,128)(2,1)}, u32[]{:S(2)}) %copy-start.3) | copy-done | bytes 8388632
  155.6 1.6 copy-done.6
  157.2 4.4 %shard_map.63.early_ref = f32[8,256,128]{2,1,0:T(8,128)S(1)} custom-call(bf16[4,4096,256]{2,1,0:T(8,128)(2,1)S(1)} %copy-done.3, bf16[4,64,4096]{2,1,0:T(8,128)(2,1)S(1)} %copy-done.4, bf16[4,64,4096]{2,1,0:T(8,128)(2,1)S(1)} %copy-done.6, bf16[4,64,4096]{2,1,0:T(8,128)(2,1)} %collective-permute-done.2.refs_2_, ...), custom_call_target="tpu_custom_call" | custom-call | flops 1 | bytes 1 | tf_op jit(solution)/shard_map/pallas_call | solution.py:208
  161.6 0.0 collective-permute-done.8
  161.6 0.0 slice-start
  161.6 11.3 %shard_map.64 = (f32[32,64,128]{2,1,0:T(8,128)S(1)}, f32[32,64,128]{2,1,0:T(8,128)S(1)}) custom-call(s32[64]{0:T(128)S(1)} %squeeze.39.block_ref, s32[64]{0:T(128)S(1)} %mul.24.row_ref, bf16[4,4096,256]{2,1,0:T(8,128)(2,1)S(1)} %copy-done.3, f32[8,256,128]{2,1,0:T(8,128)S(1)} %shard_map.61.early_ref, bf16[256,4096]{1,0:T(8,128)(2,1)} %bitcast.10.refs_0_, ...), custom_call_target="tpu_custom_call" | custom-call | flops 1 | bytes 1 | tf_op jit(solution)/shard_map/pallas_call | solution.py:255
  172.9 0.8 collective-permute-start.9
  173.8 2.3 %collective-permute-done.9.got_ref = f32[32,64,128]{2,1,0:T(8,128)S(1)} collective-permute-done((f32[32,64,128]{2,1,0:T(8,128)S(1)}, f32[32,64,128]{2,1,0:T(8,128)S(1)}, u32[]{:S(2)}, u32[]{:S(2)}) %collective-permute-start.9) | collective-permute-done | bytes 1048608 | tf_op jit(solution)/shard_map/ppermute | solution.py:327
  176.0 0.1 shard_map.65
  176.2 20.5 %collective-permute-done.11 = bf16[4,64,4096]{2,1,0:T(8,128)(2,1)} collective-permute-done((bf16[4,64,4096]{2,1,0:T(8,128)(2,1)}, bf16[4,64,4096]{2,1,0:T(8,128)(2,1)}, u32[]{:S(2)}, u32[]{:S(2)}) %collective-permute-start.11) | collective-permute-done | bytes 2097184 | tf_op jit(solution)/shard_map/ppermute | solution.py:323
  196.6 1.8 collective-permute-done.12
  198.5 11.0 %shard_map.66 = (f32[32,64,128]{2,1,0:T(8,128)S(1)}, f32[32,64,128]{2,1,0:T(8,128)S(1)}) custom-call(s32[64]{0:T(128)S(1)} %squeeze.39.block_ref, s32[64]{0:T(128)S(1)} %mul.24.row_ref, bf16[4,4096,256]{2,1,0:T(8,128)(2,1)S(1)} %bitcast.23, f32[8,256,128]{2,1,0:T(8,128)S(1)} %shard_map.63.early_ref, bf16[256,4096]{1,0:T(8,128)(2,1)} %bitcast.13.refs_0_, ...), custom_call_target="tpu_custom_call" | custom-call | flops 1 | bytes 1 | tf_op jit(solution)/shard_map/pallas_call | solution.py:255
  209.4 0.1 collective-permute-start.16
  209.5 2.0 collective-permute-start.13
  211.5 3.6 %collective-permute-start.14 = (bf16[8,64,128]{2,1,0:T(8,128)(2,1)S(1)}, bf16[8,64,128]{2,1,0:T(8,128)(2,1)S(1)}, u32[]{:S(2)}, u32[]{:S(2)}) collective-permute-start(bf16[8,64,128]{2,1,0:T(8,128)(2,1)S(1)} %get-tuple-element.100), channel_id=1, source_target_pairs={{0,4},{1,5},{2,6},{3,7},{4,0},{5,1},{6,2},{7,3},{8,12},{9,13},{10,... | collective-permute-start | bytes 393224 | tf_op jit(solution)/shard_map/ppermute | solution.py:332
  215.1 1.0 collective-permute-start.15
  216.1 0.1 shard_map.67
  216.2 1.1 collective-permute-start.17
  217.3 0.5 collective-permute-start.18
  217.9 2.2 collective-permute-start.19
  220.1 2.1 collective-permute-done.14.refs_2_
  222.2 2.8 %collective-permute-done.17.refs_5_ = bf16[8,64,128]{2,1,0:T(8,128)(2,1)S(1)} collective-permute-done((bf16[8,64,128]{2,1,0:T(8,128)(2,1)S(1)}, bf16[8,64,128]{2,1,0:T(8,128)(2,1)S(1)}, u32[]{:S(2)}, u32[]{:S(2)}) %collective-permute-start.17) | collective-permute-done | bytes 131104 | tf_op jit(solution)/shard_map/ppermute | solution.py:332
  225.0 2.4 %collective-permute-done.18.refs_6_ = bf16[8,64,128]{2,1,0:T(8,128)(2,1)S(1)} collective-permute-done((bf16[8,64,128]{2,1,0:T(8,128)(2,1)S(1)}, bf16[8,64,128]{2,1,0:T(8,128)(2,1)S(1)}, u32[]{:S(2)}, u32[]{:S(2)}) %collective-permute-start.18) | collective-permute-done | bytes 131104 | tf_op jit(solution)/shard_map/ppermute | solution.py:332
  227.4 1.0 shard_map.68
  (37 shorter events, 0.2 us)
Async XLA Ops:
  0.0 0.7 copy-start
  5.0 38.2 %collective-permute-start = (bf16[4,64,4096]{2,1,0:T(8,128)(2,1)}, bf16[4,64,4096]{2,1,0:T(8,128)(2,1)}, u32[]{:S(2)}, u32[]{:S(2)}) collective-permute-start(bf16[4,64,4096]{2,1,0:T(8,128)(2,1)} %shard_map.57), channel_id=1, source_target_pairs={{0,32},{1,9},{2,34},{3,11},{4,36},{5,13},{6,38},{7,15},{8,40},{9,1... | collective-permute-start | bytes 6291464 | tf_op jit(solution)/shard_map/ppermute | solution.py:323
  9.9 50.3 %collective-permute-start.4 = (bf16[4,64,4096]{2,1,0:T(8,128)(2,1)}, bf16[4,64,4096]{2,1,0:T(8,128)(2,1)}, u32[]{:S(2)}, u32[]{:S(2)}) collective-permute-start(bf16[4,64,4096]{2,1,0:T(8,128)(2,1)} %shard_map.58), channel_id=1, source_target_pairs={{0,64},{1,17},{2,66},{3,19},{4,68},{5,21},{6,70},{7,23},{8,72},{9,... | collective-permute-start | bytes 6291464 | tf_op jit(solution)/shard_map/ppermute | solution.py:323
  12.9 5.1 %copy-start.8 = (s32[4]{0:T(128)S(1)}, s32[4]{0:T(128)}, u32[]{:S(2)}) copy-start(s32[4]{0:T(128)} %get-tuple-element.115.index_ref) | copy-start | bytes 52
  12.9 5.1 %copy-start.9 = (s32[4]{0:T(128)S(1)}, s32[4]{0:T(128)}, u32[]{:S(2)}) copy-start(s32[4]{0:T(128)} %get-tuple-element.116.index_ref) | copy-start | bytes 52
  12.9 5.1 %copy-start.10 = (s32[4]{0:T(128)S(1)}, s32[4]{0:T(128)}, u32[]{:S(2)}) copy-start(s32[4]{0:T(128)} %get-tuple-element.117.index_ref) | copy-start | bytes 52
  16.2 44.0 %collective-permute-start.5 = (bf16[4,64,4096]{2,1,0:T(8,128)(2,1)}, bf16[4,64,4096]{2,1,0:T(8,128)(2,1)}, u32[]{:S(2)}, u32[]{:S(2)}) collective-permute-start(bf16[4,64,4096]{2,1,0:T(8,128)(2,1)} %shard_map.59), channel_id=1, source_target_pairs={{0,96},{1,25},{2,98},{3,27},{4,100},{5,29},{6,102},{7,31},{8,104},... | collective-permute-start | bytes 6291464 | tf_op jit(solution)/shard_map/ppermute | solution.py:323
  43.2 48.8 %collective-permute-start.1 = (bf16[4,64,4096]{2,1,0:T(8,128)(2,1)}, bf16[4,64,4096]{2,1,0:T(8,128)(2,1)S(1)}, u32[]{:S(2)}, u32[]{:S(2)}) collective-permute-start(bf16[4,64,4096]{2,1,0:T(8,128)(2,1)} %get-tuple-element.64), channel_id=1, source_target_pairs={{0,32},{1,9},{2,34},{3,11},{4,36},{5,13},{6,38},{7,15},{8,40},{9,1... | collective-permute-start | bytes 6291464 | tf_op jit(solution)/shard_map/ppermute | solution.py:323
  55.1 83.7 %collective-permute-start.2 = (bf16[4,64,4096]{2,1,0:T(8,128)(2,1)}, bf16[4,64,4096]{2,1,0:T(8,128)(2,1)}, u32[]{:S(2)}, u32[]{:S(2)}) collective-permute-start(bf16[4,64,4096]{2,1,0:T(8,128)(2,1)} %get-tuple-element.65), channel_id=1, source_target_pairs={{0,64},{1,17},{2,66},{3,19},{4,68},{5,21},{6,70},{7,23},{8,72},{9,... | collective-permute-start | bytes 6291464 | tf_op jit(solution)/shard_map/ppermute | solution.py:323
  57.6 83.1 %collective-permute-start.3 = (bf16[4,64,4096]{2,1,0:T(8,128)(2,1)}, bf16[4,64,4096]{2,1,0:T(8,128)(2,1)}, u32[]{:S(2)}, u32[]{:S(2)}) collective-permute-start(bf16[4,64,4096]{2,1,0:T(8,128)(2,1)} %get-tuple-element.66), channel_id=1, source_target_pairs={{0,96},{1,25},{2,98},{3,27},{4,100},{5,29},{6,102},{7,31},{8,104},... | collective-permute-start | bytes 6291464 | tf_op jit(solution)/shard_map/ppermute | solution.py:323
  65.7 80.4 %collective-permute-start.6 = (bf16[4,64,4096]{2,1,0:T(8,128)(2,1)}, bf16[4,64,4096]{2,1,0:T(8,128)(2,1)}, u32[]{:S(2)}, u32[]{:S(2)}) collective-permute-start(bf16[4,64,4096]{2,1,0:T(8,128)(2,1)} %get-tuple-element.68), channel_id=1, source_target_pairs={{0,8},{1,33},{2,10},{3,35},{4,12},{5,37},{6,14},{7,39},{8,16},{9,4... | collective-permute-start | bytes 6291464 | tf_op jit(solution)/shard_map/ppermute | solution.py:323
  66.9 94.7 %collective-permute-start.7 = (bf16[4,64,4096]{2,1,0:T(8,128)(2,1)}, bf16[4,64,4096]{2,1,0:T(8,128)(2,1)}, u32[]{:S(2)}, u32[]{:S(2)}) collective-permute-start(bf16[4,64,4096]{2,1,0:T(8,128)(2,1)} %get-tuple-element.70), channel_id=1, source_target_pairs={{0,24},{1,97},{2,26},{3,99},{4,28},{5,101},{6,30},{7,103},{8,0},{9... | collective-permute-start | bytes 6291464 | tf_op jit(solution)/shard_map/ppermute | solution.py:323
  92.0 1.4 copy-start.5
  92.0 69.6 %collective-permute-start.8 = (bf16[4,64,4096]{2,1,0:T(8,128)(2,1)}, bf16[4,64,4096]{2,1,0:T(8,128)(2,1)}, u32[]{:S(2)}, u32[]{:S(2)}) collective-permute-start(bf16[4,64,4096]{2,1,0:T(8,128)(2,1)} %get-tuple-element.69), channel_id=1, source_target_pairs={{0,16},{1,65},{2,18},{3,67},{4,20},{5,69},{6,22},{7,71},{8,24},{9,... | collective-permute-start | bytes 6291464 | tf_op jit(solution)/shard_map/ppermute | solution.py:323
  93.4 3.4 %copy-start.2 = (bf16[4,4096,256]{2,1,0:T(8,128)(2,1)S(1)}, bf16[4,4096,256]{2,1,0:T(8,128)(2,1)}, u32[]{:S(2)}) copy-start(bf16[4,4096,256]{2,1,0:T(8,128)(2,1)} %shard_map.56.left_ref) | copy-start | bytes 25165828
  96.8 1.6 copy-start.7
  102.9 48.8 %copy-start.11 = (s32[64,2]{0,1:T(2,128)S(1)}, s32[64,2]{0,1:T(2,128)}, u32[]{:S(2)}) copy-start(s32[64,2]{0,1:T(2,128)} %param.9) | copy-start | bytes 1540
  103.0 49.3 %copy-start.4 = (bf16[4,64,4096]{2,1,0:T(8,128)(2,1)S(1)}, bf16[4,64,4096]{2,1,0:T(8,128)(2,1)}, u32[]{:S(2)}) copy-start(bf16[4,64,4096]{2,1,0:T(8,128)(2,1)} %get-tuple-element.83.refs_0_) | copy-start | bytes 6291460
  146.1 30.0 %collective-permute-start.10 = (bf16[4,64,4096]{2,1,0:T(8,128)(2,1)}, bf16[4,64,4096]{2,1,0:T(8,128)(2,1)}, u32[]{:S(2)}, u32[]{:S(2)}) collective-permute-start(bf16[4,64,4096]{2,1,0:T(8,128)(2,1)} %get-tuple-element.96), channel_id=1, source_target_pairs={{0,8},{1,33},{2,10},{3,35},{4,12},{5,37},{6,14},{7,39},{8,16},{9,4... | collective-permute-start | bytes 6291464 | tf_op jit(solution)/shard_map/ppermute | solution.py:323
  146.7 50.0 %collective-permute-start.11 = (bf16[4,64,4096]{2,1,0:T(8,128)(2,1)}, bf16[4,64,4096]{2,1,0:T(8,128)(2,1)}, u32[]{:S(2)}, u32[]{:S(2)}) collective-permute-start(bf16[4,64,4096]{2,1,0:T(8,128)(2,1)} %get-tuple-element.97), channel_id=1, source_target_pairs={{0,24},{1,97},{2,26},{3,99},{4,28},{5,101},{6,30},{7,103},{8,0},{9... | collective-permute-start | bytes 6291464 | tf_op jit(solution)/shard_map/ppermute | solution.py:323
  150.3 48.2 %collective-permute-start.12 = (bf16[4,64,4096]{2,1,0:T(8,128)(2,1)}, bf16[4,64,4096]{2,1,0:T(8,128)(2,1)}, u32[]{:S(2)}, u32[]{:S(2)}) collective-permute-start(bf16[4,64,4096]{2,1,0:T(8,128)(2,1)} %get-tuple-element.98), channel_id=1, source_target_pairs={{0,16},{1,65},{2,18},{3,67},{4,20},{5,69},{6,22},{7,71},{8,24},{9,... | collective-permute-start | bytes 6291464 | tf_op jit(solution)/shard_map/ppermute | solution.py:323
  152.2 3.4 %copy-start.3 = (bf16[4,4096,256]{2,1,0:T(8,128)(2,1)S(1)}, bf16[4,4096,256]{2,1,0:T(8,128)(2,1)}, u32[]{:S(2)}) copy-start(bf16[4,4096,256]{2,1,0:T(8,128)(2,1)} %shard_map.56.left_ref) | copy-start | bytes 25165828
  155.6 1.6 copy-start.6
  161.6 36.8 %slice-start = ((s8[8388608]{0:T(1024)(128)(4,1)}), s8[4194304]{0:T(1024)(128)(4,1)S(1)}, s32[]{:S(2)}) async-start(s8[8388608]{0:T(1024)(128)(4,1)} %bitcast.22), calls=%async_computation | async-start | bytes 8388608
  161.6 36.8 %slice-start.1 = ((s8[8388608]{0:T(1024)(128)(4,1)}), s8[4194304]{0:T(1024)(128)(4,1)S(1)}, s32[]{:S(2)}) async-start(s8[8388608]{0:T(1024)(128)(4,1)} %bitcast.22), calls=%async_computation.1 | async-start | bytes 8388608
  172.9 3.1 %collective-permute-start.9 = (f32[32,64,128]{2,1,0:T(8,128)S(1)}, f32[32,64,128]{2,1,0:T(8,128)S(1)}, u32[]{:S(2)}, u32[]{:S(2)}) collective-permute-start(f32[32,64,128]{2,1,0:T(8,128)S(1)} %get-tuple-element.91), channel_id=1, source_target_pairs={{0,1},{1,0},{2,3},{3,2},{4,5},{5,4},{6,7},{7,6},{8,9},{9,8},{10,11... | collective-permute-start | bytes 3145736 | tf_op jit(solution)/shard_map/ppermute | solution.py:327
  198.4 29.9 %copy-start.1 = (s32[16,16]{1,0:T(8,128)S(1)}, s32[16,16]{1,0:T(8,128)}, u32[]{:S(2)}) copy-start(s32[16,16]{1,0:T(8,128)} %param.8) | copy-start | bytes 3076
  209.4 6.7 %collective-permute-start.16 = (f32[32,64,128]{2,1,0:T(8,128)S(1)}, f32[32,64,128]{2,1,0:T(8,128)S(1)}, u32[]{:S(2)}, u32[]{:S(2)}) collective-permute-start(f32[32,64,128]{2,1,0:T(8,128)S(1)} %get-tuple-element.106), channel_id=1, source_target_pairs={{0,1},{1,0},{2,3},{3,2},{4,5},{5,4},{6,7},{7,6},{8,9},{9,8},{10,11... | collective-permute-start | bytes 3145736 | tf_op jit(solution)/shard_map/ppermute | solution.py:327
  209.5 8.3 %collective-permute-start.13 = (bf16[8,64,128]{2,1,0:T(8,128)(2,1)S(1)}, bf16[8,64,128]{2,1,0:T(8,128)(2,1)S(1)}, u32[]{:S(2)}, u32[]{:S(2)}) collective-permute-start(bf16[8,64,128]{2,1,0:T(8,128)(2,1)S(1)} %get-tuple-element.99), channel_id=1, source_target_pairs={{0,2},{1,3},{2,4},{3,5},{4,6},{5,7},{6,0},{7,1},{8,10},{9,11},{10,... | collective-permute-start | bytes 393224 | tf_op jit(solution)/shard_map/ppermute | solution.py:332
  211.5 10.7 %collective-permute-start.14 = (bf16[8,64,128]{2,1,0:T(8,128)(2,1)S(1)}, bf16[8,64,128]{2,1,0:T(8,128)(2,1)S(1)}, u32[]{:S(2)}, u32[]{:S(2)}) collective-permute-start(bf16[8,64,128]{2,1,0:T(8,128)(2,1)S(1)} %get-tuple-element.100), channel_id=1, source_target_pairs={{0,4},{1,5},{2,6},{3,7},{4,0},{5,1},{6,2},{7,3},{8,12},{9,13},{10,... | collective-permute-start | bytes 393224 | tf_op jit(solution)/shard_map/ppermute | solution.py:332
  215.1 7.1 %collective-permute-start.15 = (bf16[8,64,128]{2,1,0:T(8,128)(2,1)S(1)}, bf16[8,64,128]{2,1,0:T(8,128)(2,1)S(1)}, u32[]{:S(2)}, u32[]{:S(2)}) collective-permute-start(bf16[8,64,128]{2,1,0:T(8,128)(2,1)S(1)} %get-tuple-element.101), channel_id=1, source_target_pairs={{0,6},{1,7},{2,0},{3,1},{4,2},{5,3},{6,4},{7,5},{8,14},{9,15},{10,... | collective-permute-start | bytes 393224 | tf_op jit(solution)/shard_map/ppermute | solution.py:332
  216.2 8.8 %collective-permute-start.17 = (bf16[8,64,128]{2,1,0:T(8,128)(2,1)S(1)}, bf16[8,64,128]{2,1,0:T(8,128)(2,1)S(1)}, u32[]{:S(2)}, u32[]{:S(2)}) collective-permute-start(bf16[8,64,128]{2,1,0:T(8,128)(2,1)S(1)} %get-tuple-element.108), channel_id=1, source_target_pairs={{0,2},{1,3},{2,4},{3,5},{4,6},{5,7},{6,0},{7,1},{8,10},{9,11},{10,... | collective-permute-start | bytes 393224 | tf_op jit(solution)/shard_map/ppermute | solution.py:332
  217.3 10.1 %collective-permute-start.18 = (bf16[8,64,128]{2,1,0:T(8,128)(2,1)S(1)}, bf16[8,64,128]{2,1,0:T(8,128)(2,1)S(1)}, u32[]{:S(2)}, u32[]{:S(2)}) collective-permute-start(bf16[8,64,128]{2,1,0:T(8,128)(2,1)S(1)} %get-tuple-element.109), channel_id=1, source_target_pairs={{0,4},{1,5},{2,6},{3,7},{4,0},{5,1},{6,2},{7,3},{8,12},{9,13},{10,... | collective-permute-start | bytes 393224 | tf_op jit(solution)/shard_map/ppermute | solution.py:332
  217.9 9.5 %collective-permute-start.19 = (bf16[8,64,128]{2,1,0:T(8,128)(2,1)S(1)}, bf16[8,64,128]{2,1,0:T(8,128)(2,1)S(1)}, u32[]{:S(2)}, u32[]{:S(2)}) collective-permute-start(bf16[8,64,128]{2,1,0:T(8,128)(2,1)S(1)} %get-tuple-element.110), channel_id=1, source_target_pairs={{0,6},{1,7},{2,0},{3,1},{4,2},{5,3},{6,4},{7,5},{8,14},{9,15},{10,... | collective-permute-start | bytes 393224 | tf_op jit(solution)/shard_map/ppermute | solution.py:332

commit v6 on v5

--- a/solution.py
+++ b/solution.py
@@ -175,30 +175,37 @@
     )(grads, prec_in, prec_out)
 
 
-def fetch(rights, right_ref, sems):
-    copies, at = [], 0
-    for k, ref in enumerate(rights):
-        rows = ref.shape[0]
-        copies.append(pltpu.make_async_copy(ref, right_ref.at[pl.ds(at, rows)], sems.at[k]))
-        at += rows
-    run_copies(copies)
-
-
-def multiply(right_ref, left_ref, product_ref, first_block, at):
-    rows = right_ref.shape[0]
-    product = jnp.dot(right_ref[...], left_ref[0], preferred_element_type=f32)
+def multiply(right, left_ref, product_ref, first_block, at):
+    product = jnp.dot(right, left_ref[0], preferred_element_type=f32)
     for b in range(left_ref.shape[2] // BLOCK):
-        product_ref[first_block + b, at : at + rows, :] = product[:, b * BLOCK : (b + 1) * BLOCK]
+        columns = product[:, b * BLOCK : (b + 1) * BLOCK]
+        product_ref[first_block + b, at : at + right.shape[0], :] = columns
+
+
+def multiply_pieces(pieces, right_ref, sems, left_ref, product_ref, first_block, at):
+    step = pl.program_id(0)
+
+    @pl.when(step == 0)
+    def _():
+        copies, row = [], 0
+        for k, ref in enumerate(pieces):
+            slot = right_ref.at[pl.ds(row, ref.shape[0])]
+            copies.append((pltpu.make_async_copy(ref, slot, sems.at[k]), row, ref.shape[0]))
+            row += ref.shape[0]
+        for copy, _, _ in copies:
+            copy.start()
+        for copy, row, rows in copies:
+            copy.wait()
+            multiply(right_ref[row : row + rows, :], left_ref, product_ref, first_block, at + row)
+
+    @pl.when(step > 0)
+    def _():
+        multiply(right_ref[...], left_ref, product_ref, first_block, at)
 
 
 def early_kernel(count, left_ref, *refs):
     owns, (out_ref, right_ref, sems) = refs[:count], refs[count:]
-
-    @pl.when(pl.program_id(0) == 0)
-    def _():
-        fetch([ref.at[0] for ref in owns], right_ref, sems)
-
-    multiply(right_ref, left_ref, out_ref, 0, 0)
+    multiply_pieces([ref.at[0] for ref in owns], right_ref, sems, left_ref, out_ref, 0, 0)
 
 
 def early_products(left, owns):
@@ -231,9 +238,9 @@
     @pl.when(step == 0)
     def _():
         early_copy.start()
-        fetch(rights, right_ref, sems)
-
-    multiply(right_ref, left_ref, product_ref, step * (left_ref.shape[2] // BLOCK), early)
+
+    block = step * (left_ref.shape[2] // BLOCK)
+    multiply_pieces(rights, right_ref, sems, left_ref, product_ref, block, early)
 
     @pl.when(step == pl.num_programs(0) - 1)
     def _():
@@ -394,10 +401,10 @@
     for (_, rows), early in zip(PARTS, (early_one, early_two)):
         got = two_in if sums else one_in
         rest = [v.reshape(-1, width) for v in got]
+        if sums:
+            rest = after(rest, sums[-1])
         keep, give = tiles(left, early, rest, rows, listed[0], listed[1] * rows)
         mine, *sends = merge(keep, swap_cores(give))
-        if not sums:
-            sends, two_in = lax.optimization_barrier((sends, two_in))
         sums.append([mine] + [shift_z(s, k) for k, s in enumerate(sends, 1)])
     return finish(sums)
 

time: 229 us -> 226 us (0.987)
  starting transfers between devices: 45.1 us -> 33.5 us
  waiting for transfers between devices: 92.5 us -> 96.9 us
  Pallas kernels: 77.5 us -> 81.6 us
    ppermute x12, starting transfers between devices: 33.8 us -> 18.7 us  [shift(): return lax.ppermute(array, ('ex', 'lay'), pairs)]
    ppermute x6, starting transfers between devices: 10.4 us -> 14.7 us  [shift_z(): return lax.ppermute(array, 'lay', pairs)]
    ppermute x2, waiting for transfers between devices: 2.29 us -> 5.29 us  [swap_cores(): return lax.ppermute(array, 'lay', [(i, i ^ 1) for i in range(2 * SIDE)])]
    ppermute x6, waiting for transfers between devices: 7.29 us -> 10.2 us  [shift_z(): return lax.ppermute(array, 'lay', pairs)]
  transfers between devices with their start and end apart: 20 -> 20, of which waited for: 9 -> 14; matrix products, arithmetic and copies ran while one was open for 0% -> 0% of each run, Pallas kernels for 27% -> 29%
where the time goes in v6:
time: 226 us; the launch traced here: 225 us
  waiting for transfers between devices  96.9 us (43%)
  Pallas kernels  81.6 us (36%)
  starting transfers between devices  33.5 us (15%)
  local copies, waits for them, and re-layouts  12.7 us (6%)
    ppermute x12, waiting for transfers between devices, shift(): return lax.ppermute(array, ('ex', 'lay'), pairs)  81.3 us
    pallas_call x2, Pallas kernels, tiles(): pl.pallas_call(functools.partial(tiles_kernel, len(rights)), out_shape=(o...  22.6 us
    pallas_call x4, Pallas kernels, gather(): pl.pallas_call(functools.partial(gather_kernel, [start for _, start, _ in...  19.9 us
    ppermute x12, starting transfers between devices, shift(): return lax.ppermute(array, ('ex', 'lay'), pairs)  18.7 us
    pallas_call x1, Pallas kernels, left_transposed(): pl.pallas_call(left_kernel, out_shape=jax.ShapeDtypeStruct((examples // t...  16 us
    ppermute x6, starting transfers between devices, shift_z(): return lax.ppermute(array, 'lay', pairs)  14.7 us
    pallas_call x2, Pallas kernels, turn(): pl.pallas_call(turn_kernel, out_shape=outs, in_specs=[pl.BlockSpec(memory...  11 us
    pallas_call x2, Pallas kernels, early_products(): pl.pallas_call(functools.partial(early_kernel, len(owns)), out_shape=jax....  10.9 us
  transfers between devices with their start and end apart: 20, of which 14 were waited for; matrix products, arithmetic and copies ran while one was open for 0% of the time, Pallas kernels for 29%

profile of v6, /device:TPU:0, one launch (start us, length us, event | category | flops | bytes accessed | tf_op | source)
XLA Modules:
  0.0 225.2 jit_solution(4435294036426384584)
XLA Ops:
  0.0 0.7 copy-done
  0.7 0.2 dynamic-slice_reduce_fusion
  0.9 0.1 reshape.249
  1.0 0.1 add_add_fusion
  1.1 0.1 copy.17
  1.2 0.1 bitcast_select_fusion
  1.3 0.6 slice_bitcast_fusion
  1.9 3.6 %shard_map.57 = bf16[4,64,4096]{2,1,0:T(8,128)(2,1)} custom-call(s32[4]{0:T(128)} %get-tuple-element.111.index_ref, bf16[8,128,4096]{2,1,0:T(8,128)(2,1)} %bitcast.24), custom_call_target="tpu_custom_call" | custom-call | flops 1 | bytes 1 | tf_op jit(solution)/shard_map/pallas_call | solution.py:63
  5.5 1.9 collective-permute-start
  7.4 3.7 %shard_map.58 = bf16[4,64,4096]{2,1,0:T(8,128)(2,1)} custom-call(s32[4]{0:T(128)} %get-tuple-element.110.index_ref, bf16[8,128,4096]{2,1,0:T(8,128)(2,1)} %bitcast.25), custom_call_target="tpu_custom_call" | custom-call | flops 1 | bytes 1 | tf_op jit(solution)/shard_map/pallas_call | solution.py:63
  11.1 2.5 %collective-permute-start.4 = (bf16[4,64,4096]{2,1,0:T(8,128)(2,1)}, bf16[4,64,4096]{2,1,0:T(8,128)(2,1)}, u32[]{:S(2)}, u32[]{:S(2)}) collective-permute-start(bf16[4,64,4096]{2,1,0:T(8,128)(2,1)} %shard_map.58), channel_id=1, source_target_pairs={{0,64},{1,17},{2,66},{3,19},{4,68},{5,21},{6,70},{7,23},{8,72},{9,... | collective-permute-start | bytes 6291464 | tf_op jit(solution)/shard_map/ppermute | solution.py:330
  13.7 3.7 %shard_map.59 = bf16[4,64,4096]{2,1,0:T(8,128)(2,1)} custom-call(s32[4]{0:T(128)} %get-tuple-element.109.index_ref, bf16[8,128,4096]{2,1,0:T(8,128)(2,1)} %bitcast.26), custom_call_target="tpu_custom_call" | custom-call | flops 1 | bytes 1 | tf_op jit(solution)/shard_map/pallas_call | solution.py:63
  17.4 1.1 collective-permute-start.5
  18.5 0.6 concatenate.16.index_ref
  19.1 8.9 %shard_map.55 = (bf16[4,64,4096]{2,1,0:T(8,128)(2,1)}, bf16[4,64,4096]{2,1,0:T(8,128)(2,1)}, bf16[4,64,4096]{2,1,0:T(8,128)(2,1)}, bf16[4,64,4096]{2,1,0:T(8,128)(2,1)}, bf16[4,64,4096]{2,1,0:T(8,128)(2,1)}) custom-call(s32[20]{0:T(128)} %concatenate.16.index_ref, bf16[8,128,4096]{2,1,0:T(8,128)(2,1)} %bitcast.27), custom_call_target="tpu_custom_call" | custom-call | flops 1 | bytes 1 | tf_op jit(solution)/shard_map/pallas_call | solution.py:63
  28.0 16.0 %shard_map.56.left_ref = bf16[4,4096,256]{2,1,0:T(8,128)(2,1)} custom-call(bf16[1024,4096]{1,0:T(8,128)(2,1)} %bitcast.28, bf16[64,64]{1,0:T(8,128)(2,1)} %bitcast.29, bf16[64,64]{1,0:T(8,128)(2,1)} %bitcast.30), custom_call_target="tpu_custom_call" | custom-call | flops 1 | bytes 1 | tf_op jit(solution)/shard_map/pallas_call | solution.py:162
  44.0 0.8 collective-permute-start.1
  44.8 0.8 collective-permute-start.2
  45.6 1.9 collective-permute-start.3
  47.6 9.4 %collective-permute-done.4.refs_2_ = bf16[4,64,4096]{2,1,0:T(8,128)(2,1)} collective-permute-done((bf16[4,64,4096]{2,1,0:T(8,128)(2,1)}, bf16[4,64,4096]{2,1,0:T(8,128)(2,1)}, u32[]{:S(2)}, u32[]{:S(2)}) %collective-permute-start.4) | collective-permute-done | bytes 2097184 | tf_op jit(solution)/shard_map/ppermute | solution.py:330
  57.0 2.8 %collective-permute-done.5.refs_3_ = bf16[4,64,4096]{2,1,0:T(8,128)(2,1)} collective-permute-done((bf16[4,64,4096]{2,1,0:T(8,128)(2,1)}, bf16[4,64,4096]{2,1,0:T(8,128)(2,1)}, u32[]{:S(2)}, u32[]{:S(2)}) %collective-permute-start.5) | collective-permute-done | bytes 2097184 | tf_op jit(solution)/shard_map/ppermute | solution.py:330
  59.7 5.5 %shard_map.60 = (bf16[4,64,4096]{2,1,0:T(8,128)(2,1)}, bf16[4,64,4096]{2,1,0:T(8,128)(2,1)}, bf16[4,64,4096]{2,1,0:T(8,128)(2,1)}) custom-call(bf16[4,64,4096]{2,1,0:T(8,128)(2,1)} %get-tuple-element.64.refs_0_, bf16[4,64,4096]{2,1,0:T(8,128)(2,1)} %copy-done.5, bf16[4,64,4096]{2,1,0:T(8,128)(2,1)} %collective-permute-done.4.refs_2_, ...), custom_call_target="tpu_custom_call" | custom-call | flops 1 | bytes 1 | tf_op jit(solution)/shard_map/pallas_call | solution.py:89
  65.3 2.0 collective-permute-start.6
  67.3 1.3 collective-permute-start.7
  68.6 22.9 %collective-permute-done.1.refs_1_ = bf16[4,64,4096]{2,1,0:T(8,128)(2,1)} collective-permute-done((bf16[4,64,4096]{2,1,0:T(8,128)(2,1)}, bf16[4,64,4096]{2,1,0:T(8,128)(2,1)}, u32[]{:S(2)}, u32[]{:S(2)}) %collective-permute-start.1) | collective-permute-done | bytes 2097184 | tf_op jit(solution)/shard_map/ppermute | solution.py:330
  91.5 1.5 collective-permute-start.8
  93.0 0.1 sub.60
  93.1 0.1 squeeze.38
  93.2 3.4 %copy-done.2 = bf16[4,4096,256]{2,1,0:T(8,128)(2,1)S(1)} copy-done((bf16[4,4096,256]{2,1,0:T(8,128)(2,1)S(1)}, bf16[4,4096,256]{2,1,0:T(8,128)(2,1)}, u32[]{:S(2)}) %copy-start.2) | copy-done | bytes 8388632
  96.6 1.6 copy-done.6
  98.2 1.6 copy-done.7
  99.8 5.3 %shard_map.61.early_ref = f32[8,256,128]{2,1,0:T(8,128)S(1)} custom-call(bf16[4,4096,256]{2,1,0:T(8,128)(2,1)S(1)} %copy-done.2, bf16[4,64,4096]{2,1,0:T(8,128)(2,1)S(1)} %copy-done.7, bf16[4,64,4096]{2,1,0:T(8,128)(2,1)S(1)} %copy-done.6, bf16[4,64,4096]{2,1,0:T(8,128)(2,1)} %collective-permute-done.4.refs_2_, ...), custom_call_target="tpu_custom_call" | custom-call | flops 1 | bytes 1 | tf_op jit(solution)/shard_map/pallas_call | solution.py:215
  105.1 29.1 %collective-permute-done.2.refs_2_ = bf16[4,64,4096]{2,1,0:T(8,128)(2,1)} collective-permute-done((bf16[4,64,4096]{2,1,0:T(8,128)(2,1)}, bf16[4,64,4096]{2,1,0:T(8,128)(2,1)}, u32[]{:S(2)}, u32[]{:S(2)}) %collective-permute-start.2) | collective-permute-done | bytes 2097184 | tf_op jit(solution)/shard_map/ppermute | solution.py:330
  134.2 7.0 %collective-permute-done.3.refs_3_ = bf16[4,64,4096]{2,1,0:T(8,128)(2,1)} collective-permute-done((bf16[4,64,4096]{2,1,0:T(8,128)(2,1)}, bf16[4,64,4096]{2,1,0:T(8,128)(2,1)}, u32[]{:S(2)}, u32[]{:S(2)}) %collective-permute-start.3) | collective-permute-done | bytes 2097184 | tf_op jit(solution)/shard_map/ppermute | solution.py:330
  141.3 5.5 %shard_map.62 = (bf16[4,64,4096]{2,1,0:T(8,128)(2,1)}, bf16[4,64,4096]{2,1,0:T(8,128)(2,1)}, bf16[4,64,4096]{2,1,0:T(8,128)(2,1)}) custom-call(bf16[4,64,4096]{2,1,0:T(8,128)(2,1)} %get-tuple-element.80.refs_0_, bf16[4,64,4096]{2,1,0:T(8,128)(2,1)} %collective-permute-done.1.refs_1_, bf16[4,64,4096]{2,1,0:T(8,128)(2,1)} %collective-permute-done.2.refs_2_, ...), custom_call_target="tpu_custom_call" | custom-call | flops 1 | bytes 1 | tf_op jit(solution)/shard_map/pallas_call | solution.py:89
  146.8 0.9 collective-permute-start.13
  147.7 2.4 %collective-permute-start.14 = (bf16[4,64,4096]{2,1,0:T(8,128)(2,1)}, bf16[4,64,4096]{2,1,0:T(8,128)(2,1)}, u32[]{:S(2)}, u32[]{:S(2)}) collective-permute-start(bf16[4,64,4096]{2,1,0:T(8,128)(2,1)} %get-tuple-element.94), channel_id=1, source_target_pairs={{0,24},{1,97},{2,26},{3,99},{4,28},{5,101},{6,30},{7,103},{8,0},{9... | collective-permute-start | bytes 6291464 | tf_op jit(solution)/shard_map/ppermute | solution.py:330
  150.1 1.4 collective-permute-start.15
  151.6 0.1 squeeze.39.block_ref
  151.7 0.1 mul.24.row_ref
  151.8 3.4 %copy-done.3 = bf16[4,4096,256]{2,1,0:T(8,128)(2,1)S(1)} copy-done((bf16[4,4096,256]{2,1,0:T(8,128)(2,1)S(1)}, bf16[4,4096,256]{2,1,0:T(8,128)(2,1)}, u32[]{:S(2)}) %copy-start.3) | copy-done | bytes 8388632
  155.2 5.6 %shard_map.63.early_ref = f32[8,256,128]{2,1,0:T(8,128)S(1)} custom-call(bf16[4,4096,256]{2,1,0:T(8,128)(2,1)S(1)} %copy-done.3, bf16[4,64,4096]{2,1,0:T(8,128)(2,1)S(1)} %copy-done.4, bf16[4,64,4096]{2,1,0:T(8,128)(2,1)} %collective-permute-done.1.refs_1_, bf16[4,64,4096]{2,1,0:T(8,128)(2,1)} %collective-permute-done.2.refs_2_, ...), custom_call_target="tpu_custom_call" | custom-call | flops 1 | bytes 1 | tf_op jit(solution)/shard_map/pallas_call | solution.py:215
  160.8 11.5 %shard_map.64 = (f32[32,64,128]{2,1,0:T(8,128)S(1)}, f32[32,64,128]{2,1,0:T(8,128)S(1)}) custom-call(s32[64]{0:T(128)S(1)} %squeeze.39.block_ref, s32[64]{0:T(128)S(1)} %mul.24.row_ref, bf16[4,4096,256]{2,1,0:T(8,128)(2,1)S(1)} %copy-done.3, f32[8,256,128]{2,1,0:T(8,128)S(1)} %shard_map.61.early_ref, bf16[256,4096]{1,0:T(8,128)(2,1)} %bitcast.10.refs_0_, ...), custom_call_target="tpu_custom_call" | custom-call | flops 1 | bytes 1 | tf_op jit(solution)/shard_map/pallas_call | solution.py:262
  172.3 0.1 collective-permute-start.9
  172.4 2.6 %collective-permute-done.9.got_ref = f32[32,64,128]{2,1,0:T(8,128)S(1)} collective-permute-done((f32[32,64,128]{2,1,0:T(8,128)S(1)}, f32[32,64,128]{2,1,0:T(8,128)S(1)}, u32[]{:S(2)}, u32[]{:S(2)}) %collective-permute-start.9) | collective-permute-done | bytes 1048608 | tf_op jit(solution)/shard_map/ppermute | solution.py:334
  175.0 0.1 shard_map.65
  175.1 2.0 collective-permute-start.10
  177.1 3.6 %collective-permute-start.11 = (bf16[8,64,128]{2,1,0:T(8,128)(2,1)S(1)}, bf16[8,64,128]{2,1,0:T(8,128)(2,1)S(1)}, u32[]{:S(2)}, u32[]{:S(2)}) collective-permute-start(bf16[8,64,128]{2,1,0:T(8,128)(2,1)S(1)} %get-tuple-element.91), channel_id=1, source_target_pairs={{0,4},{1,5},{2,6},{3,7},{4,0},{5,1},{6,2},{7,3},{8,12},{9,13},{10,... | collective-permute-start | bytes 393224 | tf_op jit(solution)/shard_map/ppermute | solution.py:339
  180.7 2.3 %collective-permute-done.10.refs_1_ = bf16[8,64,128]{2,1,0:T(8,128)(2,1)S(1)} collective-permute-done((bf16[8,64,128]{2,1,0:T(8,128)(2,1)S(1)}, bf16[8,64,128]{2,1,0:T(8,128)(2,1)S(1)}, u32[]{:S(2)}, u32[]{:S(2)}) %collective-permute-start.10) | collective-permute-done | bytes 131104 | tf_op jit(solution)/shard_map/ppermute | solution.py:339
  183.0 2.5 %collective-permute-start.12 = (bf16[8,64,128]{2,1,0:T(8,128)(2,1)S(1)}, bf16[8,64,128]{2,1,0:T(8,128)(2,1)S(1)}, u32[]{:S(2)}, u32[]{:S(2)}) collective-permute-start(bf16[8,64,128]{2,1,0:T(8,128)(2,1)S(1)} %get-tuple-element.92), channel_id=1, source_target_pairs={{0,6},{1,7},{2,0},{3,1},{4,2},{5,3},{6,4},{7,5},{8,14},{9,15},{10,... | collective-permute-start | bytes 393224 | tf_op jit(solution)/shard_map/ppermute | solution.py:339
  185.6 1.4 collective-permute-done.11.refs_2_
  187.0 1.1 collective-permute-done.12.refs_3_
  188.2 8.3 %collective-permute-done.14 = bf16[4,64,4096]{2,1,0:T(8,128)(2,1)} collective-permute-done((bf16[4,64,4096]{2,1,0:T(8,128)(2,1)}, bf16[4,64,4096]{2,1,0:T(8,128)(2,1)}, u32[]{:S(2)}, u32[]{:S(2)}) %collective-permute-start.14) | collective-permute-done | bytes 2097184 | tf_op jit(solution)/shard_map/ppermute | solution.py:330
  196.5 1.8 collective-permute-done.15
  198.3 11.1 %shard_map.66 = (f32[32,64,128]{2,1,0:T(8,128)S(1)}, f32[32,64,128]{2,1,0:T(8,128)S(1)}) custom-call(s32[64]{0:T(128)S(1)} %squeeze.39.block_ref, s32[64]{0:T(128)S(1)} %mul.24.row_ref, bf16[4,4096,256]{2,1,0:T(8,128)(2,1)S(1)} %bitcast.23, f32[8,256,128]{2,1,0:T(8,128)S(1)} %shard_map.63.early_ref, bf16[256,4096]{1,0:T(8,128)(2,1)} %bitcast.13.refs_0_, ...), custom_call_target="tpu_custom_call" | custom-call | flops 1 | bytes 1 | tf_op jit(solution)/shard_map/pallas_call | solution.py:262
  209.5 0.1 collective-permute-start.16
  209.6 2.6 %collective-permute-done.16.got_ref = f32[32,64,128]{2,1,0:T(8,128)S(1)} collective-permute-done((f32[32,64,128]{2,1,0:T(8,128)S(1)}, f32[32,64,128]{2,1,0:T(8,128)S(1)}, u32[]{:S(2)}, u32[]{:S(2)}) %collective-permute-start.16) | collective-permute-done | bytes 1048608 | tf_op jit(solution)/shard_map/ppermute | solution.py:334
  212.2 0.1 shard_map.67
  212.3 2.0 collective-permute-start.17
  214.3 3.6 %collective-permute-start.18 = (bf16[8,64,128]{2,1,0:T(8,128)(2,1)S(1)}, bf16[8,64,128]{2,1,0:T(8,128)(2,1)S(1)}, u32[]{:S(2)}, u32[]{:S(2)}) collective-permute-start(bf16[8,64,128]{2,1,0:T(8,128)(2,1)S(1)} %get-tuple-element.103), channel_id=1, source_target_pairs={{0,4},{1,5},{2,6},{3,7},{4,0},{5,1},{6,2},{7,3},{8,12},{9,13},{10,... | collective-permute-start | bytes 393224 | tf_op jit(solution)/shard_map/ppermute | solution.py:339
  217.9 1.0 collective-permute-start.19
  218.9 1.3 collective-permute-done.17.refs_5_
  220.2 4.0 %collective-permute-done.18.refs_6_ = bf16[8,64,128]{2,1,0:T(8,128)(2,1)S(1)} collective-permute-done((bf16[8,64,128]{2,1,0:T(8,128)(2,1)S(1)}, bf16[8,64,128]{2,1,0:T(8,128)(2,1)S(1)}, u32[]{:S(2)}, u32[]{:S(2)}) %collective-permute-start.18) | collective-permute-done | bytes 131104 | tf_op jit(solution)/shard_map/ppermute | solution.py:339
  224.2 1.0 shard_map.68
  (37 shorter events, 0.2 us)
Async XLA Ops:
  0.0 0.7 copy-start
  5.5 38.5 %collective-permute-start = (bf16[4,64,4096]{2,1,0:T(8,128)(2,1)}, bf16[4,64,4096]{2,1,0:T(8,128)(2,1)S(1)}, u32[]{:S(2)}, u32[]{:S(2)}) collective-permute-start(bf16[4,64,4096]{2,1,0:T(8,128)(2,1)} %shard_map.57), channel_id=1, source_target_pairs={{0,32},{1,9},{2,34},{3,11},{4,36},{5,13},{6,38},{7,15},{8,40},{9,1... | collective-permute-start | bytes 6291464 | tf_op jit(solution)/shard_map/ppermute | solution.py:330
  11.1 45.9 %collective-permute-start.4 = (bf16[4,64,4096]{2,1,0:T(8,128)(2,1)}, bf16[4,64,4096]{2,1,0:T(8,128)(2,1)}, u32[]{:S(2)}, u32[]{:S(2)}) collective-permute-start(bf16[4,64,4096]{2,1,0:T(8,128)(2,1)} %shard_map.58), channel_id=1, source_target_pairs={{0,64},{1,17},{2,66},{3,19},{4,68},{5,21},{6,70},{7,23},{8,72},{9,... | collective-permute-start | bytes 6291464 | tf_op jit(solution)/shard_map/ppermute | solution.py:330
  13.6 4.8 %copy-start.8 = (s32[4]{0:T(128)S(1)}, s32[4]{0:T(128)}, u32[]{:S(2)}) copy-start(s32[4]{0:T(128)} %get-tuple-element.109.index_ref) | copy-start | bytes 52
  13.6 4.8 %copy-start.9 = (s32[4]{0:T(128)S(1)}, s32[4]{0:T(128)}, u32[]{:S(2)}) copy-start(s32[4]{0:T(128)} %get-tuple-element.110.index_ref) | copy-start | bytes 52
  13.6 4.8 %copy-start.10 = (s32[4]{0:T(128)S(1)}, s32[4]{0:T(128)}, u32[]{:S(2)}) copy-start(s32[4]{0:T(128)} %get-tuple-element.111.index_ref) | copy-start | bytes 52
  17.4 42.4 %collective-permute-start.5 = (bf16[4,64,4096]{2,1,0:T(8,128)(2,1)}, bf16[4,64,4096]{2,1,0:T(8,128)(2,1)}, u32[]{:S(2)}, u32[]{:S(2)}) collective-permute-start(bf16[4,64,4096]{2,1,0:T(8,128)(2,1)} %shard_map.59), channel_id=1, source_target_pairs={{0,96},{1,25},{2,98},{3,27},{4,100},{5,29},{6,102},{7,31},{8,104},... | collective-permute-start | bytes 6291464 | tf_op jit(solution)/shard_map/ppermute | solution.py:330
  44.0 15.8 %copy-start.5 = (bf16[4,64,4096]{2,1,0:T(8,128)(2,1)}, bf16[4,64,4096]{2,1,0:T(8,128)(2,1)S(1)}, u32[]{:S(2)}) copy-start(bf16[4,64,4096]{2,1,0:T(8,128)(2,1)S(1)} %collective-permute-done.refs_1_) | copy-start | bytes 6291460
  44.0 47.5 %collective-permute-start.1 = (bf16[4,64,4096]{2,1,0:T(8,128)(2,1)}, bf16[4,64,4096]{2,1,0:T(8,128)(2,1)}, u32[]{:S(2)}, u32[]{:S(2)}) collective-permute-start(bf16[4,64,4096]{2,1,0:T(8,128)(2,1)} %get-tuple-element.61), channel_id=1, source_target_pairs={{0,32},{1,9},{2,34},{3,11},{4,36},{5,13},{6,38},{7,15},{8,40},{9,1... | collective-permute-start | bytes 6291464 | tf_op jit(solution)/shard_map/ppermute | solution.py:330
  44.8 89.4 %collective-permute-start.2 = (bf16[4,64,4096]{2,1,0:T(8,128)(2,1)}, bf16[4,64,4096]{2,1,0:T(8,128)(2,1)}, u32[]{:S(2)}, u32[]{:S(2)}) collective-permute-start(bf16[4,64,4096]{2,1,0:T(8,128)(2,1)} %get-tuple-element.62), channel_id=1, source_target_pairs={{0,64},{1,17},{2,66},{3,19},{4,68},{5,21},{6,70},{7,23},{8,72},{9,... | collective-permute-start | bytes 6291464 | tf_op jit(solution)/shard_map/ppermute | solution.py:330
  45.6 95.7 %collective-permute-start.3 = (bf16[4,64,4096]{2,1,0:T(8,128)(2,1)}, bf16[4,64,4096]{2,1,0:T(8,128)(2,1)}, u32[]{:S(2)}, u32[]{:S(2)}) collective-permute-start(bf16[4,64,4096]{2,1,0:T(8,128)(2,1)} %get-tuple-element.63), channel_id=1, source_target_pairs={{0,96},{1,25},{2,98},{3,27},{4,100},{5,29},{6,102},{7,31},{8,104},... | collective-permute-start | bytes 6291464 | tf_op jit(solution)/shard_map/ppermute | solution.py:330
  59.7 33.3 %copy-start.11 = (s32[64,2]{0,1:T(2,128)S(1)}, s32[64,2]{0,1:T(2,128)}, u32[]{:S(2)}) copy-start(s32[64,2]{0,1:T(2,128)} %param.9) | copy-start | bytes 1540
  65.3 81.5 %collective-permute-start.6 = (bf16[4,64,4096]{2,1,0:T(8,128)(2,1)}, bf16[4,64,4096]{2,1,0:T(8,128)(2,1)}, u32[]{:S(2)}, u32[]{:S(2)}) collective-permute-start(bf16[4,64,4096]{2,1,0:T(8,128)(2,1)} %get-tuple-element.65), channel_id=1, source_target_pairs={{0,8},{1,33},{2,10},{3,35},{4,12},{5,37},{6,14},{7,39},{8,16},{9,4... | collective-permute-start | bytes 6291464 | tf_op jit(solution)/shard_map/ppermute | solution.py:330
  67.3 93.5 %collective-permute-start.7 = (bf16[4,64,4096]{2,1,0:T(8,128)(2,1)}, bf16[4,64,4096]{2,1,0:T(8,128)(2,1)}, u32[]{:S(2)}, u32[]{:S(2)}) collective-permute-start(bf16[4,64,4096]{2,1,0:T(8,128)(2,1)} %get-tuple-element.67), channel_id=1, source_target_pairs={{0,24},{1,97},{2,26},{3,99},{4,28},{5,101},{6,30},{7,103},{8,0},{9... | collective-permute-start | bytes 6291464 | tf_op jit(solution)/shard_map/ppermute | solution.py:330
  91.5 69.3 %collective-permute-start.8 = (bf16[4,64,4096]{2,1,0:T(8,128)(2,1)}, bf16[4,64,4096]{2,1,0:T(8,128)(2,1)}, u32[]{:S(2)}, u32[]{:S(2)}) collective-permute-start(bf16[4,64,4096]{2,1,0:T(8,128)(2,1)} %get-tuple-element.66), channel_id=1, source_target_pairs={{0,16},{1,65},{2,18},{3,67},{4,20},{5,69},{6,22},{7,71},{8,24},{9,... | collective-permute-start | bytes 6291464 | tf_op jit(solution)/shard_map/ppermute | solution.py:330
  93.2 3.4 %copy-start.2 = (bf16[4,4096,256]{2,1,0:T(8,128)(2,1)S(1)}, bf16[4,4096,256]{2,1,0:T(8,128)(2,1)}, u32[]{:S(2)}) copy-start(bf16[4,4096,256]{2,1,0:T(8,128)(2,1)} %shard_map.56.left_ref) | copy-start | bytes 25165828
  96.6 1.6 copy-start.6
  98.2 1.6 copy-start.7
  105.1 46.6 %copy-start.4 = (bf16[4,64,4096]{2,1,0:T(8,128)(2,1)S(1)}, bf16[4,64,4096]{2,1,0:T(8,128)(2,1)}, u32[]{:S(2)}) copy-start(bf16[4,64,4096]{2,1,0:T(8,128)(2,1)} %get-tuple-element.80.refs_0_) | copy-start | bytes 6291460
  146.8 41.4 %collective-permute-start.13 = (bf16[4,64,4096]{2,1,0:T(8,128)(2,1)}, bf16[4,64,4096]{2,1,0:T(8,128)(2,1)}, u32[]{:S(2)}, u32[]{:S(2)}) collective-permute-start(bf16[4,64,4096]{2,1,0:T(8,128)(2,1)} %get-tuple-element.93), channel_id=1, source_target_pairs={{0,8},{1,33},{2,10},{3,35},{4,12},{5,37},{6,14},{7,39},{8,16},{9,4... | collective-permute-start | bytes 6291464 | tf_op jit(solution)/shard_map/ppermute | solution.py:330
  147.7 48.8 %collective-permute-start.14 = (bf16[4,64,4096]{2,1,0:T(8,128)(2,1)}, bf16[4,64,4096]{2,1,0:T(8,128)(2,1)}, u32[]{:S(2)}, u32[]{:S(2)}) collective-permute-start(bf16[4,64,4096]{2,1,0:T(8,128)(2,1)} %get-tuple-element.94), channel_id=1, source_target_pairs={{0,24},{1,97},{2,26},{3,99},{4,28},{5,101},{6,30},{7,103},{8,0},{9... | collective-permute-start | bytes 6291464 | tf_op jit(solution)/shard_map/ppermute | solution.py:330
  150.1 48.2 %collective-permute-start.15 = (bf16[4,64,4096]{2,1,0:T(8,128)(2,1)}, bf16[4,64,4096]{2,1,0:T(8,128)(2,1)}, u32[]{:S(2)}, u32[]{:S(2)}) collective-permute-start(bf16[4,64,4096]{2,1,0:T(8,128)(2,1)} %get-tuple-element.95), channel_id=1, source_target_pairs={{0,16},{1,65},{2,18},{3,67},{4,20},{5,69},{6,22},{7,71},{8,24},{9,... | collective-permute-start | bytes 6291464 | tf_op jit(solution)/shard_map/ppermute | solution.py:330
  151.8 3.4 %copy-start.3 = (bf16[4,4096,256]{2,1,0:T(8,128)(2,1)S(1)}, bf16[4,4096,256]{2,1,0:T(8,128)(2,1)}, u32[]{:S(2)}) copy-start(bf16[4,4096,256]{2,1,0:T(8,128)(2,1)} %shard_map.56.left_ref) | copy-start | bytes 25165828
  160.8 37.5 %slice-start = ((s8[8388608]{0:T(1024)(128)(4,1)}), s8[4194304]{0:T(1024)(128)(4,1)S(1)}, s32[]{:S(2)}) async-start(s8[8388608]{0:T(1024)(128)(4,1)} %bitcast.22), calls=%async_computation | async-start | bytes 8388608
  160.8 37.5 %slice-start.1 = ((s8[8388608]{0:T(1024)(128)(4,1)}), s8[4194304]{0:T(1024)(128)(4,1)S(1)}, s32[]{:S(2)}) async-start(s8[8388608]{0:T(1024)(128)(4,1)} %bitcast.22), calls=%async_computation.1 | async-start | bytes 8388608
  172.3 2.7 %collective-permute-start.9 = (f32[32,64,128]{2,1,0:T(8,128)S(1)}, f32[32,64,128]{2,1,0:T(8,128)S(1)}, u32[]{:S(2)}, u32[]{:S(2)}) collective-permute-start(f32[32,64,128]{2,1,0:T(8,128)S(1)} %get-tuple-element.88), channel_id=1, source_target_pairs={{0,1},{1,0},{2,3},{3,2},{4,5},{5,4},{6,7},{7,6},{8,9},{9,8},{10,11... | collective-permute-start | bytes 3145736 | tf_op jit(solution)/shard_map/ppermute | solution.py:334
  175.1 7.9 %collective-permute-start.10 = (bf16[8,64,128]{2,1,0:T(8,128)(2,1)S(1)}, bf16[8,64,128]{2,1,0:T(8,128)(2,1)S(1)}, u32[]{:S(2)}, u32[]{:S(2)}) collective-permute-start(bf16[8,64,128]{2,1,0:T(8,128)(2,1)S(1)} %get-tuple-element.90), channel_id=1, source_target_pairs={{0,2},{1,3},{2,4},{3,5},{4,6},{5,7},{6,0},{7,1},{8,10},{9,11},{10,... | collective-permute-start | bytes 393224 | tf_op jit(solution)/shard_map/ppermute | solution.py:339
  177.1 9.9 %collective-permute-start.11 = (bf16[8,64,128]{2,1,0:T(8,128)(2,1)S(1)}, bf16[8,64,128]{2,1,0:T(8,128)(2,1)S(1)}, u32[]{:S(2)}, u32[]{:S(2)}) collective-permute-start(bf16[8,64,128]{2,1,0:T(8,128)(2,1)S(1)} %get-tuple-element.91), channel_id=1, source_target_pairs={{0,4},{1,5},{2,6},{3,7},{4,0},{5,1},{6,2},{7,3},{8,12},{9,13},{10,... | collective-permute-start | bytes 393224 | tf_op jit(solution)/shard_map/ppermute | solution.py:339
  183.0 5.1 %collective-permute-start.12 = (bf16[8,64,128]{2,1,0:T(8,128)(2,1)S(1)}, bf16[8,64,128]{2,1,0:T(8,128)(2,1)S(1)}, u32[]{:S(2)}, u32[]{:S(2)}) collective-permute-start(bf16[8,64,128]{2,1,0:T(8,128)(2,1)S(1)} %get-tuple-element.92), channel_id=1, source_target_pairs={{0,6},{1,7},{2,0},{3,1},{4,2},{5,3},{6,4},{7,5},{8,14},{9,15},{10,... | collective-permute-start | bytes 393224 | tf_op jit(solution)/shard_map/ppermute | solution.py:339
  198.3 26.9 %copy-start.1 = (s32[16,16]{1,0:T(8,128)S(1)}, s32[16,16]{1,0:T(8,128)}, u32[]{:S(2)}) copy-start(s32[16,16]{1,0:T(8,128)} %param.8) | copy-start | bytes 3076
  209.5 2.7 %collective-permute-start.16 = (f32[32,64,128]{2,1,0:T(8,128)S(1)}, f32[32,64,128]{2,1,0:T(8,128)S(1)}, u32[]{:S(2)}, u32[]{:S(2)}) collective-permute-start(f32[32,64,128]{2,1,0:T(8,128)S(1)} %get-tuple-element.100), channel_id=1, source_target_pairs={{0,1},{1,0},{2,3},{3,2},{4,5},{5,4},{6,7},{7,6},{8,9},{9,8},{10,11... | collective-permute-start | bytes 3145736 | tf_op jit(solution)/shard_map/ppermute | solution.py:334
  212.3 7.9 %collective-permute-start.17 = (bf16[8,64,128]{2,1,0:T(8,128)(2,1)S(1)}, bf16[8,64,128]{2,1,0:T(8,128)(2,1)S(1)}, u32[]{:S(2)}, u32[]{:S(2)}) collective-permute-start(bf16[8,64,128]{2,1,0:T(8,128)(2,1)S(1)} %get-tuple-element.102), channel_id=1, source_target_pairs={{0,2},{1,3},{2,4},{3,5},{4,6},{5,7},{6,0},{7,1},{8,10},{9,11},{10,... | collective-permute-start | bytes 393224 | tf_op jit(solution)/shard_map/ppermute | solution.py:339
  214.3 9.9 %collective-permute-start.18 = (bf16[8,64,128]{2,1,0:T(8,128)(2,1)S(1)}, bf16[8,64,128]{2,1,0:T(8,128)(2,1)S(1)}, u32[]{:S(2)}, u32[]{:S(2)}) collective-permute-start(bf16[8,64,128]{2,1,0:T(8,128)(2,1)S(1)} %get-tuple-element.103), channel_id=1, source_target_pairs={{0,4},{1,5},{2,6},{3,7},{4,0},{5,1},{6,2},{7,3},{8,12},{9,13},{10,... | collective-permute-start | bytes 393224 | tf_op jit(solution)/shard_map/ppermute | solution.py:339
  217.9 6.3 %collective-permute-start.19 = (bf16[8,64,128]{2,1,0:T(8,128)(2,1)S(1)}, bf16[8,64,128]{2,1,0:T(8,128)(2,1)S(1)}, u32[]{:S(2)}, u32[]{:S(2)}) collective-permute-start(bf16[8,64,128]{2,1,0:T(8,128)(2,1)S(1)} %get-tuple-element.104), channel_id=1, source_target_pairs={{0,6},{1,7},{2,0},{3,1},{4,2},{5,3},{6,4},{7,5},{8,14},{9,15},{10,... | collective-permute-start | bytes 393224 | tf_op jit(solution)/shard_map/ppermute | solution.py:339

commit v7 on v6

--- a/solution.py
+++ b/solution.py
@@ -375,7 +375,7 @@
     two = {d: shift(bundles[d], 0, d) for d in STEPS} | {0: bundles[0]}
     one = [one[d] for d in range(SIDE)]
     turned = dict(enumerate(turn(one), 1))
-    one_in = [shift(turned[k], 1, k) for k in STEPS]
+    one_in = [shift(after(turned[k], two[1]), 1, k) for k in STEPS]
     early_one = early_products(after(left, turned), one)
     two = after([two[d] for d in range(SIDE)], early_one)
     turned = dict(enumerate(turn(two), 1))

time: 226 us -> 225 us (level)
  waiting for transfers between devices: 96.9 us -> 62.1 us
  starting transfers between devices: 33.5 us -> 67.4 us
    ppermute x12, waiting for transfers between devices: 81.3 us -> 46.4 us  [shift(): return lax.ppermute(array, ('ex', 'lay'), pairs)]
    ppermute x2, starting transfers between devices: 0.17 us -> 19.6 us  [swap_cores(): return lax.ppermute(array, 'lay', [(i, i ^ 1) for i in range(2 * SIDE)])]
    ppermute x12, starting transfers between devices: 18.7 us -> 33.3 us  [shift(): return lax.ppermute(array, ('ex', 'lay'), pairs)]
  transfers between devices with their start and end apart: 20 -> 20, of which waited for: 14 -> 11; matrix products, arithmetic and copies ran while one was open for 0% -> 0% of each run, Pallas kernels for 29% -> 29%
where the time goes in v7:
time: 225 us; the launch traced here: 224 us
  Pallas kernels  81.4 us (36%)
  starting transfers between devices  67.4 us (30%)
  waiting for transfers between devices  62.1 us (28%)
  local copies, waits for them, and re-layouts  12.6 us (6%)
    ppermute x12, waiting for transfers between devices, shift(): return lax.ppermute(array, ('ex', 'lay'), pairs)  46.4 us
    ppermute x12, starting transfers between devices, shift(): return lax.ppermute(array, ('ex', 'lay'), pairs)  33.3 us
    pallas_call x2, Pallas kernels, tiles(): pl.pallas_call(functools.partial(tiles_kernel, len(rights)), out_shape=(o...  22.6 us
    pallas_call x4, Pallas kernels, gather(): pl.pallas_call(functools.partial(gather_kernel, [start for _, start, _ in...  19.6 us
    ppermute x2, starting transfers between devices, swap_cores(): return lax.ppermute(array, 'lay', [(i, i ^ 1) for i in range(2 * SIDE)])  19.6 us
    pallas_call x1, Pallas kernels, left_transposed(): pl.pallas_call(left_kernel, out_shape=jax.ShapeDtypeStruct((examples // t...  16 us
    ppermute x6, starting transfers between devices, shift_z(): return lax.ppermute(array, 'lay', pairs)  14.5 us
    ppermute x6, waiting for transfers between devices, shift_z(): return lax.ppermute(array, 'lay', pairs)  11.1 us
  transfers between devices with their start and end apart: 20, of which 11 were waited for; matrix products, arithmetic and copies ran while one was open for 0% of the time, Pallas kernels for 29%

profile of v7, /device:TPU:0, one launch (start us, length us, event | category | flops | bytes accessed | tf_op | source)
XLA Modules:
  0.0 223.9 jit_solution(17998548213237860616)
XLA Ops:
  0.0 0.7 copy-done
  0.7 0.2 dynamic-slice_reduce_fusion
  0.9 0.1 reshape.249
  1.0 0.1 add_add_fusion
  1.0 0.1 dynamic_slice.12
  1.1 0.1 copy.17
  1.2 0.1 bitcast_select_fusion
  1.3 0.5 slice_bitcast_fusion
  1.8 3.6 %shard_map.57 = bf16[4,64,4096]{2,1,0:T(8,128)(2,1)} custom-call(s32[4]{0:T(128)} %get-tuple-element.117.index_ref, bf16[8,128,4096]{2,1,0:T(8,128)(2,1)} %bitcast.24), custom_call_target="tpu_custom_call" | custom-call | flops 1 | bytes 1 | tf_op jit(solution)/shard_map/pallas_call | solution.py:63
  5.4 1.8 collective-permute-start
  7.2 3.6 %shard_map.58 = bf16[4,64,4096]{2,1,0:T(8,128)(2,1)} custom-call(s32[4]{0:T(128)} %get-tuple-element.116.index_ref, bf16[8,128,4096]{2,1,0:T(8,128)(2,1)} %bitcast.25), custom_call_target="tpu_custom_call" | custom-call | flops 1 | bytes 1 | tf_op jit(solution)/shard_map/pallas_call | solution.py:63
  10.9 2.0 collective-permute-start.4
  12.8 3.7 %shard_map.59 = bf16[4,64,4096]{2,1,0:T(8,128)(2,1)} custom-call(s32[4]{0:T(128)} %get-tuple-element.115.index_ref, bf16[8,128,4096]{2,1,0:T(8,128)(2,1)} %bitcast.26), custom_call_target="tpu_custom_call" | custom-call | flops 1 | bytes 1 | tf_op jit(solution)/shard_map/pallas_call | solution.py:63
  16.6 0.6 concatenate.16.index_ref
  17.2 1.8 collective-permute-start.5
  19.0 8.7 %shard_map.55 = (bf16[4,64,4096]{2,1,0:T(8,128)(2,1)}, bf16[4,64,4096]{2,1,0:T(8,128)(2,1)}, bf16[4,64,4096]{2,1,0:T(8,128)(2,1)}, bf16[4,64,4096]{2,1,0:T(8,128)(2,1)}, bf16[4,64,4096]{2,1,0:T(8,128)(2,1)}) custom-call(s32[20]{0:T(128)} %concatenate.16.index_ref, bf16[8,128,4096]{2,1,0:T(8,128)(2,1)} %bitcast.27), custom_call_target="tpu_custom_call" | custom-call | flops 1 | bytes 1 | tf_op jit(solution)/shard_map/pallas_call | solution.py:63
  27.7 16.0 %shard_map.56.left_ref = bf16[4,4096,256]{2,1,0:T(8,128)(2,1)} custom-call(bf16[1024,4096]{1,0:T(8,128)(2,1)} %bitcast.28, bf16[64,64]{1,0:T(8,128)(2,1)} %bitcast.29, bf16[64,64]{1,0:T(8,128)(2,1)} %bitcast.30), custom_call_target="tpu_custom_call" | custom-call | flops 1 | bytes 1 | tf_op jit(solution)/shard_map/pallas_call | solution.py:162
  43.7 0.9 collective-permute-start.1
  44.6 13.1 %collective-permute-start.2 = (bf16[4,64,4096]{2,1,0:T(8,128)(2,1)}, bf16[4,64,4096]{2,1,0:T(8,128)(2,1)}, u32[]{:S(2)}, u32[]{:S(2)}) collective-permute-start(bf16[4,64,4096]{2,1,0:T(8,128)(2,1)} %get-tuple-element.65), channel_id=1, source_target_pairs={{0,64},{1,17},{2,66},{3,19},{4,68},{5,21},{6,70},{7,23},{8,72},{9,... | collective-permute-start | bytes 6291464 | tf_op jit(solution)/shard_map/ppermute | solution.py:330
  57.6 2.6 %collective-permute-start.3 = (bf16[4,64,4096]{2,1,0:T(8,128)(2,1)}, bf16[4,64,4096]{2,1,0:T(8,128)(2,1)}, u32[]{:S(2)}, u32[]{:S(2)}) collective-permute-start(bf16[4,64,4096]{2,1,0:T(8,128)(2,1)} %get-tuple-element.66), channel_id=1, source_target_pairs={{0,96},{1,25},{2,98},{3,27},{4,100},{5,29},{6,102},{7,31},{8,104},... | collective-permute-start | bytes 6291464 | tf_op jit(solution)/shard_map/ppermute | solution.py:330
  60.3 0.0 collective-permute-done.4.refs_2_
  60.3 0.0 copy-start.11
  60.3 5.5 %shard_map.60 = (bf16[4,64,4096]{2,1,0:T(8,128)(2,1)}, bf16[4,64,4096]{2,1,0:T(8,128)(2,1)}, bf16[4,64,4096]{2,1,0:T(8,128)(2,1)}) custom-call(bf16[4,64,4096]{2,1,0:T(8,128)(2,1)} %get-tuple-element.67.refs_0_, bf16[4,64,4096]{2,1,0:T(8,128)(2,1)} %copy-done.5, bf16[4,64,4096]{2,1,0:T(8,128)(2,1)} %collective-permute-done.4.refs_2_, ...), custom_call_target="tpu_custom_call" | custom-call | flops 1 | bytes 1 | tf_op jit(solution)/shard_map/pallas_call | solution.py:89
  65.8 13.1 %collective-permute-done.1.refs_1_ = bf16[4,64,4096]{2,1,0:T(8,128)(2,1)} collective-permute-done((bf16[4,64,4096]{2,1,0:T(8,128)(2,1)}, bf16[4,64,4096]{2,1,0:T(8,128)(2,1)}, u32[]{:S(2)}, u32[]{:S(2)}) %collective-permute-start.1) | collective-permute-done | bytes 2097184 | tf_op jit(solution)/shard_map/ppermute | solution.py:330
  78.8 1.9 collective-permute-start.6
  80.8 1.3 collective-permute-start.7
  82.1 1.8 collective-permute-start.8
  83.9 0.1 squeeze.38
  84.0 0.1 sub.60
  84.1 3.4 %copy-done.2 = bf16[4,4096,256]{2,1,0:T(8,128)(2,1)S(1)} copy-done((bf16[4,4096,256]{2,1,0:T(8,128)(2,1)S(1)}, bf16[4,4096,256]{2,1,0:T(8,128)(2,1)}, u32[]{:S(2)}) %copy-start.2) | copy-done | bytes 8388632
  87.5 1.6 copy-done.6
  89.1 1.6 copy-done.7
  90.7 5.3 %shard_map.61.early_ref = f32[8,256,128]{2,1,0:T(8,128)S(1)} custom-call(bf16[4,4096,256]{2,1,0:T(8,128)(2,1)S(1)} %copy-done.2, bf16[4,64,4096]{2,1,0:T(8,128)(2,1)S(1)} %copy-done.7, bf16[4,64,4096]{2,1,0:T(8,128)(2,1)S(1)} %copy-done.6, bf16[4,64,4096]{2,1,0:T(8,128)(2,1)} %collective-permute-done.4.refs_2_, ...), custom_call_target="tpu_custom_call" | custom-call | flops 1 | bytes 1 | tf_op jit(solution)/shard_map/pallas_call | solution.py:215
  96.0 29.8 %collective-permute-done.2.refs_2_ = bf16[4,64,4096]{2,1,0:T(8,128)(2,1)} collective-permute-done((bf16[4,64,4096]{2,1,0:T(8,128)(2,1)}, bf16[4,64,4096]{2,1,0:T(8,128)(2,1)}, u32[]{:S(2)}, u32[]{:S(2)}) %collective-permute-start.2) | collective-permute-done | bytes 2097184 | tf_op jit(solution)/shard_map/ppermute | solution.py:330
  125.8 1.7 collective-permute-done.3.refs_3_
  127.6 5.5 %shard_map.62 = (bf16[4,64,4096]{2,1,0:T(8,128)(2,1)}, bf16[4,64,4096]{2,1,0:T(8,128)(2,1)}, bf16[4,64,4096]{2,1,0:T(8,128)(2,1)}) custom-call(bf16[4,64,4096]{2,1,0:T(8,128)(2,1)} %get-tuple-element.86.refs_0_, bf16[4,64,4096]{2,1,0:T(8,128)(2,1)} %collective-permute-done.1.refs_1_, bf16[4,64,4096]{2,1,0:T(8,128)(2,1)} %collective-permute-done.2.refs_2_, ...), custom_call_target="tpu_custom_call" | custom-call | flops 1 | bytes 1 | tf_op jit(solution)/shard_map/pallas_call | solution.py:89
  133.1 4.6 %collective-permute-start.14 = (bf16[4,64,4096]{2,1,0:T(8,128)(2,1)}, bf16[4,64,4096]{2,1,0:T(8,128)(2,1)}, u32[]{:S(2)}, u32[]{:S(2)}) collective-permute-start(bf16[4,64,4096]{2,1,0:T(8,128)(2,1)} %get-tuple-element.100), channel_id=1, source_target_pairs={{0,24},{1,97},{2,26},{3,99},{4,28},{5,101},{6,30},{7,103},{8,0},{9... | collective-permute-start | bytes 6291464 | tf_op jit(solution)/shard_map/ppermute | solution.py:330
  137.7 0.4 collective-permute-start.15
  138.1 1.2 collective-permute-start.13
  139.3 0.1 mul.24.row_ref
  139.4 0.1 squeeze.39.block_ref
  139.5 3.4 %copy-done.3 = bf16[4,4096,256]{2,1,0:T(8,128)(2,1)S(1)} copy-done((bf16[4,4096,256]{2,1,0:T(8,128)(2,1)S(1)}, bf16[4,4096,256]{2,1,0:T(8,128)(2,1)}, u32[]{:S(2)}) %copy-start.3) | copy-done | bytes 8388632
  142.9 5.6 %shard_map.63.early_ref = f32[8,256,128]{2,1,0:T(8,128)S(1)} custom-call(bf16[4,4096,256]{2,1,0:T(8,128)(2,1)S(1)} %copy-done.3, bf16[4,64,4096]{2,1,0:T(8,128)(2,1)S(1)} %copy-done.4, bf16[4,64,4096]{2,1,0:T(8,128)(2,1)} %collective-permute-done.1.refs_1_, bf16[4,64,4096]{2,1,0:T(8,128)(2,1)} %collective-permute-done.2.refs_2_, ...), custom_call_target="tpu_custom_call" | custom-call | flops 1 | bytes 1 | tf_op jit(solution)/shard_map/pallas_call | solution.py:215
  148.6 11.5 %shard_map.64 = (f32[32,64,128]{2,1,0:T(8,128)S(1)}, f32[32,64,128]{2,1,0:T(8,128)S(1)}) custom-call(s32[64]{0:T(128)S(1)} %squeeze.39.block_ref, s32[64]{0:T(128)S(1)} %mul.24.row_ref, bf16[4,4096,256]{2,1,0:T(8,128)(2,1)S(1)} %copy-done.3, f32[8,256,128]{2,1,0:T(8,128)S(1)} %shard_map.61.early_ref, bf16[256,4096]{1,0:T(8,128)(2,1)} %bitcast.10.refs_0_, ...), custom_call_target="tpu_custom_call" | custom-call | flops 1 | bytes 1 | tf_op jit(solution)/shard_map/pallas_call | solution.py:262
  160.0 12.6 %collective-permute-start.9 = (f32[32,64,128]{2,1,0:T(8,128)S(1)}, f32[32,64,128]{2,1,0:T(8,128)S(1)}, u32[]{:S(2)}, u32[]{:S(2)}) collective-permute-start(f32[32,64,128]{2,1,0:T(8,128)S(1)} %get-tuple-element.94), channel_id=1, source_target_pairs={{0,1},{1,0},{2,3},{3,2},{4,5},{5,4},{6,7},{7,6},{8,9},{9,8},{10,11... | collective-permute-start | bytes 3145736 | tf_op jit(solution)/shard_map/ppermute | solution.py:334
  172.6 2.3 %collective-permute-done.9.got_ref = f32[32,64,128]{2,1,0:T(8,128)S(1)} collective-permute-done((f32[32,64,128]{2,1,0:T(8,128)S(1)}, f32[32,64,128]{2,1,0:T(8,128)S(1)}, u32[]{:S(2)}, u32[]{:S(2)}) %collective-permute-start.9) | collective-permute-done | bytes 1048608 | tf_op jit(solution)/shard_map/ppermute | solution.py:334
  174.9 0.1 shard_map.65
  175.0 2.0 collective-permute-start.10
  177.0 3.6 %collective-permute-start.11 = (bf16[8,64,128]{2,1,0:T(8,128)(2,1)S(1)}, bf16[8,64,128]{2,1,0:T(8,128)(2,1)S(1)}, u32[]{:S(2)}, u32[]{:S(2)}) collective-permute-start(bf16[8,64,128]{2,1,0:T(8,128)(2,1)S(1)} %get-tuple-element.97), channel_id=1, source_target_pairs={{0,4},{1,5},{2,6},{3,7},{4,0},{5,1},{6,2},{7,3},{8,12},{9,13},{10,... | collective-permute-start | bytes 393224 | tf_op jit(solution)/shard_map/ppermute | solution.py:339
  180.6 2.6 %collective-permute-done.10.refs_1_ = bf16[8,64,128]{2,1,0:T(8,128)(2,1)S(1)} collective-permute-done((bf16[8,64,128]{2,1,0:T(8,128)(2,1)S(1)}, bf16[8,64,128]{2,1,0:T(8,128)(2,1)S(1)}, u32[]{:S(2)}, u32[]{:S(2)}) %collective-permute-start.10) | collective-permute-done | bytes 131104 | tf_op jit(solution)/shard_map/ppermute | solution.py:339
  183.2 2.3 %collective-permute-start.12 = (bf16[8,64,128]{2,1,0:T(8,128)(2,1)S(1)}, bf16[8,64,128]{2,1,0:T(8,128)(2,1)S(1)}, u32[]{:S(2)}, u32[]{:S(2)}) collective-permute-start(bf16[8,64,128]{2,1,0:T(8,128)(2,1)S(1)} %get-tuple-element.98), channel_id=1, source_target_pairs={{0,6},{1,7},{2,0},{3,1},{4,2},{5,3},{6,4},{7,5},{8,14},{9,15},{10,... | collective-permute-start | bytes 393224 | tf_op jit(solution)/shard_map/ppermute | solution.py:339
  185.5 1.7 collective-permute-done.11.refs_2_
  187.2 1.3 collective-permute-done.12.refs_3_
  188.5 1.7 collective-permute-done.13
  190.2 11.1 %shard_map.66 = (f32[32,64,128]{2,1,0:T(8,128)S(1)}, f32[32,64,128]{2,1,0:T(8,128)S(1)}) custom-call(s32[64]{0:T(128)S(1)} %squeeze.39.block_ref, s32[64]{0:T(128)S(1)} %mul.24.row_ref, bf16[4,4096,256]{2,1,0:T(8,128)(2,1)S(1)} %bitcast.23, f32[8,256,128]{2,1,0:T(8,128)S(1)} %shard_map.63.early_ref, bf16[256,4096]{1,0:T(8,128)(2,1)} %bitcast.13.refs_0_, ...), custom_call_target="tpu_custom_call" | custom-call | flops 1 | bytes 1 | tf_op jit(solution)/shard_map/pallas_call | solution.py:262
  201.4 7.0 %collective-permute-start.16 = (f32[32,64,128]{2,1,0:T(8,128)S(1)}, f32[32,64,128]{2,1,0:T(8,128)S(1)}, u32[]{:S(2)}, u32[]{:S(2)}) collective-permute-start(f32[32,64,128]{2,1,0:T(8,128)S(1)} %get-tuple-element.106), channel_id=1, source_target_pairs={{0,1},{1,0},{2,3},{3,2},{4,5},{5,4},{6,7},{7,6},{8,9},{9,8},{10,11... | collective-permute-start | bytes 3145736 | tf_op jit(solution)/shard_map/ppermute | solution.py:334
  208.4 2.3 %collective-permute-done.16.got_ref = f32[32,64,128]{2,1,0:T(8,128)S(1)} collective-permute-done((f32[32,64,128]{2,1,0:T(8,128)S(1)}, f32[32,64,128]{2,1,0:T(8,128)S(1)}, u32[]{:S(2)}, u32[]{:S(2)}) %collective-permute-start.16) | collective-permute-done | bytes 1048608 | tf_op jit(solution)/shard_map/ppermute | solution.py:334
  210.7 0.1 shard_map.67
  210.8 2.0 collective-permute-start.17
  212.8 3.6 %collective-permute-start.18 = (bf16[8,64,128]{2,1,0:T(8,128)(2,1)S(1)}, bf16[8,64,128]{2,1,0:T(8,128)(2,1)S(1)}, u32[]{:S(2)}, u32[]{:S(2)}) collective-permute-start(bf16[8,64,128]{2,1,0:T(8,128)(2,1)S(1)} %get-tuple-element.109), channel_id=1, source_target_pairs={{0,4},{1,5},{2,6},{3,7},{4,0},{5,1},{6,2},{7,3},{8,12},{9,13},{10,... | collective-permute-start | bytes 393224 | tf_op jit(solution)/shard_map/ppermute | solution.py:339
  216.4 1.0 collective-permute-start.19
  217.4 1.6 collective-permute-done.17.refs_5_
  218.9 4.0 %collective-permute-done.18.refs_6_ = bf16[8,64,128]{2,1,0:T(8,128)(2,1)S(1)} collective-permute-done((bf16[8,64,128]{2,1,0:T(8,128)(2,1)S(1)}, bf16[8,64,128]{2,1,0:T(8,128)(2,1)S(1)}, u32[]{:S(2)}, u32[]{:S(2)}) %collective-permute-start.18) | collective-permute-done | bytes 131104 | tf_op jit(solution)/shard_map/ppermute | solution.py:339
  222.9 1.0 shard_map.68
  (37 shorter events, 0.1 us)
Async XLA Ops:
  0.0 0.7 copy-start
  5.4 38.3 %collective-permute-start = (bf16[4,64,4096]{2,1,0:T(8,128)(2,1)}, bf16[4,64,4096]{2,1,0:T(8,128)(2,1)S(1)}, u32[]{:S(2)}, u32[]{:S(2)}) collective-permute-start(bf16[4,64,4096]{2,1,0:T(8,128)(2,1)} %shard_map.57), channel_id=1, source_target_pairs={{0,32},{1,9},{2,34},{3,11},{4,36},{5,13},{6,38},{7,15},{8,40},{9,1... | collective-permute-start | bytes 6291464 | tf_op jit(solution)/shard_map/ppermute | solution.py:330
  10.9 49.4 %collective-permute-start.4 = (bf16[4,64,4096]{2,1,0:T(8,128)(2,1)}, bf16[4,64,4096]{2,1,0:T(8,128)(2,1)}, u32[]{:S(2)}, u32[]{:S(2)}) collective-permute-start(bf16[4,64,4096]{2,1,0:T(8,128)(2,1)} %shard_map.58), channel_id=1, source_target_pairs={{0,64},{1,17},{2,66},{3,19},{4,68},{5,21},{6,70},{7,23},{8,72},{9,... | collective-permute-start | bytes 6291464 | tf_op jit(solution)/shard_map/ppermute | solution.py:330
  12.8 3.7 %copy-start.8 = (s32[4]{0:T(128)S(1)}, s32[4]{0:T(128)}, u32[]{:S(2)}) copy-start(s32[4]{0:T(128)} %get-tuple-element.115.index_ref) | copy-start | bytes 52
  12.8 3.7 %copy-start.9 = (s32[4]{0:T(128)S(1)}, s32[4]{0:T(128)}, u32[]{:S(2)}) copy-start(s32[4]{0:T(128)} %get-tuple-element.116.index_ref) | copy-start | bytes 52
  12.8 3.7 %copy-start.10 = (s32[4]{0:T(128)S(1)}, s32[4]{0:T(128)}, u32[]{:S(2)}) copy-start(s32[4]{0:T(128)} %get-tuple-element.117.index_ref) | copy-start | bytes 52
  17.2 43.1 %collective-permute-start.5 = (bf16[4,64,4096]{2,1,0:T(8,128)(2,1)}, bf16[4,64,4096]{2,1,0:T(8,128)(2,1)}, u32[]{:S(2)}, u32[]{:S(2)}) collective-permute-start(bf16[4,64,4096]{2,1,0:T(8,128)(2,1)} %shard_map.59), channel_id=1, source_target_pairs={{0,96},{1,25},{2,98},{3,27},{4,100},{5,29},{6,102},{7,31},{8,104},... | collective-permute-start | bytes 6291464 | tf_op jit(solution)/shard_map/ppermute | solution.py:330
  43.7 16.6 %copy-start.5 = (bf16[4,64,4096]{2,1,0:T(8,128)(2,1)}, bf16[4,64,4096]{2,1,0:T(8,128)(2,1)S(1)}, u32[]{:S(2)}) copy-start(bf16[4,64,4096]{2,1,0:T(8,128)(2,1)S(1)} %collective-permute-done.refs_1_) | copy-start | bytes 6291460
  43.7 35.1 %collective-permute-start.1 = (bf16[4,64,4096]{2,1,0:T(8,128)(2,1)}, bf16[4,64,4096]{2,1,0:T(8,128)(2,1)}, u32[]{:S(2)}, u32[]{:S(2)}) collective-permute-start(bf16[4,64,4096]{2,1,0:T(8,128)(2,1)} %get-tuple-element.64), channel_id=1, source_target_pairs={{0,32},{1,9},{2,34},{3,11},{4,36},{5,13},{6,38},{7,15},{8,40},{9,1... | collective-permute-start | bytes 6291464 | tf_op jit(solution)/shard_map/ppermute | solution.py:330
  44.6 81.3 %collective-permute-start.2 = (bf16[4,64,4096]{2,1,0:T(8,128)(2,1)}, bf16[4,64,4096]{2,1,0:T(8,128)(2,1)}, u32[]{:S(2)}, u32[]{:S(2)}) collective-permute-start(bf16[4,64,4096]{2,1,0:T(8,128)(2,1)} %get-tuple-element.65), channel_id=1, source_target_pairs={{0,64},{1,17},{2,66},{3,19},{4,68},{5,21},{6,70},{7,23},{8,72},{9,... | collective-permute-start | bytes 6291464 | tf_op jit(solution)/shard_map/ppermute | solution.py:330
  57.6 70.0 %collective-permute-start.3 = (bf16[4,64,4096]{2,1,0:T(8,128)(2,1)}, bf16[4,64,4096]{2,1,0:T(8,128)(2,1)}, u32[]{:S(2)}, u32[]{:S(2)}) collective-permute-start(bf16[4,64,4096]{2,1,0:T(8,128)(2,1)} %get-tuple-element.66), channel_id=1, source_target_pairs={{0,96},{1,25},{2,98},{3,27},{4,100},{5,29},{6,102},{7,31},{8,104},... | collective-permute-start | bytes 6291464 | tf_op jit(solution)/shard_map/ppermute | solution.py:330
  60.3 23.6 %copy-start.11 = (s32[64,2]{0,1:T(2,128)S(1)}, s32[64,2]{0,1:T(2,128)}, u32[]{:S(2)}) copy-start(s32[64,2]{0,1:T(2,128)} %param.9) | copy-start | bytes 1540
  78.8 54.2 %collective-permute-start.6 = (bf16[4,64,4096]{2,1,0:T(8,128)(2,1)}, bf16[4,64,4096]{2,1,0:T(8,128)(2,1)}, u32[]{:S(2)}, u32[]{:S(2)}) collective-permute-start(bf16[4,64,4096]{2,1,0:T(8,128)(2,1)} %get-tuple-element.80), channel_id=1, source_target_pairs={{0,8},{1,33},{2,10},{3,35},{4,12},{5,37},{6,14},{7,39},{8,16},{9,4... | collective-permute-start | bytes 6291464 | tf_op jit(solution)/shard_map/ppermute | solution.py:330
  80.8 67.8 %collective-permute-start.7 = (bf16[4,64,4096]{2,1,0:T(8,128)(2,1)}, bf16[4,64,4096]{2,1,0:T(8,128)(2,1)}, u32[]{:S(2)}, u32[]{:S(2)}) collective-permute-start(bf16[4,64,4096]{2,1,0:T(8,128)(2,1)} %get-tuple-element.81), channel_id=1, source_target_pairs={{0,24},{1,97},{2,26},{3,99},{4,28},{5,101},{6,30},{7,103},{8,0},{9... | collective-permute-start | bytes 6291464 | tf_op jit(solution)/shard_map/ppermute | solution.py:330
  82.1 66.4 %collective-permute-start.8 = (bf16[4,64,4096]{2,1,0:T(8,128)(2,1)}, bf16[4,64,4096]{2,1,0:T(8,128)(2,1)}, u32[]{:S(2)}, u32[]{:S(2)}) collective-permute-start(bf16[4,64,4096]{2,1,0:T(8,128)(2,1)} %get-tuple-element.82), channel_id=1, source_target_pairs={{0,16},{1,65},{2,18},{3,67},{4,20},{5,69},{6,22},{7,71},{8,24},{9,... | collective-permute-start | bytes 6291464 | tf_op jit(solution)/shard_map/ppermute | solution.py:330
  84.1 3.4 %copy-start.2 = (bf16[4,4096,256]{2,1,0:T(8,128)(2,1)S(1)}, bf16[4,4096,256]{2,1,0:T(8,128)(2,1)}, u32[]{:S(2)}) copy-start(bf16[4,4096,256]{2,1,0:T(8,128)(2,1)} %shard_map.56.left_ref) | copy-start | bytes 25165828
  87.5 1.6 copy-start.6
  89.1 1.6 copy-start.7
  96.0 43.5 %copy-start.4 = (bf16[4,64,4096]{2,1,0:T(8,128)(2,1)S(1)}, bf16[4,64,4096]{2,1,0:T(8,128)(2,1)}, u32[]{:S(2)}) copy-start(bf16[4,64,4096]{2,1,0:T(8,128)(2,1)} %get-tuple-element.86.refs_0_) | copy-start | bytes 6291460
  133.1 55.4 %collective-permute-start.14 = (bf16[4,64,4096]{2,1,0:T(8,128)(2,1)}, bf16[4,64,4096]{2,1,0:T(8,128)(2,1)}, u32[]{:S(2)}, u32[]{:S(2)}) collective-permute-start(bf16[4,64,4096]{2,1,0:T(8,128)(2,1)} %get-tuple-element.100), channel_id=1, source_target_pairs={{0,24},{1,97},{2,26},{3,99},{4,28},{5,101},{6,30},{7,103},{8,0},{9... | collective-permute-start | bytes 6291464 | tf_op jit(solution)/shard_map/ppermute | solution.py:330
  137.7 50.8 %collective-permute-start.15 = (bf16[4,64,4096]{2,1,0:T(8,128)(2,1)}, bf16[4,64,4096]{2,1,0:T(8,128)(2,1)}, u32[]{:S(2)}, u32[]{:S(2)}) collective-permute-start(bf16[4,64,4096]{2,1,0:T(8,128)(2,1)} %get-tuple-element.101), channel_id=1, source_target_pairs={{0,16},{1,65},{2,18},{3,67},{4,20},{5,69},{6,22},{7,71},{8,24},{9,... | collective-permute-start | bytes 6291464 | tf_op jit(solution)/shard_map/ppermute | solution.py:330
  138.1 52.1 %collective-permute-start.13 = (bf16[4,64,4096]{2,1,0:T(8,128)(2,1)}, bf16[4,64,4096]{2,1,0:T(8,128)(2,1)}, u32[]{:S(2)}, u32[]{:S(2)}) collective-permute-start(bf16[4,64,4096]{2,1,0:T(8,128)(2,1)} %get-tuple-element.99), channel_id=1, source_target_pairs={{0,8},{1,33},{2,10},{3,35},{4,12},{5,37},{6,14},{7,39},{8,16},{9,4... | collective-permute-start | bytes 6291464 | tf_op jit(solution)/shard_map/ppermute | solution.py:330
  139.5 3.4 %copy-start.3 = (bf16[4,4096,256]{2,1,0:T(8,128)(2,1)S(1)}, bf16[4,4096,256]{2,1,0:T(8,128)(2,1)}, u32[]{:S(2)}) copy-start(bf16[4,4096,256]{2,1,0:T(8,128)(2,1)} %shard_map.56.left_ref) | copy-start | bytes 25165828
  148.5 41.7 %slice-start = ((s8[8388608]{0:T(1024)(128)(4,1)}), s8[4194304]{0:T(1024)(128)(4,1)S(1)}, s32[]{:S(2)}) async-start(s8[8388608]{0:T(1024)(128)(4,1)} %bitcast.22), calls=%async_computation | async-start | bytes 8388608
  148.5 41.7 %slice-start.1 = ((s8[8388608]{0:T(1024)(128)(4,1)}), s8[4194304]{0:T(1024)(128)(4,1)S(1)}, s32[]{:S(2)}) async-start(s8[8388608]{0:T(1024)(128)(4,1)} %bitcast.22), calls=%async_computation.1 | async-start | bytes 8388608
  160.0 14.9 %collective-permute-start.9 = (f32[32,64,128]{2,1,0:T(8,128)S(1)}, f32[32,64,128]{2,1,0:T(8,128)S(1)}, u32[]{:S(2)}, u32[]{:S(2)}) collective-permute-start(f32[32,64,128]{2,1,0:T(8,128)S(1)} %get-tuple-element.94), channel_id=1, source_target_pairs={{0,1},{1,0},{2,3},{3,2},{4,5},{5,4},{6,7},{7,6},{8,9},{9,8},{10,11... | collective-permute-start | bytes 3145736 | tf_op jit(solution)/shard_map/ppermute | solution.py:334
  175.0 8.1 %collective-permute-start.10 = (bf16[8,64,128]{2,1,0:T(8,128)(2,1)S(1)}, bf16[8,64,128]{2,1,0:T(8,128)(2,1)S(1)}, u32[]{:S(2)}, u32[]{:S(2)}) collective-permute-start(bf16[8,64,128]{2,1,0:T(8,128)(2,1)S(1)} %get-tuple-element.96), channel_id=1, source_target_pairs={{0,2},{1,3},{2,4},{3,5},{4,6},{5,7},{6,0},{7,1},{8,10},{9,11},{10,... | collective-permute-start | bytes 393224 | tf_op jit(solution)/shard_map/ppermute | solution.py:339
  177.0 10.1 %collective-permute-start.11 = (bf16[8,64,128]{2,1,0:T(8,128)(2,1)S(1)}, bf16[8,64,128]{2,1,0:T(8,128)(2,1)S(1)}, u32[]{:S(2)}, u32[]{:S(2)}) collective-permute-start(bf16[8,64,128]{2,1,0:T(8,128)(2,1)S(1)} %get-tuple-element.97), channel_id=1, source_target_pairs={{0,4},{1,5},{2,6},{3,7},{4,0},{5,1},{6,2},{7,3},{8,12},{9,13},{10,... | collective-permute-start | bytes 393224 | tf_op jit(solution)/shard_map/ppermute | solution.py:339
  183.2 5.3 %collective-permute-start.12 = (bf16[8,64,128]{2,1,0:T(8,128)(2,1)S(1)}, bf16[8,64,128]{2,1,0:T(8,128)(2,1)S(1)}, u32[]{:S(2)}, u32[]{:S(2)}) collective-permute-start(bf16[8,64,128]{2,1,0:T(8,128)(2,1)S(1)} %get-tuple-element.98), channel_id=1, source_target_pairs={{0,6},{1,7},{2,0},{3,1},{4,2},{5,3},{6,4},{7,5},{8,14},{9,15},{10,... | collective-permute-start | bytes 393224 | tf_op jit(solution)/shard_map/ppermute | solution.py:339
  190.2 33.7 %copy-start.1 = (s32[16,16]{1,0:T(8,128)S(1)}, s32[16,16]{1,0:T(8,128)}, u32[]{:S(2)}) copy-start(s32[16,16]{1,0:T(8,128)} %param.8) | copy-start | bytes 3076
  201.4 9.3 %collective-permute-start.16 = (f32[32,64,128]{2,1,0:T(8,128)S(1)}, f32[32,64,128]{2,1,0:T(8,128)S(1)}, u32[]{:S(2)}, u32[]{:S(2)}) collective-permute-start(f32[32,64,128]{2,1,0:T(8,128)S(1)} %get-tuple-element.106), channel_id=1, source_target_pairs={{0,1},{1,0},{2,3},{3,2},{4,5},{5,4},{6,7},{7,6},{8,9},{9,8},{10,11... | collective-permute-start | bytes 3145736 | tf_op jit(solution)/shard_map/ppermute | solution.py:334
  210.8 8.1 %collective-permute-start.17 = (bf16[8,64,128]{2,1,0:T(8,128)(2,1)S(1)}, bf16[8,64,128]{2,1,0:T(8,128)(2,1)S(1)}, u32[]{:S(2)}, u32[]{:S(2)}) collective-permute-start(bf16[8,64,128]{2,1,0:T(8,128)(2,1)S(1)} %get-tuple-element.108), channel_id=1, source_target_pairs={{0,2},{1,3},{2,4},{3,5},{4,6},{5,7},{6,0},{7,1},{8,10},{9,11},{10,... | collective-permute-start | bytes 393224 | tf_op jit(solution)/shard_map/ppermute | solution.py:339
  212.8 10.1 %collective-permute-start.18 = (bf16[8,64,128]{2,1,0:T(8,128)(2,1)S(1)}, bf16[8,64,128]{2,1,0:T(8,128)(2,1)S(1)}, u32[]{:S(2)}, u32[]{:S(2)}) collective-permute-start(bf16[8,64,128]{2,1,0:T(8,128)(2,1)S(1)} %get-tuple-element.109), channel_id=1, source_target_pairs={{0,4},{1,5},{2,6},{3,7},{4,0},{5,1},{6,2},{7,3},{8,12},{9,13},{10,... | collective-permute-start | bytes 393224 | tf_op jit(solution)/shard_map/ppermute | solution.py:339
  216.4 6.5 %collective-permute-start.19 = (bf16[8,64,128]{2,1,0:T(8,128)(2,1)S(1)}, bf16[8,64,128]{2,1,0:T(8,128)(2,1)S(1)}, u32[]{:S(2)}, u32[]{:S(2)}) collective-permute-start(bf16[8,64,128]{2,1,0:T(8,128)(2,1)S(1)} %get-tuple-element.110), channel_id=1, source_target_pairs={{0,6},{1,7},{2,0},{3,1},{4,2},{5,3},{6,4},{7,5},{8,14},{9,15},{10,... | collective-permute-start | bytes 393224 | tf_op jit(solution)/shard_map/ppermute | solution.py:339

commit v8 on v7

--- a/solution.py
+++ b/solution.py
@@ -10,7 +10,7 @@
 BLOCK = 128
 SIDE = 4
 PARTS = ((0, 64), (64, 64))
-STEP = 256
+STEP = 512
 VMEM = 60 * 2**20
 bf16, f32 = jnp.bfloat16, jnp.float32
 BRIEF = pl.CostEstimate(flops=1, bytes_accessed=1, transcendentals=0)

time: 225 us -> 229 us (1.018)
  the two profiles are of different devices: /device:TPU:0 before, /device:TPU:4 now
where the time goes in v8:
time: 229 us; the launch traced here: 231 us
  Pallas kernels  76.7 us (33%)
  waiting for transfers between devices  74.7 us (33%)
  starting transfers between devices  66.2 us (29%)
  local copies, waits for them, and re-layouts  12.6 us (6%)
    ppermute x12, waiting for transfers between devices, shift(): return lax.ppermute(array, ('ex', 'lay'), pairs)  59.1 us
    ppermute x12, starting transfers between devices, shift(): return lax.ppermute(array, ('ex', 'lay'), pairs)  26.2 us
    ppermute x2, starting transfers between devices, swap_cores(): return lax.ppermute(array, 'lay', [(i, i ^ 1) for i in range(2 * SIDE)])  25.5 us
    pallas_call x2, Pallas kernels, tiles(): pl.pallas_call(functools.partial(tiles_kernel, len(rights)), out_shape=(o...  19.4 us
    pallas_call x4, Pallas kernels, gather(): pl.pallas_call(functools.partial(gather_kernel, [start for _, start, _ in...  18.7 us
    pallas_call x1, Pallas kernels, left_transposed(): pl.pallas_call(left_kernel, out_shape=jax.ShapeDtypeStruct((examples // t...  16.8 us
    ppermute x6, starting transfers between devices, shift_z(): return lax.ppermute(array, 'lay', pairs)  14.5 us
    ppermute x6, waiting for transfers between devices, shift_z(): return lax.ppermute(array, 'lay', pairs)  11 us
  transfers between devices with their start and end apart: 20, of which 10 were waited for; matrix products, arithmetic and copies ran while one was open for 0% of the time, Pallas kernels for 27%

profile of v8, /device:TPU:4, one launch (start us, length us, event | category | flops | bytes accessed | tf_op | source)
XLA Modules:
  0.0 230.7 jit_solution(11870370035486107916)
XLA Ops:
  0.0 0.7 copy-done
  0.7 0.2 dynamic-slice_reduce_fusion
  0.9 0.1 reshape.249
  1.0 0.1 add_add_fusion
  1.0 0.1 dynamic_slice.12
  1.1 0.1 copy.17
  1.2 0.1 bitcast_select_fusion
  1.3 0.5 slice_bitcast_fusion
  1.8 3.1 %shard_map.57 = bf16[4,64,4096]{2,1,0:T(8,128)(2,1)} custom-call(s32[4]{0:T(128)} %get-tuple-element.117.index_ref, bf16[8,128,4096]{2,1,0:T(8,128)(2,1)} %bitcast.24), custom_call_target="tpu_custom_call" | custom-call | flops 1 | bytes 1 | tf_op jit(solution)/shard_map/pallas_call | solution.py:63
  5.0 1.6 collective-permute-start
  6.6 3.2 %shard_map.58 = bf16[4,64,4096]{2,1,0:T(8,128)(2,1)} custom-call(s32[4]{0:T(128)} %get-tuple-element.116.index_ref, bf16[8,128,4096]{2,1,0:T(8,128)(2,1)} %bitcast.25), custom_call_target="tpu_custom_call" | custom-call | flops 1 | bytes 1 | tf_op jit(solution)/shard_map/pallas_call | solution.py:63
  9.8 3.2 %collective-permute-start.4 = (bf16[4,64,4096]{2,1,0:T(8,128)(2,1)}, bf16[4,64,4096]{2,1,0:T(8,128)(2,1)}, u32[]{:S(2)}, u32[]{:S(2)}) collective-permute-start(bf16[4,64,4096]{2,1,0:T(8,128)(2,1)} %shard_map.58), channel_id=1, source_target_pairs={{0,64},{1,17},{2,66},{3,19},{4,68},{5,21},{6,70},{7,23},{8,72},{9,... | collective-permute-start | bytes 6291464 | tf_op jit(solution)/shard_map/ppermute | solution.py:330
  13.0 3.8 %shard_map.59 = bf16[4,64,4096]{2,1,0:T(8,128)(2,1)} custom-call(s32[4]{0:T(128)} %get-tuple-element.115.index_ref, bf16[8,128,4096]{2,1,0:T(8,128)(2,1)} %bitcast.26), custom_call_target="tpu_custom_call" | custom-call | flops 1 | bytes 1 | tf_op jit(solution)/shard_map/pallas_call | solution.py:63
  16.8 0.6 concatenate.16.index_ref
  17.4 1.6 collective-permute-start.5
  19.0 8.7 %shard_map.55 = (bf16[4,64,4096]{2,1,0:T(8,128)(2,1)}, bf16[4,64,4096]{2,1,0:T(8,128)(2,1)}, bf16[4,64,4096]{2,1,0:T(8,128)(2,1)}, bf16[4,64,4096]{2,1,0:T(8,128)(2,1)}, bf16[4,64,4096]{2,1,0:T(8,128)(2,1)}) custom-call(s32[20]{0:T(128)} %concatenate.16.index_ref, bf16[8,128,4096]{2,1,0:T(8,128)(2,1)} %bitcast.27), custom_call_target="tpu_custom_call" | custom-call | flops 1 | bytes 1 | tf_op jit(solution)/shard_map/pallas_call | solution.py:63
  27.7 16.8 %shard_map.56.left_ref = bf16[2,4096,512]{2,1,0:T(8,128)(2,1)} custom-call(bf16[1024,4096]{1,0:T(8,128)(2,1)} %bitcast.28, bf16[64,64]{1,0:T(8,128)(2,1)} %bitcast.29, bf16[64,64]{1,0:T(8,128)(2,1)} %bitcast.30), custom_call_target="tpu_custom_call" | custom-call | flops 1 | bytes 1 | tf_op jit(solution)/shard_map/pallas_call | solution.py:162
  44.4 10.7 %collective-permute-start.1 = (bf16[4,64,4096]{2,1,0:T(8,128)(2,1)}, bf16[4,64,4096]{2,1,0:T(8,128)(2,1)}, u32[]{:S(2)}, u32[]{:S(2)}) collective-permute-start(bf16[4,64,4096]{2,1,0:T(8,128)(2,1)} %get-tuple-element.64), channel_id=1, source_target_pairs={{0,32},{1,9},{2,34},{3,11},{4,36},{5,13},{6,38},{7,15},{8,40},{9,1... | collective-permute-start | bytes 6291464 | tf_op jit(solution)/shard_map/ppermute | solution.py:330
  55.1 2.4 %collective-permute-start.2 = (bf16[4,64,4096]{2,1,0:T(8,128)(2,1)}, bf16[4,64,4096]{2,1,0:T(8,128)(2,1)}, u32[]{:S(2)}, u32[]{:S(2)}) collective-permute-start(bf16[4,64,4096]{2,1,0:T(8,128)(2,1)} %get-tuple-element.65), channel_id=1, source_target_pairs={{0,64},{1,17},{2,66},{3,19},{4,68},{5,21},{6,70},{7,23},{8,72},{9,... | collective-permute-start | bytes 6291464 | tf_op jit(solution)/shard_map/ppermute | solution.py:330
  57.5 2.6 %collective-permute-start.3 = (bf16[4,64,4096]{2,1,0:T(8,128)(2,1)}, bf16[4,64,4096]{2,1,0:T(8,128)(2,1)}, u32[]{:S(2)}, u32[]{:S(2)}) collective-permute-start(bf16[4,64,4096]{2,1,0:T(8,128)(2,1)} %get-tuple-element.66), channel_id=1, source_target_pairs={{0,96},{1,25},{2,98},{3,27},{4,100},{5,29},{6,102},{7,31},{8,104},... | collective-permute-start | bytes 6291464 | tf_op jit(solution)/shard_map/ppermute | solution.py:330
  60.2 0.0 copy-start.11
  60.2 5.5 %shard_map.60 = (bf16[4,64,4096]{2,1,0:T(8,128)(2,1)}, bf16[4,64,4096]{2,1,0:T(8,128)(2,1)}, bf16[4,64,4096]{2,1,0:T(8,128)(2,1)}) custom-call(bf16[4,64,4096]{2,1,0:T(8,128)(2,1)} %get-tuple-element.67.refs_0_, bf16[4,64,4096]{2,1,0:T(8,128)(2,1)} %copy-done.5, bf16[4,64,4096]{2,1,0:T(8,128)(2,1)} %collective-permute-done.4.refs_2_, ...), custom_call_target="tpu_custom_call" | custom-call | flops 1 | bytes 1 | tf_op jit(solution)/shard_map/pallas_call | solution.py:89
  65.7 15.0 %collective-permute-done.1.refs_1_ = bf16[4,64,4096]{2,1,0:T(8,128)(2,1)} collective-permute-done((bf16[4,64,4096]{2,1,0:T(8,128)(2,1)}, bf16[4,64,4096]{2,1,0:T(8,128)(2,1)}, u32[]{:S(2)}, u32[]{:S(2)}) %collective-permute-start.1) | collective-permute-done | bytes 2097184 | tf_op jit(solution)/shard_map/ppermute | solution.py:330
  80.6 2.0 collective-permute-start.7
  82.7 0.0 collective-permute-start.8
  82.7 0.1 squeeze.38
  82.8 0.1 sub.60
  82.9 3.4 %copy-done.2 = bf16[2,4096,512]{2,1,0:T(8,128)(2,1)S(1)} copy-done((bf16[2,4096,512]{2,1,0:T(8,128)(2,1)S(1)}, bf16[2,4096,512]{2,1,0:T(8,128)(2,1)}, u32[]{:S(2)}) %copy-start.2) | copy-done | bytes 8388632
  86.3 1.6 copy-done.6
  87.9 1.6 copy-done.7
  89.5 4.7 %shard_map.61.early_ref = f32[8,256,128]{2,1,0:T(8,128)S(1)} custom-call(bf16[2,4096,512]{2,1,0:T(8,128)(2,1)S(1)} %copy-done.2, bf16[4,64,4096]{2,1,0:T(8,128)(2,1)S(1)} %copy-done.7, bf16[4,64,4096]{2,1,0:T(8,128)(2,1)S(1)} %copy-done.6, bf16[4,64,4096]{2,1,0:T(8,128)(2,1)} %collective-permute-done.4.refs_2_, ...), custom_call_target="tpu_custom_call" | custom-call | flops 1 | bytes 1 | tf_op jit(solution)/shard_map/pallas_call | solution.py:215
  94.2 31.5 %collective-permute-done.2.refs_2_ = bf16[4,64,4096]{2,1,0:T(8,128)(2,1)} collective-permute-done((bf16[4,64,4096]{2,1,0:T(8,128)(2,1)}, bf16[4,64,4096]{2,1,0:T(8,128)(2,1)}, u32[]{:S(2)}, u32[]{:S(2)}) %collective-permute-start.2) | collective-permute-done | bytes 2097184 | tf_op jit(solution)/shard_map/ppermute | solution.py:330
  125.6 5.5 %shard_map.62 = (bf16[4,64,4096]{2,1,0:T(8,128)(2,1)}, bf16[4,64,4096]{2,1,0:T(8,128)(2,1)}, bf16[4,64,4096]{2,1,0:T(8,128)(2,1)}) custom-call(bf16[4,64,4096]{2,1,0:T(8,128)(2,1)} %get-tuple-element.86.refs_0_, bf16[4,64,4096]{2,1,0:T(8,128)(2,1)} %collective-permute-done.1.refs_1_, bf16[4,64,4096]{2,1,0:T(8,128)(2,1)} %collective-permute-done.2.refs_2_, ...), custom_call_target="tpu_custom_call" | custom-call | flops 1 | bytes 1 | tf_op jit(solution)/shard_map/pallas_call | solution.py:89
  131.1 12.7 %collective-permute-done.6 = bf16[4,64,4096]{2,1,0:T(8,128)(2,1)} collective-permute-done((bf16[4,64,4096]{2,1,0:T(8,128)(2,1)}, bf16[4,64,4096]{2,1,0:T(8,128)(2,1)}, u32[]{:S(2)}, u32[]{:S(2)}) %collective-permute-start.6) | collective-permute-done | bytes 2097184 | tf_op jit(solution)/shard_map/ppermute | solution.py:330
  143.8 0.0 collective-permute-start.14
  143.8 0.0 collective-permute-start.15
  143.8 2.0 collective-permute-start.13
  145.9 0.1 mul.24.row_ref
  146.0 0.1 squeeze.39.block_ref
  146.1 3.4 %copy-done.3 = bf16[2,4096,512]{2,1,0:T(8,128)(2,1)S(1)} copy-done((bf16[2,4096,512]{2,1,0:T(8,128)(2,1)S(1)}, bf16[2,4096,512]{2,1,0:T(8,128)(2,1)}, u32[]{:S(2)}) %copy-start.3) | copy-done | bytes 8388632
  149.5 4.9 %shard_map.63.early_ref = f32[8,256,128]{2,1,0:T(8,128)S(1)} custom-call(bf16[2,4096,512]{2,1,0:T(8,128)(2,1)S(1)} %copy-done.3, bf16[4,64,4096]{2,1,0:T(8,128)(2,1)S(1)} %copy-done.4, bf16[4,64,4096]{2,1,0:T(8,128)(2,1)} %collective-permute-done.1.refs_1_, bf16[4,64,4096]{2,1,0:T(8,128)(2,1)} %collective-permute-done.2.refs_2_, ...), custom_call_target="tpu_custom_call" | custom-call | flops 1 | bytes 1 | tf_op jit(solution)/shard_map/pallas_call | solution.py:215
  154.3 0.0 collective-permute-done.8
  154.4 0.0 slice-start
  154.4 9.9 %shard_map.64 = (f32[32,64,128]{2,1,0:T(8,128)S(1)}, f32[32,64,128]{2,1,0:T(8,128)S(1)}) custom-call(s32[64]{0:T(128)S(1)} %squeeze.39.block_ref, s32[64]{0:T(128)S(1)} %mul.24.row_ref, bf16[2,4096,512]{2,1,0:T(8,128)(2,1)S(1)} %copy-done.3, f32[8,256,128]{2,1,0:T(8,128)S(1)} %shard_map.61.early_ref, bf16[256,4096]{1,0:T(8,128)(2,1)} %bitcast.10.refs_0_, ...), custom_call_target="tpu_custom_call" | custom-call | flops 1 | bytes 1 | tf_op jit(solution)/shard_map/pallas_call | solution.py:262
  164.3 14.4 %collective-permute-start.9 = (f32[32,64,128]{2,1,0:T(8,128)S(1)}, f32[32,64,128]{2,1,0:T(8,128)S(1)}, u32[]{:S(2)}, u32[]{:S(2)}) collective-permute-start(f32[32,64,128]{2,1,0:T(8,128)S(1)} %get-tuple-element.94), channel_id=1, source_target_pairs={{0,1},{1,0},{2,3},{3,2},{4,5},{5,4},{6,7},{7,6},{8,9},{9,8},{10,11... | collective-permute-start | bytes 3145736 | tf_op jit(solution)/shard_map/ppermute | solution.py:334
  178.7 2.3 collective-permute-done.9.got_ref
  181.0 0.1 shard_map.65
  181.1 2.0 collective-permute-start.10
  183.1 3.6 %collective-permute-start.11 = (bf16[8,64,128]{2,1,0:T(8,128)(2,1)S(1)}, bf16[8,64,128]{2,1,0:T(8,128)(2,1)S(1)}, u32[]{:S(2)}, u32[]{:S(2)}) collective-permute-start(bf16[8,64,128]{2,1,0:T(8,128)(2,1)S(1)} %get-tuple-element.97), channel_id=1, source_target_pairs={{0,4},{1,5},{2,6},{3,7},{4,0},{5,1},{6,2},{7,3},{8,12},{9,13},{10,... | collective-permute-start | bytes 393224 | tf_op jit(solution)/shard_map/ppermute | solution.py:339
  186.7 2.6 %collective-permute-done.10.refs_1_ = bf16[8,64,128]{2,1,0:T(8,128)(2,1)S(1)} collective-permute-done((bf16[8,64,128]{2,1,0:T(8,128)(2,1)S(1)}, bf16[8,64,128]{2,1,0:T(8,128)(2,1)S(1)}, u32[]{:S(2)}, u32[]{:S(2)}) %collective-permute-start.10) | collective-permute-done | bytes 131104 | tf_op jit(solution)/shard_map/ppermute | solution.py:339
  189.2 2.3 collective-permute-start.12
  191.5 1.7 collective-permute-done.11.refs_2_
  193.2 1.2 collective-permute-done.12.refs_3_
  194.4 0.0 copy-start.1
  194.5 9.6 %shard_map.66 = (f32[32,64,128]{2,1,0:T(8,128)S(1)}, f32[32,64,128]{2,1,0:T(8,128)S(1)}) custom-call(s32[64]{0:T(128)S(1)} %squeeze.39.block_ref, s32[64]{0:T(128)S(1)} %mul.24.row_ref, bf16[2,4096,512]{2,1,0:T(8,128)(2,1)S(1)} %bitcast.23, f32[8,256,128]{2,1,0:T(8,128)S(1)} %shard_map.63.early_ref, bf16[256,4096]{1,0:T(8,128)(2,1)} %bitcast.13.refs_0_, ...), custom_call_target="tpu_custom_call" | custom-call | flops 1 | bytes 1 | tf_op jit(solution)/shard_map/pallas_call | solution.py:262
  204.0 11.1 %collective-permute-start.16 = (f32[32,64,128]{2,1,0:T(8,128)S(1)}, f32[32,64,128]{2,1,0:T(8,128)S(1)}, u32[]{:S(2)}, u32[]{:S(2)}) collective-permute-start(f32[32,64,128]{2,1,0:T(8,128)S(1)} %get-tuple-element.106), channel_id=1, source_target_pairs={{0,1},{1,0},{2,3},{3,2},{4,5},{5,4},{6,7},{7,6},{8,9},{9,8},{10,11... | collective-permute-start | bytes 3145736 | tf_op jit(solution)/shard_map/ppermute | solution.py:334
  215.2 2.3 collective-permute-done.16.got_ref
  217.4 0.1 shard_map.67
  217.5 2.0 collective-permute-start.17
  219.5 3.6 %collective-permute-start.18 = (bf16[8,64,128]{2,1,0:T(8,128)(2,1)S(1)}, bf16[8,64,128]{2,1,0:T(8,128)(2,1)S(1)}, u32[]{:S(2)}, u32[]{:S(2)}) collective-permute-start(bf16[8,64,128]{2,1,0:T(8,128)(2,1)S(1)} %get-tuple-element.109), channel_id=1, source_target_pairs={{0,4},{1,5},{2,6},{3,7},{4,0},{5,1},{6,2},{7,3},{8,12},{9,13},{10,... | collective-permute-start | bytes 393224 | tf_op jit(solution)/shard_map/ppermute | solution.py:339
  223.1 1.0 collective-permute-start.19
  224.1 1.5 collective-permute-done.17.refs_5_
  225.7 4.0 %collective-permute-done.18.refs_6_ = bf16[8,64,128]{2,1,0:T(8,128)(2,1)S(1)} collective-permute-done((bf16[8,64,128]{2,1,0:T(8,128)(2,1)S(1)}, bf16[8,64,128]{2,1,0:T(8,128)(2,1)S(1)}, u32[]{:S(2)}, u32[]{:S(2)}) %collective-permute-start.18) | collective-permute-done | bytes 131104 | tf_op jit(solution)/shard_map/ppermute | solution.py:339
  229.7 1.0 shard_map.68
  (37 shorter events, 0.1 us)
Async XLA Ops:
  0.0 0.7 copy-start
  5.0 39.5 %collective-permute-start = (bf16[4,64,4096]{2,1,0:T(8,128)(2,1)}, bf16[4,64,4096]{2,1,0:T(8,128)(2,1)S(1)}, u32[]{:S(2)}, u32[]{:S(2)}) collective-permute-start(bf16[4,64,4096]{2,1,0:T(8,128)(2,1)} %shard_map.57), channel_id=1, source_target_pairs={{0,32},{1,9},{2,34},{3,11},{4,36},{5,13},{6,38},{7,15},{8,40},{9,1... | collective-permute-start | bytes 6291464 | tf_op jit(solution)/shard_map/ppermute | solution.py:330
  9.8 50.4 %collective-permute-start.4 = (bf16[4,64,4096]{2,1,0:T(8,128)(2,1)}, bf16[4,64,4096]{2,1,0:T(8,128)(2,1)}, u32[]{:S(2)}, u32[]{:S(2)}) collective-permute-start(bf16[4,64,4096]{2,1,0:T(8,128)(2,1)} %shard_map.58), channel_id=1, source_target_pairs={{0,64},{1,17},{2,66},{3,19},{4,68},{5,21},{6,70},{7,23},{8,72},{9,... | collective-permute-start | bytes 6291464 | tf_op jit(solution)/shard_map/ppermute | solution.py:330
  13.0 3.8 %copy-start.8 = (s32[4]{0:T(128)S(1)}, s32[4]{0:T(128)}, u32[]{:S(2)}) copy-start(s32[4]{0:T(128)} %get-tuple-element.115.index_ref) | copy-start | bytes 52
  13.0 3.8 %copy-start.9 = (s32[4]{0:T(128)S(1)}, s32[4]{0:T(128)}, u32[]{:S(2)}) copy-start(s32[4]{0:T(128)} %get-tuple-element.116.index_ref) | copy-start | bytes 52
  13.0 3.8 %copy-start.10 = (s32[4]{0:T(128)S(1)}, s32[4]{0:T(128)}, u32[]{:S(2)}) copy-start(s32[4]{0:T(128)} %get-tuple-element.117.index_ref) | copy-start | bytes 52
  17.4 42.7 %collective-permute-start.5 = (bf16[4,64,4096]{2,1,0:T(8,128)(2,1)}, bf16[4,64,4096]{2,1,0:T(8,128)(2,1)}, u32[]{:S(2)}, u32[]{:S(2)}) collective-permute-start(bf16[4,64,4096]{2,1,0:T(8,128)(2,1)} %shard_map.59), channel_id=1, source_target_pairs={{0,96},{1,25},{2,98},{3,27},{4,100},{5,29},{6,102},{7,31},{8,104},... | collective-permute-start | bytes 6291464 | tf_op jit(solution)/shard_map/ppermute | solution.py:330
  44.4 15.7 %copy-start.5 = (bf16[4,64,4096]{2,1,0:T(8,128)(2,1)}, bf16[4,64,4096]{2,1,0:T(8,128)(2,1)S(1)}, u32[]{:S(2)}) copy-start(bf16[4,64,4096]{2,1,0:T(8,128)(2,1)S(1)} %collective-permute-done.refs_1_) | copy-start | bytes 6291460
  44.4 36.2 %collective-permute-start.1 = (bf16[4,64,4096]{2,1,0:T(8,128)(2,1)}, bf16[4,64,4096]{2,1,0:T(8,128)(2,1)}, u32[]{:S(2)}, u32[]{:S(2)}) collective-permute-start(bf16[4,64,4096]{2,1,0:T(8,128)(2,1)} %get-tuple-element.64), channel_id=1, source_target_pairs={{0,32},{1,9},{2,34},{3,11},{4,36},{5,13},{6,38},{7,15},{8,40},{9,1... | collective-permute-start | bytes 6291464 | tf_op jit(solution)/shard_map/ppermute | solution.py:330
  55.1 70.5 %collective-permute-start.2 = (bf16[4,64,4096]{2,1,0:T(8,128)(2,1)}, bf16[4,64,4096]{2,1,0:T(8,128)(2,1)}, u32[]{:S(2)}, u32[]{:S(2)}) collective-permute-start(bf16[4,64,4096]{2,1,0:T(8,128)(2,1)} %get-tuple-element.65), channel_id=1, source_target_pairs={{0,64},{1,17},{2,66},{3,19},{4,68},{5,21},{6,70},{7,23},{8,72},{9,... | collective-permute-start | bytes 6291464 | tf_op jit(solution)/shard_map/ppermute | solution.py:330
  57.5 68.1 %collective-permute-start.3 = (bf16[4,64,4096]{2,1,0:T(8,128)(2,1)}, bf16[4,64,4096]{2,1,0:T(8,128)(2,1)}, u32[]{:S(2)}, u32[]{:S(2)}) collective-permute-start(bf16[4,64,4096]{2,1,0:T(8,128)(2,1)} %get-tuple-element.66), channel_id=1, source_target_pairs={{0,96},{1,25},{2,98},{3,27},{4,100},{5,29},{6,102},{7,31},{8,104},... | collective-permute-start | bytes 6291464 | tf_op jit(solution)/shard_map/ppermute | solution.py:330
  60.2 22.5 %copy-start.11 = (s32[64,2]{0,1:T(2,128)S(1)}, s32[64,2]{0,1:T(2,128)}, u32[]{:S(2)}) copy-start(s32[64,2]{0,1:T(2,128)} %param.9) | copy-start | bytes 1540
  80.6 63.1 %collective-permute-start.6 = (bf16[4,64,4096]{2,1,0:T(8,128)(2,1)}, bf16[4,64,4096]{2,1,0:T(8,128)(2,1)}, u32[]{:S(2)}, u32[]{:S(2)}) collective-permute-start(bf16[4,64,4096]{2,1,0:T(8,128)(2,1)} %get-tuple-element.80), channel_id=1, source_target_pairs={{0,8},{1,33},{2,10},{3,35},{4,12},{5,37},{6,14},{7,39},{8,16},{9,4... | collective-permute-start | bytes 6291464 | tf_op jit(solution)/shard_map/ppermute | solution.py:330
  80.6 73.7 %collective-permute-start.7 = (bf16[4,64,4096]{2,1,0:T(8,128)(2,1)}, bf16[4,64,4096]{2,1,0:T(8,128)(2,1)}, u32[]{:S(2)}, u32[]{:S(2)}) collective-permute-start(bf16[4,64,4096]{2,1,0:T(8,128)(2,1)} %get-tuple-element.81), channel_id=1, source_target_pairs={{0,24},{1,97},{2,26},{3,99},{4,28},{5,101},{6,30},{7,103},{8,0},{9... | collective-permute-start | bytes 6291464 | tf_op jit(solution)/shard_map/ppermute | solution.py:330
  82.7 71.7 %collective-permute-start.8 = (bf16[4,64,4096]{2,1,0:T(8,128)(2,1)}, bf16[4,64,4096]{2,1,0:T(8,128)(2,1)}, u32[]{:S(2)}, u32[]{:S(2)}) collective-permute-start(bf16[4,64,4096]{2,1,0:T(8,128)(2,1)} %get-tuple-element.82), channel_id=1, source_target_pairs={{0,16},{1,65},{2,18},{3,67},{4,20},{5,69},{6,22},{7,71},{8,24},{9,... | collective-permute-start | bytes 6291464 | tf_op jit(solution)/shard_map/ppermute | solution.py:330
  82.9 3.4 %copy-start.2 = (bf16[2,4096,512]{2,1,0:T(8,128)(2,1)S(1)}, bf16[2,4096,512]{2,1,0:T(8,128)(2,1)}, u32[]{:S(2)}) copy-start(bf16[2,4096,512]{2,1,0:T(8,128)(2,1)} %shard_map.56.left_ref) | copy-start | bytes 25165828
  86.3 1.6 copy-start.6
  87.9 1.6 copy-start.7
  94.2 51.9 %copy-start.4 = (bf16[4,64,4096]{2,1,0:T(8,128)(2,1)S(1)}, bf16[4,64,4096]{2,1,0:T(8,128)(2,1)}, u32[]{:S(2)}) copy-start(bf16[4,64,4096]{2,1,0:T(8,128)(2,1)} %get-tuple-element.86.refs_0_) | copy-start | bytes 6291460
  143.8 50.6 %collective-permute-start.14 = (bf16[4,64,4096]{2,1,0:T(8,128)(2,1)}, bf16[4,64,4096]{2,1,0:T(8,128)(2,1)}, u32[]{:S(2)}, u32[]{:S(2)}) collective-permute-start(bf16[4,64,4096]{2,1,0:T(8,128)(2,1)} %get-tuple-element.100), channel_id=1, source_target_pairs={{0,24},{1,97},{2,26},{3,99},{4,28},{5,101},{6,30},{7,103},{8,0},{9... | collective-permute-start | bytes 6291464 | tf_op jit(solution)/shard_map/ppermute | solution.py:330
  143.8 50.6 %collective-permute-start.15 = (bf16[4,64,4096]{2,1,0:T(8,128)(2,1)}, bf16[4,64,4096]{2,1,0:T(8,128)(2,1)}, u32[]{:S(2)}, u32[]{:S(2)}) collective-permute-start(bf16[4,64,4096]{2,1,0:T(8,128)(2,1)} %get-tuple-element.101), channel_id=1, source_target_pairs={{0,16},{1,65},{2,18},{3,67},{4,20},{5,69},{6,22},{7,71},{8,24},{9,... | collective-permute-start | bytes 6291464 | tf_op jit(solution)/shard_map/ppermute | solution.py:330
  143.8 50.6 %collective-permute-start.13 = (bf16[4,64,4096]{2,1,0:T(8,128)(2,1)}, bf16[4,64,4096]{2,1,0:T(8,128)(2,1)}, u32[]{:S(2)}, u32[]{:S(2)}) collective-permute-start(bf16[4,64,4096]{2,1,0:T(8,128)(2,1)} %get-tuple-element.99), channel_id=1, source_target_pairs={{0,8},{1,33},{2,10},{3,35},{4,12},{5,37},{6,14},{7,39},{8,16},{9,4... | collective-permute-start | bytes 6291464 | tf_op jit(solution)/shard_map/ppermute | solution.py:330
  146.1 3.4 %copy-start.3 = (bf16[2,4096,512]{2,1,0:T(8,128)(2,1)S(1)}, bf16[2,4096,512]{2,1,0:T(8,128)(2,1)}, u32[]{:S(2)}) copy-start(bf16[2,4096,512]{2,1,0:T(8,128)(2,1)} %shard_map.56.left_ref) | copy-start | bytes 25165828
  154.4 40.1 %slice-start = ((s8[8388608]{0:T(1024)(128)(4,1)}), s8[4194304]{0:T(1024)(128)(4,1)S(1)}, s32[]{:S(2)}) async-start(s8[8388608]{0:T(1024)(128)(4,1)} %bitcast.22), calls=%async_computation | async-start | bytes 8388608
  154.4 40.1 %slice-start.1 = ((s8[8388608]{0:T(1024)(128)(4,1)}), s8[4194304]{0:T(1024)(128)(4,1)S(1)}, s32[]{:S(2)}) async-start(s8[8388608]{0:T(1024)(128)(4,1)} %bitcast.22), calls=%async_computation.1 | async-start | bytes 8388608
  164.3 16.7 %collective-permute-start.9 = (f32[32,64,128]{2,1,0:T(8,128)S(1)}, f32[32,64,128]{2,1,0:T(8,128)S(1)}, u32[]{:S(2)}, u32[]{:S(2)}) collective-permute-start(f32[32,64,128]{2,1,0:T(8,128)S(1)} %get-tuple-element.94), channel_id=1, source_target_pairs={{0,1},{1,0},{2,3},{3,2},{4,5},{5,4},{6,7},{7,6},{8,9},{9,8},{10,11... | collective-permute-start | bytes 3145736 | tf_op jit(solution)/shard_map/ppermute | solution.py:334
  181.1 8.1 %collective-permute-start.10 = (bf16[8,64,128]{2,1,0:T(8,128)(2,1)S(1)}, bf16[8,64,128]{2,1,0:T(8,128)(2,1)S(1)}, u32[]{:S(2)}, u32[]{:S(2)}) collective-permute-start(bf16[8,64,128]{2,1,0:T(8,128)(2,1)S(1)} %get-tuple-element.96), channel_id=1, source_target_pairs={{0,2},{1,3},{2,4},{3,5},{4,6},{5,7},{6,0},{7,1},{8,10},{9,11},{10,... | collective-permute-start | bytes 393224 | tf_op jit(solution)/shard_map/ppermute | solution.py:339
  183.1 10.1 %collective-permute-start.11 = (bf16[8,64,128]{2,1,0:T(8,128)(2,1)S(1)}, bf16[8,64,128]{2,1,0:T(8,128)(2,1)S(1)}, u32[]{:S(2)}, u32[]{:S(2)}) collective-permute-start(bf16[8,64,128]{2,1,0:T(8,128)(2,1)S(1)} %get-tuple-element.97), channel_id=1, source_target_pairs={{0,4},{1,5},{2,6},{3,7},{4,0},{5,1},{6,2},{7,3},{8,12},{9,13},{10,... | collective-permute-start | bytes 393224 | tf_op jit(solution)/shard_map/ppermute | solution.py:339
  189.2 5.2 %collective-permute-start.12 = (bf16[8,64,128]{2,1,0:T(8,128)(2,1)S(1)}, bf16[8,64,128]{2,1,0:T(8,128)(2,1)S(1)}, u32[]{:S(2)}, u32[]{:S(2)}) collective-permute-start(bf16[8,64,128]{2,1,0:T(8,128)(2,1)S(1)} %get-tuple-element.98), channel_id=1, source_target_pairs={{0,6},{1,7},{2,0},{3,1},{4,2},{5,3},{6,4},{7,5},{8,14},{9,15},{10,... | collective-permute-start | bytes 393224 | tf_op jit(solution)/shard_map/ppermute | solution.py:339
  194.4 36.2 %copy-start.1 = (s32[16,16]{1,0:T(8,128)S(1)}, s32[16,16]{1,0:T(8,128)}, u32[]{:S(2)}) copy-start(s32[16,16]{1,0:T(8,128)} %param.8) | copy-start | bytes 3076
  204.0 13.4 %collective-permute-start.16 = (f32[32,64,128]{2,1,0:T(8,128)S(1)}, f32[32,64,128]{2,1,0:T(8,128)S(1)}, u32[]{:S(2)}, u32[]{:S(2)}) collective-permute-start(f32[32,64,128]{2,1,0:T(8,128)S(1)} %get-tuple-element.106), channel_id=1, source_target_pairs={{0,1},{1,0},{2,3},{3,2},{4,5},{5,4},{6,7},{7,6},{8,9},{9,8},{10,11... | collective-permute-start | bytes 3145736 | tf_op jit(solution)/shard_map/ppermute | solution.py:334
  217.5 8.1 %collective-permute-start.17 = (bf16[8,64,128]{2,1,0:T(8,128)(2,1)S(1)}, bf16[8,64,128]{2,1,0:T(8,128)(2,1)S(1)}, u32[]{:S(2)}, u32[]{:S(2)}) collective-permute-start(bf16[8,64,128]{2,1,0:T(8,128)(2,1)S(1)} %get-tuple-element.108), channel_id=1, source_target_pairs={{0,2},{1,3},{2,4},{3,5},{4,6},{5,7},{6,0},{7,1},{8,10},{9,11},{10,... | collective-permute-start | bytes 393224 | tf_op jit(solution)/shard_map/ppermute | solution.py:339
  219.5 10.1 %collective-permute-start.18 = (bf16[8,64,128]{2,1,0:T(8,128)(2,1)S(1)}, bf16[8,64,128]{2,1,0:T(8,128)(2,1)S(1)}, u32[]{:S(2)}, u32[]{:S(2)}) collective-permute-start(bf16[8,64,128]{2,1,0:T(8,128)(2,1)S(1)} %get-tuple-element.109), channel_id=1, source_target_pairs={{0,4},{1,5},{2,6},{3,7},{4,0},{5,1},{6,2},{7,3},{8,12},{9,13},{10,... | collective-permute-start | bytes 393224 | tf_op jit(solution)/shard_map/ppermute | solution.py:339
  223.1 6.5 %collective-permute-start.19 = (bf16[8,64,128]{2,1,0:T(8,128)(2,1)S(1)}, bf16[8,64,128]{2,1,0:T(8,128)(2,1)S(1)}, u32[]{:S(2)}, u32[]{:S(2)}) collective-permute-start(bf16[8,64,128]{2,1,0:T(8,128)(2,1)S(1)} %get-tuple-element.110), channel_id=1, source_target_pairs={{0,6},{1,7},{2,0},{3,1},{4,2},{5,3},{6,4},{7,5},{8,14},{9,15},{10,... | collective-permute-start | bytes 393224 | tf_op jit(solution)/shard_map/ppermute | solution.py:339
